TPU v7x, 32 devices: a whole 2x2x4 slice. The times are simulated.
32 devices in a mesh: rows: 16 (over z, y, x), rhs: 2 (over core).
Axes of the slice: x: 2, y: 2, z: 4, core: 2. Of those that a mesh axis runs over, the one named last changes fastest.
Arguments:
- right_side: float32 [64, 8192], P('rhs', 'rows'), may hold values from -6 to 6
- tiles: float32 [128, 7, 64, 64], P('rows'), may hold values from -2 to 5.5, as said below
- pivots: float32 [128, 64, 64], P('rows'), may hold values from -0.05 to 0.8, as said below
- columns: int32 [128, 7], P('rows'), may hold values from 0 to 127, as said below
Outputs:
- solution: float32 [64, 8192], P('rhs', 'rows')
- residual: float32 [64, 8192], P('rhs', 'rows')
Inputs may be any that keep to these rules, and one draw needn't show every extreme that they name: columns[i, 0] = i. The other six columns of block row i are i - o and i + o for three offsets o shared by all block rows, the largest of them exactly 8, in an order of the slots drawn for each block row; a column that would fall outside 0 to 127 is i itself. tiles[i, 0] is the diagonal tile of block row i; A is symmetric positive definite: the tile of block row i in a slot whose column j differs from i is the transpose of the tile of block row j in its slot whose column is i. Every pivots[i] is symmetric positive definite.
All inputs are finite; a program needn't handle non-finite values.
Results may differ from a plain program's by a relative error of at most 0.0003.
Values sent between devices are 32-bit elements; how exact they have to be, the bound alone decides.
No kernel may reach another device: no remote copies, remote signals or barrier semaphores. Data moves between devices by JAX's collectives and lax.ppermute only.
A program may use at most 64 MiB of HBM per device.

v0:
```python
import jax
import jax.numpy as jnp
from jax import lax
from jax.sharding import PartitionSpec as P

SPAN = 8
ITERS = 2


def passed_along(value, axis, steps):
    count = lax.axis_size(axis)
    first, last = (max(0, -steps), min(count, count - steps))
    return lax.ppermute(value, axis, [(source, source + steps) for source in range(first, last)])


def extended_2(block, sides, width):
    for axis, dim in sides:
        count = lax.axis_size(axis)
        forward = [(i, i + 1) for i in range(count - 1)]
        backward = [(target, source) for source, target in forward]
        low = lax.ppermute(
            lax.slice_in_dim(block, block.shape[dim] - width, None, axis=dim), axis, forward
        )
        high = lax.ppermute(lax.slice_in_dim(block, 0, width, axis=dim), axis, backward)
        block = jnp.concatenate([low, block, high], axis=dim)
    return block


def inner(left, right):
    return jnp.dot(left, right.T, precision=lax.Precision.HIGHEST)


def chol_solve(factor, values):
    middle = lax.linalg.triangular_solve(factor, values, left_side=True, lower=True)
    return lax.linalg.triangular_solve(factor, middle, left_side=True, lower=True, transpose_a=True)


def shards(right_side, tiles, pivots, columns):
    count = right_side.shape[0]
    shard_rows = tiles.shape[0]
    width = tiles.shape[2]
    cells = shard_rows * width
    where_row = lax.axis_index("rows")
    start = where_row * shard_rows
    position = where_row % SPAN
    block_low = (where_row - position) * shard_rows
    block_high = block_low + SPAN * shard_rows
    global_rows = start + jnp.arange(shard_rows, dtype=jnp.int32)
    lower = (columns < global_rows[:, None]) & (columns >= block_low)
    upper = (columns > global_rows[:, None]) & (columns < block_high)
    lower_tiles = tiles * lower[:, :, None, None].astype(tiles.dtype)
    upper_tiles = tiles * upper[:, :, None, None].astype(tiles.dtype)
    forward_cols = jnp.clip(columns - start + shard_rows, 0, 2 * shard_rows - 1)
    backward_cols = jnp.clip(columns - start, 0, 2 * shard_rows - 1)
    halo_cols = columns - start + shard_rows
    from_below = (position != 0).astype(jnp.float32)
    from_above = (position != SPAN - 1).astype(jnp.float32)

    def forward_local(source, incoming):
        extended = jnp.concatenate([incoming, jnp.zeros_like(source)], axis=1)

        def forward_one_row(row, extended):
            picked = jnp.take(extended, forward_cols[row], axis=1)
            summed = jnp.einsum(
                "kab,ckb->ca", lower_tiles[row], picked, precision=lax.Precision.HIGHEST
            )
            remain = source[:, row] - summed
            value = jnp.einsum("ab,cb->ca", pivots[row], remain, precision=lax.Precision.HIGHEST)
            return lax.dynamic_update_slice_in_dim(extended, value[:, None], shard_rows + row, 1)

        extended = lax.fori_loop(0, shard_rows, forward_one_row, extended)
        return extended[:, shard_rows:]

    def backward_local(source, incoming):
        extended = jnp.concatenate([jnp.zeros_like(source), incoming], axis=1)

        def backward_one_row(turn, extended):
            row = shard_rows - 1 - turn
            picked = jnp.take(extended, backward_cols[row], axis=1)
            summed = jnp.einsum(
                "kab,ckb->ca", upper_tiles[row], picked, precision=lax.Precision.HIGHEST
            )
            value = source[:, row] - jnp.einsum(
                "ab,cb->ca", pivots[row], summed, precision=lax.Precision.HIGHEST
            )
            return lax.dynamic_update_slice_in_dim(extended, value[:, None], row, 1)

        extended = lax.fori_loop(0, shard_rows, backward_one_row, extended)
        return extended[:, :shard_rows]

    def precondition(vector):
        source = vector.reshape(count, shard_rows, width)
        lowered = forward_local(source, jnp.zeros_like(source))
        for turn in range(SPAN - 1):
            incoming = passed_along(lowered, "rows", 1) * from_below
            lowered = forward_local(source, incoming)
        result = backward_local(lowered, jnp.zeros_like(lowered))
        for turn in range(SPAN - 1):
            incoming = passed_along(result, "rows", -1) * from_above
            result = backward_local(lowered, incoming)
        return result.reshape(count, cells)

    solution = jnp.zeros_like(right_side)
    residual = right_side
    direction = precondition(residual)
    for turn in range(ITERS):
        blocks = extended_2(direction, (("rows", 1),), cells).reshape(count, 3 * shard_rows, width)
        apply_picked = jnp.take(blocks, halo_cols, axis=1)
        image = jnp.einsum(
            "ikab,cikb->cia", tiles, apply_picked, precision=lax.Precision.HIGHEST
        ).reshape(count, cells)
        every_direction = lax.all_gather(direction, "rhs", axis=0, tiled=True)
        partial_pq = inner(every_direction, image)
        partial_pr = inner(every_direction, residual)
        summed_pq, summed_pr = lax.psum((partial_pq, partial_pr), "rows")
        gram = lax.all_gather(summed_pq, "rhs", axis=1, tiled=True)
        factor = jnp.linalg.cholesky(0.5 * (gram + gram.T))
        alpha = chol_solve(factor, summed_pr)
        change = jnp.dot(alpha.T, every_direction, precision=lax.Precision.HIGHEST)
        solution = solution + change
        if turn + 1 < ITERS:
            every_image = lax.all_gather(image, "rhs", axis=0, tiled=True)
            residual = residual - jnp.dot(alpha.T, every_image, precision=lax.Precision.HIGHEST)
            preconditioned = precondition(residual)
            summed_qz = lax.psum(inner(every_image, preconditioned), "rows")
            beta = -chol_solve(factor, summed_qz)
            direction = preconditioned + jnp.dot(
                beta.T, every_direction, precision=lax.Precision.HIGHEST
            )
        else:
            every_image = lax.all_gather(image, "rhs", axis=0, tiled=True)
            residual = residual - jnp.dot(alpha.T, every_image, precision=lax.Precision.HIGHEST)
    return (solution, residual)


def solution(mesh):
    return jax.shard_map(
        shards,
        mesh=mesh,
        in_specs=(
            P("rhs", "rows"),
            P("rows", None, None, None),
            P("rows", None, None),
            P("rows", None),
        ),
        out_specs=(P("rhs", "rows"), P("rhs", "rows")),
        check_vma=False,
    )
```

profile of v0, /device:TPU:14, one launch (start us, length us, event | category | flops | bytes accessed | tf_op | source)
XLA Modules:
  0.0 929.6 jit_solution(10296941111528039919)
XLA Ops:
  6.2 17.0 %while.480 = (s32[]{:T(128)}, f32[32,16,64]{2,0,1:T(8,128)S(1)}, f32[32,8,64]{2,0,1:T(8,128)S(1)}, s32[8,7]{1,0:T(8,128)S(1)}, f32[8,7,64,64]{3,2,1,0:T(8,128)},...) while((s32[]{:T(128)}, f32[32,16,64]{2,0,1:T(8,128)S(1)}, ...), condition=%wide.region_1.3_spmd, body=%wide.region_0.2_spmd.sunk | while | flops 12600368 | bytes 488733 | solution.py:71
  30.3 17.0 %while.481 = (s32[]{:T(128)}, f32[32,16,64]{2,0,1:T(8,128)S(1)}, f32[32,8,64]{2,0,1:T(8,128)S(1)}, s32[8,7]{1,0:T(8,128)S(1)}, f32[8,7,64,64]{3,2,1,0:T(8,128)},...) while((s32[]{:T(128)}, f32[32,16,64]{2,0,1:T(8,128)S(1)}, ...), condition=%wide.region_3.5_spmd, body=%wide.region_2.4_spmd.sunk | while | flops 12600368 | bytes 488733 | solution.py:71
  55.1 17.0 %while.482 = (s32[]{:T(128)}, f32[32,16,64]{2,0,1:T(8,128)S(1)}, f32[32,8,64]{2,0,1:T(8,128)S(1)}, s32[8,7]{1,0:T(8,128)S(1)}, f32[8,7,64,64]{3,2,1,0:T(8,128)},...) while((s32[]{:T(128)}, f32[32,16,64]{2,0,1:T(8,128)S(1)}, ...), condition=%wide.region_5.7_spmd, body=%wide.region_4.6_spmd.sunk | while | flops 12600368 | bytes 488733 | solution.py:71
  80.7 17.0 %while.483 = (s32[]{:T(128)}, f32[32,16,64]{2,0,1:T(8,128)S(1)}, f32[32,8,64]{2,0,1:T(8,128)S(1)}, s32[8,7]{1,0:T(8,128)S(1)}, f32[8,7,64,64]{3,2,1,0:T(8,128)},...) while((s32[]{:T(128)}, f32[32,16,64]{2,0,1:T(8,128)S(1)}, ...), condition=%wide.region_7.9_spmd, body=%wide.region_6.8_spmd.sunk | while | flops 12600368 | bytes 488733 | solution.py:71
  106.4 17.0 %while.484 = (s32[]{:T(128)}, f32[32,16,64]{2,0,1:T(8,128)S(1)}, f32[32,8,64]{2,0,1:T(8,128)S(1)}, s32[8,7]{1,0:T(8,128)S(1)}, f32[8,7,64,64]{3,2,1,0:T(8,128)},...) while((s32[]{:T(128)}, f32[32,16,64]{2,0,1:T(8,128)S(1)}, ...), condition=%wide.region_9.11_spmd, body=%wide.region_8.10_spmd.sunk | while | flops 12600368 | bytes 488733 | solution.py:71
  132.1 17.0 %while.485 = (s32[]{:T(128)}, f32[32,16,64]{2,0,1:T(8,128)S(1)}, f32[32,8,64]{2,0,1:T(8,128)S(1)}, s32[8,7]{1,0:T(8,128)S(1)}, f32[8,7,64,64]{3,2,1,0:T(8,128)},...) while((s32[]{:T(128)}, f32[32,16,64]{2,0,1:T(8,128)S(1)}, ...), condition=%wide.region_11.13_spmd, body=%wide.region_10.12_spmd.sunk | while | flops 12600368 | bytes 488733 | solution.py:71
  157.8 17.0 %while.486 = (s32[]{:T(128)}, f32[32,16,64]{2,0,1:T(8,128)S(1)}, f32[32,8,64]{2,0,1:T(8,128)S(1)}, s32[8,7]{1,0:T(8,128)S(1)}, f32[8,7,64,64]{3,2,1,0:T(8,128)},...) while((s32[]{:T(128)}, f32[32,16,64]{2,0,1:T(8,128)S(1)}, ...), condition=%wide.region_13.15_spmd, body=%wide.region_12.14_spmd.sunk | while | flops 12600368 | bytes 488733 | solution.py:71
  183.5 17.0 %while.487 = (s32[]{:T(128)}, f32[32,16,64]{2,0,1:T(8,128)S(1)}, f32[32,8,64]{2,0,1:T(8,128)S(1)}, s32[8,7]{1,0:T(8,128)S(1)}, f32[8,7,64,64]{3,2,1,0:T(8,128)},...) while((s32[]{:T(128)}, f32[32,16,64]{2,0,1:T(8,128)S(1)}, ...), condition=%wide.region_15.17_spmd, body=%wide.region_14.16_spmd.sunk | while | flops 12600368 | bytes 488733 | solution.py:71
  237.4 9.6 %while.490 = (s32[]{:T(128)}, f32[32,16,64]{2,0,1:T(8,128)S(1)}, f32[32,8,64]{2,0,1:T(8,128)S(1)}, s32[8,7]{1,0:T(8,128)S(1)}, f32[8,7,64,64]{3,2,1,0:T(8,128)S(...) while((s32[]{:T(128)}, f32[32,16,64]{2,0,1:T(8,128)S(1)}, ...), condition=%wide.region_21.23_spmd, body=%wide.region_20.22_spmd.sunk | while | flops 12600370 | bytes 555315 | solution.py:88
  274.0 9.6 %while.492 = (s32[]{:T(128)}, f32[32,16,64]{2,0,1:T(8,128)S(1)}, f32[32,8,64]{2,0,1:T(8,128)S(1)}, s32[8,7]{1,0:T(8,128)S(1)}, f32[8,7,64,64]{3,2,1,0:T(8,128)S(...) while((s32[]{:T(128)}, f32[32,16,64]{2,0,1:T(8,128)S(1)}, ...), condition=%wide.region_25.27_spmd, body=%wide.region_24.26_spmd.sunk | while | flops 12600370 | bytes 555315 | solution.py:88
  292.3 9.6 %while.493 = (s32[]{:T(128)}, f32[32,16,64]{2,0,1:T(8,128)S(1)}, f32[32,8,64]{2,0,1:T(8,128)S(1)}, s32[8,7]{1,0:T(8,128)S(1)}, f32[8,7,64,64]{3,2,1,0:T(8,128)S(...) while((s32[]{:T(128)}, f32[32,16,64]{2,0,1:T(8,128)S(1)}, ...), condition=%wide.region_27.29_spmd, body=%wide.region_26.28_spmd.sunk | while | flops 12600370 | bytes 555315 | solution.py:88
  310.6 9.6 %while.494 = (s32[]{:T(128)}, f32[32,16,64]{2,0,1:T(8,128)S(1)}, f32[32,8,64]{2,0,1:T(8,128)S(1)}, s32[8,7]{1,0:T(8,128)S(1)}, f32[8,7,64,64]{3,2,1,0:T(8,128)S(...) while((s32[]{:T(128)}, f32[32,16,64]{2,0,1:T(8,128)S(1)}, ...), condition=%wide.region_29.31_spmd, body=%wide.region_28.30_spmd.sunk | while | flops 12600370 | bytes 555315 | solution.py:88
  328.9 9.6 %while.495 = (s32[]{:T(128)}, f32[32,16,64]{2,0,1:T(8,128)S(1)}, f32[32,8,64]{2,0,1:T(8,128)S(1)}, s32[8,7]{1,0:T(8,128)S(1)}, f32[8,7,64,64]{3,2,1,0:T(8,128)S(...) while((s32[]{:T(128)}, f32[32,16,64]{2,0,1:T(8,128)S(1)}, ...), condition=%wide.region_31.33_spmd, body=%wide.region_30.32_spmd.sunk | while | flops 12600370 | bytes 555315 | solution.py:88
  355.1 57.7 %all-reduce.29 = (f32[64,32]{0,1:T(8,128)S(1)}, f32[64,32]{0,1:T(8,128)S(1)}) all-reduce(f32[64,32]{0,1:T(8,128)} %fusion.476, f32[64,32]{0,1:T(8,128)S(1)} %fusion.475), channel_id=1, replica_groups=mesh['rows'=16,'rhs'=2] {'rows'}, use_global_device_ids=true, to_apply=%region_35.39 | all-reduce | flops 4096 | bytes 32768 | tf_op jit(solution)/shard_map/psum | solution.py:115
  427.5 17.0 %while.496 = (s32[]{:T(128)}, f32[32,16,64]{2,0,1:T(8,128)S(1)}, f32[32,8,64]{2,0,1:T(8,128)S(1)}, s32[8,7]{1,0:T(8,128)S(1)}, f32[8,7,64,64]{3,2,1,0:T(8,128)},...) while((s32[]{:T(128)}, f32[32,16,64]{2,0,1:T(8,128)S(1)}, ...), condition=%wide.region_37.43_spmd, body=%wide.region_36.42_spmd.sunk | while | flops 12600368 | bytes 488733 | solution.py:71
  455.5 17.0 %while.497 = (s32[]{:T(128)}, f32[32,16,64]{2,0,1:T(8,128)S(1)}, f32[32,8,64]{2,0,1:T(8,128)S(1)}, s32[8,7]{1,0:T(8,128)S(1)}, f32[8,7,64,64]{3,2,1,0:T(8,128)},...) while((s32[]{:T(128)}, f32[32,16,64]{2,0,1:T(8,128)S(1)}, ...), condition=%wide.region_39.45_spmd, body=%wide.region_38.44_spmd.sunk | while | flops 12600368 | bytes 488733 | solution.py:71
  480.0 17.0 %while.498 = (s32[]{:T(128)}, f32[32,16,64]{2,0,1:T(8,128)S(1)}, f32[32,8,64]{2,0,1:T(8,128)S(1)}, s32[8,7]{1,0:T(8,128)S(1)}, f32[8,7,64,64]{3,2,1,0:T(8,128)},...) while((s32[]{:T(128)}, f32[32,16,64]{2,0,1:T(8,128)S(1)}, ...), condition=%wide.region_41.47_spmd, body=%wide.region_40.46_spmd.sunk | while | flops 12600368 | bytes 488733 | solution.py:71
  505.2 17.0 %while.499 = (s32[]{:T(128)}, f32[32,16,64]{2,0,1:T(8,128)S(1)}, f32[32,8,64]{2,0,1:T(8,128)S(1)}, s32[8,7]{1,0:T(8,128)S(1)}, f32[8,7,64,64]{3,2,1,0:T(8,128)},...) while((s32[]{:T(128)}, f32[32,16,64]{2,0,1:T(8,128)S(1)}, ...), condition=%wide.region_43.49_spmd, body=%wide.region_42.48_spmd.sunk | while | flops 12600368 | bytes 488733 | solution.py:71
  530.7 17.0 %while.500 = (s32[]{:T(128)}, f32[32,16,64]{2,0,1:T(8,128)S(1)}, f32[32,8,64]{2,0,1:T(8,128)S(1)}, s32[8,7]{1,0:T(8,128)S(1)}, f32[8,7,64,64]{3,2,1,0:T(8,128)},...) while((s32[]{:T(128)}, f32[32,16,64]{2,0,1:T(8,128)S(1)}, ...), condition=%wide.region_45.51_spmd, body=%wide.region_44.50_spmd.sunk | while | flops 12600368 | bytes 488733 | solution.py:71
  556.4 17.0 %while.501 = (s32[]{:T(128)}, f32[32,16,64]{2,0,1:T(8,128)S(1)}, f32[32,8,64]{2,0,1:T(8,128)S(1)}, s32[8,7]{1,0:T(8,128)S(1)}, f32[8,7,64,64]{3,2,1,0:T(8,128)},...) while((s32[]{:T(128)}, f32[32,16,64]{2,0,1:T(8,128)S(1)}, ...), condition=%wide.region_47.53_spmd, body=%wide.region_46.52_spmd.sunk | while | flops 12600368 | bytes 488733 | solution.py:71
  582.1 17.0 %while.502 = (s32[]{:T(128)}, f32[32,16,64]{2,0,1:T(8,128)S(1)}, f32[32,8,64]{2,0,1:T(8,128)S(1)}, s32[8,7]{1,0:T(8,128)S(1)}, f32[8,7,64,64]{3,2,1,0:T(8,128)},...) while((s32[]{:T(128)}, f32[32,16,64]{2,0,1:T(8,128)S(1)}, ...), condition=%wide.region_49.55_spmd, body=%wide.region_48.54_spmd.sunk | while | flops 12600368 | bytes 488733 | solution.py:71
  607.8 17.0 %while.503 = (s32[]{:T(128)}, f32[32,16,64]{2,0,1:T(8,128)S(1)}, f32[32,8,64]{2,0,1:T(8,128)S(1)}, s32[8,7]{1,0:T(8,128)S(1)}, f32[8,7,64,64]{3,2,1,0:T(8,128)},...) while((s32[]{:T(128)}, f32[32,16,64]{2,0,1:T(8,128)S(1)}, ...), condition=%wide.region_51.57_spmd, body=%wide.region_50.56_spmd.sunk | while | flops 12600368 | bytes 488733 | solution.py:71
  763.1 61.0 %psum.37 = f32[64,32]{0,1:T(8,128)S(1)} all-reduce(f32[64,32]{0,1:T(8,128)S(1)} %fusion.478), channel_id=1, replica_groups=mesh['rows'=16,'rhs'=2] {'rows'}, use_global_device_ids=true, to_apply=%region_68.74 | all-reduce | flops 2048 | bytes 16384 | tf_op jit(solution)/shard_map/psum | solution.py:125
  844.4 69.1 %all-reduce.28 = (f32[64,32]{0,1:T(8,128)S(1)}, f32[64,32]{0,1:T(8,128)S(1)}) all-reduce(f32[64,32]{0,1:T(8,128)S(1)} %fusion.480, f32[64,32]{0,1:T(8,128)S(1)} %fusion.479), channel_id=1, replica_groups=mesh['rows'=16,'rhs'=2] {'rows'}, use_global_device_ids=true, to_apply=%region_70.76 | all-reduce | flops 4096 | bytes 32768 | tf_op jit(solution)/shard_map/psum | solution.py:115
  (1531 shorter events, 827.9 us)
Async XLA Ops:
  72.0 8.7 collective-permute-start.2
  97.7 8.7 collective-permute-start.3
  123.4 8.7 collective-permute-start.4
  149.1 8.7 collective-permute-start.5
  174.8 8.7 collective-permute-start.6
  210.0 9.1 collective-permute-start.7
  228.7 8.7 collective-permute-start.8
  247.0 8.7 collective-permute-start.9
  265.3 8.7 collective-permute-start.10
  283.6 8.7 collective-permute-start.11
  301.9 8.7 collective-permute-start.12
  320.2 8.7 collective-permute-start.13
  444.5 10.9 %collective-permute-start.16 = (f32[32,8,64]{2,0,1:T(8,128)S(1)}, f32[32,8,64]{2,0,1:T(8,128)S(1)}, u32[]{:S(2)}, u32[]{:S(2)}) collective-permute-start(f32[32,8,64]{2,0,1:T(8,128)S(1)} %slice.120), channel_id=1, source_target_pairs={{0,2},{2,4},{4,6},{6,8},{8,10},{10,12},{12,14},{14,16},{16,18},{18... | collective-permute-start | bytes 196616 | tf_op jit(solution)/shard_map/ppermute | solution.py:13
  547.7 8.7 collective-permute-start.20
  573.4 8.7 collective-permute-start.21
  599.1 8.7 collective-permute-start.22
  634.3 9.1 collective-permute-start.23
  653.0 8.7 collective-permute-start.24
  671.3 8.7 collective-permute-start.25
  689.6 8.7 collective-permute-start.26
  707.9 8.7 collective-permute-start.27
  726.2 8.7 collective-permute-start.28
  744.4 8.7 collective-permute-start.29
  824.7 11.9 %collective-permute-start.30 = (f32[32,512]{1,0:T(8,128)S(1)}, f32[32,512]{1,0:T(8,128)S(1)}, u32[]{:S(2)}, u32[]{:S(2)}) collective-permute-start(f32[32,512]{1,0:T(8,128)S(1)} %convolution_add_fusion.1), channel_id=1, source_target_pairs={{0,2},{2,4},{4,6},{6,8},{8,10},{10,12},{12,14},{14,16},{16,18},{18... | collective-permute-start | bytes 196616 | tf_op jit(solution)/shard_map/ppermute | solution.py:21
  (15 other events, 749.1 us)
where the time goes:
time: 948 us; the launch traced here: 930 us
  matrix products  271 us (29%)
  blocking collectives  199 us (21%)
  local copies, waits for them, and re-layouts  148 us (16%)
  starting transfers between devices  131 us (14%)
  waiting for transfers between devices  128 us (14%)
  other arithmetic  33.9 us (4%)
  loops' own time  16.9 us (2%)
    dot_general x128, matrix products, forward_one_row(): jnp.einsum('kab,ckb->ca', lower_tiles[row], picked, precision=lax.Precisi...  169 us
    psum x2, blocking collectives, shards(): summed_pq, summed_pr = lax.psum((partial_pq, partial_pr), 'rows')  127 us
    ppermute x28, waiting for transfers between devices, passed_along(): lax.ppermute(value, axis, [(source, source + steps) for source in range(f...  125 us
    ppermute x28, starting transfers between devices, passed_along(): lax.ppermute(value, axis, [(source, source + steps) for source in range(f...  116 us
    gather x128, local copies, waits for them, and re-layouts, forward_one_row(): picked = jnp.take(extended, forward_cols[row], axis=1)  71.1 us
    gather x128, local copies, waits for them, and re-layouts, backward_one_row(): picked = jnp.take(extended, backward_cols[row], axis=1)  71.1 us
    psum x1, blocking collectives, shards(): summed_qz = lax.psum(inner(every_image, preconditioned), 'rows')  61 us
    dot_general x128, matrix products, backward_one_row(): jnp.einsum('kab,ckb->ca', upper_tiles[row], picked, precision=lax.Precisi...  48.8 us
  transfers between devices with their start and end apart: 32, of which 30 were waited for; matrix products, arithmetic and copies ran while one was open for 0% of the time, Pallas kernels for 0%

commit v1 on v0

v1 whole, which is shorter than its diff:
```python
import functools
import jax
import jax.numpy as jnp
from jax import lax
from jax.experimental import pallas as pl
from jax.experimental.pallas import tpu as pltpu
from jax.sharding import Mesh, PartitionSpec as P

SPAN = 8
F32 = jnp.float32
BF16 = jnp.bfloat16
HIGHEST = lax.Precision.HIGHEST
NN = (((1,), (0,)), ((), ()))
NT = (((1,), (1,)), ((), ()))
VMEM = pl.BlockSpec(memory_space=pltpu.VMEM)
SMEM = pl.BlockSpec(memory_space=pltpu.SMEM)


def call(kernel, name, out_shape, in_specs, out_specs=VMEM, scratch=(), limit=16):
    return pl.pallas_call(
        kernel,
        out_shape=out_shape,
        in_specs=in_specs,
        out_specs=out_specs,
        scratch_shapes=list(scratch),
        compiler_params=pltpu.CompilerParams(vmem_limit_bytes=limit * 2**20),
        name=name,
    )


def two_parts(x):
    high = x.astype(BF16).astype(F32)
    return jnp.concatenate([high, x - high], axis=0).astype(BF16)


def halves(x):
    high = x.astype(BF16)
    return high, (x - high.astype(F32)).astype(BF16)


def product(x, high, low, dims):
    parts = two_parts(x)
    both = lax.dot_general(parts, high, dims, preferred_element_type=F32)
    both = both + lax.dot_general(parts, low, dims, preferred_element_type=F32)
    rows = x.shape[0]
    return both[:rows] + both[rows:]


def offsets_of(columns, start):
    found = []
    for offset in range(1, 8):
        hit = jnp.int32(0)
        for slot in range(7):
            away = columns[0, slot] - start
            hit = hit | jnp.where((away == offset) | (away == -offset), 1, 0)
        found.append(hit * 16 + offset)
    first = functools.reduce(jnp.maximum, found)
    second = functools.reduce(jnp.maximum, [jnp.where(f == first, 0, f) for f in found])
    first, second = (first & 15, second & 15)
    return (jnp.minimum(first, second), jnp.maximum(first, second), jnp.int32(8))


def pack_kernel(rows_part, columns, tiles, pivots, packed, diagonal, offsets):
    shard_rows = tiles.shape[0]
    start = (lax.axis_index("blk") * SPAN + lax.axis_index("pos")) * shard_rows
    base = lax.axis_index("rhs") * rows_part
    offs = offsets_of(columns, start)
    for k in range(3):
        offsets[0, k] = offs[k]
    for r in range(rows_part):
        row = base + r
        here = start + row
        sums = [jnp.zeros(tiles.shape[2:], F32) for _ in range(4)]
        for slot in range(7):
            away = columns[row, slot] - here
            tile = tiles[row, slot]
            for k, want in enumerate((*offs, 0)):
                sums[k] = sums[k] + tile * jnp.where(away == want, 1.0, 0.0)
        packed[r, 0] = jnp.concatenate([sums[0], sums[1]], axis=1)
        packed[r, 1] = jnp.concatenate([sums[2], pivots[row]], axis=1)
        half = sums[3].shape[0] // 2
        diagonal[r] = jnp.concatenate([sums[3][:half], sums[3][half:]], axis=1)


def band_kernel(columns, tiles, band_high, band_low, band):
    shard_rows, slots, order, _ = tiles.shape
    start = (lax.axis_index("blk") * SPAN + lax.axis_index("pos")) * shard_rows
    band[...] = jnp.zeros_like(band)
    for row in range(shard_rows):
        for slot in range(slots):
            away = columns[row, slot] - start + shard_rows
            where = pl.ds(pl.multiple_of(away * order, order), order)
            lanes = pl.ds(row * order, order)
            band[where, lanes] = band[where, lanes] + tiles[row, slot].T
    high, low = halves(band[...])
    band_high[...] = high
    band_low[...] = low


def factor_kernel(offsets, packed, m_high, m_low, w_high, w_low):
    order = 64
    cells = 8 * order
    o = [offsets[0, k] for k in range(3)]
    m_high[...] = jnp.zeros_like(m_high)
    m_low[...] = jnp.zeros_like(m_low)

    def fill(s, carry):
        for i in range(8):
            for k in range(3):
                from_row = (i - o[k]) & 7
                kind = jnp.where(o[k] > i, 0, 1)
                tile = packed[8 * s + from_row, k // 2, :, (k % 2) * order : (k % 2 + 1) * order]
                high, low = halves(tile)
                where = pl.ds(pl.multiple_of(from_row * order, order), order)
                lanes = pl.ds(i * order, order)
                m_high[s, kind, where, lanes] = high
                m_low[s, kind, where, lanes] = low
        return carry

    lax.fori_loop(0, 8, fill, 0)

    lane = lax.broadcasted_iota(jnp.int32, (order, 2 * order), 1)
    for j in range(7, -1, -1):
        for s in range(8):
            pivot = packed[8 * s + j, 1, :, order:]
            row = jnp.pad(pivot, ((0, 0), (j * order, cells - (j + 1) * order)))
            if j < 7:
                inside = [jnp.where(o[k] + j <= 7, 1.0, 0.0) for k in range(2)]
                pair = packed[8 * s + j, 0] * jnp.where(lane < order, inside[0], inside[1])
                scaled = product(pivot, *halves(pair), NN)
                left = two_parts(scaled)
                left = jnp.concatenate([left, left], axis=1)
                where = [
                    pl.ds(pl.multiple_of(jnp.minimum(o[k] + j, 7) * order, order), order)
                    for k in range(2)
                ]
                first = (j + 1) // 4 * 256
                right = jnp.concatenate(
                    [w[s, where[k], first:] for w in (w_high, w_low) for k in range(2)], axis=0
                )
                both = lax.dot_general(left, right, NN, preferred_element_type=F32)
                away = both[:order] + both[order:]
                if first:
                    away = jnp.pad(away, ((0, 0), (first, 0)))
                row = row - away
            high, low = halves(row)
            w_high[s, j * order : (j + 1) * order] = high
            w_low[s, j * order : (j + 1) * order] = low


def upper(x, high, low):
    half = high.shape[0] // 2
    return jnp.concatenate(
        [
            product(x[:, :half], high[:half, :half], low[:half, :half], NN),
            product(x, high[:, half:], low[:, half:], NN),
        ],
        axis=1,
    )


def upper_t(x, high, low):
    half = high.shape[0] // 2
    return jnp.concatenate(
        [
            product(x, high[:half], low[:half], NT),
            product(x[:, half:], high[half:, half:], low[half:, half:], NT),
        ],
        axis=1,
    )


def lower(x, high, low):
    half = high.shape[0] // 2
    return jnp.concatenate(
        [
            product(x, high[:, :half], low[:, :half], NN),
            product(x[:, half:], high[half:, half:], low[half:, half:], NN),
        ],
        axis=1,
    )


def lower_t(x, high, low):
    half = high.shape[0] // 2
    return jnp.concatenate(
        [
            product(x[:, :half], high[:half, :half], low[:half, :half], NT),
            product(x, high[half:], low[half:], NT),
        ],
        axis=1,
    )


def forward_step(s, source, before, m, w):
    if before is not None:
        source = source - lower(before, m[0].at[s - 1, 0], m[1].at[s - 1, 0])
    value = upper(source, w[0].at[s], w[1].at[s])
    return value, source - upper(value, m[0].at[s, 1], m[1].at[s, 1])


def first_kernel(r, m_high, m_low, w_high, w_low, t, last, coupled):
    m, w = (m_high, m_low), (w_high, w_low)
    value = None
    for s in range(8):
        value, t[s] = forward_step(s, r[s], value, m, w)
    z = upper_t(t[7], w_high.at[7], w_low.at[7])
    last[...] = z
    coupled[...] = lower(z, m_high.at[7, 0], m_low.at[7, 0])


def second_kernel(t, last, m_high, m_low, w_high, w_low, z, above):
    value = last[...]
    z[7] = value
    for s in range(6, -1, -1):
        above[s] = lower_t(value, m_high.at[s, 0], m_low.at[s, 0])
        value = upper_t(t[s] - above[s], w_high.at[s], w_low.at[s])
        z[s] = value


def third_kernel(r, z, above, arrived, diagonal, m_high, m_low, w_high, w_low, image, t, value):
    m, w = (m_high, m_low), (w_high, w_low)
    order = 64
    before = None
    for s in range(8):
        x = z[s]
        total = upper(x, m_high.at[s, 1], m_low.at[s, 1]) + upper_t(x, m_high.at[s, 1], m_low.at[s, 1])
        own = []
        for i in range(8):
            pair = diagonal[8 * s + i]
            tile = jnp.concatenate([pair[:, :order], pair[:, order:]], axis=0)
            own.append(product(x[:, i * order : (i + 1) * order], *halves(tile), NN))
        total = total + jnp.concatenate(own, axis=1)
        if s:
            total = total + lower(z[s - 1], m_high.at[s - 1, 0], m_low.at[s - 1, 0])
        else:
            total = total + arrived[...]
        if s < 7:
            total = total + above[s]
        image[s] = total
        if s < 7:
            before, t[s] = forward_step(s, total - r[s], before, m, w)
    value[...] = before


def fourth_kernel(r, partial, arrived, t, value, m_high, m_low, w_high, w_low, image, out, extra):
    m, w = (m_high, m_low), (w_high, w_low)
    blocks = out.shape[0]
    block = lax.axis_index("blk")
    total = partial[...] + lower_t(arrived[...], m_high.at[7, 0], m_low.at[7, 0])
    image[...] = total
    _, final = forward_step(7, total - r[7], value[...], m, w)
    out[...] = jnp.zeros_like(out)
    y = upper_t(final, w_high.at[7], w_low.at[7])
    extra[7] = y
    for s in range(6, -1, -1):
        y = upper_t(t[s] - lower_t(y, m_high.at[s, 0], m_low.at[s, 0]), w_high.at[s], w_low.at[s])
        extra[s] = y
    for s in range(8):
        for side in range(3):
            group = s + side - 1
            if 0 <= group < 8:
                out[block, s, side] = extra[group]

    @pl.when(block + 1 < blocks)
    def _():
        out[block + 1, 0, 0] = extra[7]

    @pl.when(block > 0)
    def _():
        out[block - 1, 7, 2] = extra[0]


def place_rows(place, t, rhs, rows, lanes=slice(None)):
    count = rows.shape[0]
    place[pl.ds(pl.multiple_of((rhs ^ t) * count, count), count), lanes] = rows


def early_kernel(n, *refs):
    r_pieces, dq_pieces = refs[:n], refs[n : 2 * n]
    r, d, q, sums = refs[2 * n :]
    rhs = lax.axis_index("rhs")
    for t in range(n):
        place_rows(r, t, rhs, r_pieces[t][...])
        for kind, place in enumerate((d, q)):
            rows = jnp.concatenate([dq_pieces[t][j, kind] for j in range(SPAN)], axis=0)
            place_rows(place, t, rhs, rows)
    for k, other in enumerate((r, q)):
        sums[k] = lax.dot_general(
            d[...], other[...], NT, precision=HIGHEST, preferred_element_type=F32
        )


def late_kernel(n, *refs):
    pieces = refs[:n]
    q, band_high, band_low, e, w, sums, wide = refs[n:]
    rhs = lax.axis_index("rhs")
    blocks, _, _, _, cells = pieces[0].shape
    for side in range(3):
        lanes = slice(side * cells, (side + 1) * cells)
        for t, piece in enumerate(pieces):
            rows = [
                sum(piece[block, j, side] for block in range(blocks)) for j in range(SPAN)
            ]
            place_rows(wide, t, rhs, jnp.concatenate(rows, axis=0), lanes)
    e[...] = wide[:, cells : 2 * cells]
    w[...] = product(wide[...], band_high[...], band_low[...], NN)
    for k, other in enumerate((q, w)):
        sums[k] = lax.dot_general(
            e[...], other[...], NT, precision=HIGHEST, preferred_element_type=F32
        )


def small(a, b):
    return lax.dot_general(a, b, NN, precision=HIGHEST, preferred_element_type=F32)


def inverse(a):
    size = a.shape[0]
    row_at = lax.broadcasted_iota(jnp.int32, a.shape, 0)
    col_at = lax.broadcasted_iota(jnp.int32, a.shape, 1)
    for k in range(size):
        scale = 1.0 / a[k : k + 1, k : k + 1]
        row = jnp.where(col_at[:1] == k, 1.0, a[k : k + 1, :]) * scale
        column = a[:, k : k + 1]
        rest = jnp.where(col_at == k, 0.0, a)
        a = jnp.where(row_at == k, row, rest - column * row)
    return a


def symmetric(a):
    return 0.5 * (a + a.T)


def invert_kernel(sums, inverted):
    inverted[...] = inverse(symmetric(sums[1]))


def last_kernel(early, late, inverted, r, d, q, e, w, solution, residual):
    count = solution.shape[0]
    rhs = lax.axis_index("rhs")
    s1, s2 = symmetric(early[0]), symmetric(early[1])
    s3, s4 = symmetric(late[0]), symmetric(late[1])
    inv = inverted[...]
    c = small(inv, s3)
    schur = symmetric(s4 - small(s3, c))
    h = small(s2 - s1 - small(s1, c), inverse(schur))
    f = small(s1 - small(h, s3), inv)
    pick = lax.broadcasted_iota(jnp.int32, (count, s1.shape[0]), 0) + rhs * count
    pick = jnp.where(pick == lax.broadcasted_iota(jnp.int32, pick.shape, 1), 1.0, 0.0)
    f, h = small(pick, f), small(pick, h)
    solution[...] = small(f, d[...]) + small(h, e[...])
    own = r[pl.ds(pl.multiple_of(rhs * count, count), count), :]
    residual[...] = own - small(f, q[...]) - small(h, w[...])


def swapped(value, axis, bit):
    return lax.ppermute(value, axis, [(i, i ^ bit) for i in range(lax.axis_size(axis))])


def summed(value):
    for axis in ("pos", "blk"):
        bit = 1
        while bit < lax.axis_size(axis):
            value = value + swapped(value, axis, bit)
            bit *= 2
    return value


def shards(right_side, tiles, pivots, columns):
    count, cells = right_side.shape
    shard_rows, slots, order, _ = tiles.shape
    parts = lax.axis_size("rhs")
    blocks = lax.axis_size("blk")
    rows_part = shard_rows // parts
    each = count // SPAN
    total = count * parts
    S = jax.ShapeDtypeStruct
    up = [(i, i + 1) for i in range(blocks - 1)]
    down = [(i + 1, i) for i in range(blocks - 1)]

    packed, diagonal, offsets = call(
        functools.partial(pack_kernel, rows_part),
        "pack_tiles",
        [
            S((rows_part, 2, order, 2 * order), F32),
            S((rows_part, order // 2, 2 * order), F32),
            S((1, 3), jnp.int32),
        ],
        [SMEM, VMEM, VMEM],
        [VMEM, VMEM, SMEM],
    )(columns, tiles, pivots)
    packed = lax.all_gather(packed, ("pos", "rhs"), axis=0, tiled=True)
    diagonal = lax.all_gather(diagonal, ("pos", "rhs"), axis=0, tiled=True)
    r = lax.all_to_all(right_side.reshape(SPAN, each, cells), "pos", 0, 0, tiled=True)
    r_pieces = [right_side] + [swapped(right_side, "rhs", t) for t in range(1, parts)]
    band_high, band_low = call(
        band_kernel,
        "row_band",
        [S((3 * cells, cells), BF16)] * 2,
        [SMEM, VMEM],
        [VMEM] * 2,
        [pltpu.VMEM((3 * cells, cells), F32)],
    )(columns, tiles)

    square = pltpu.VMEM((SPAN, 2, cells, cells), BF16)
    single = pltpu.VMEM((SPAN, cells, cells), BF16)
    mats = call(
        factor_kernel,
        "block_factors",
        [square, square, single, single],
        [SMEM, VMEM],
        [VMEM] * 4,
    )(offsets, packed)
    vectors, vector = S((SPAN, each, cells), F32), S((each, cells), F32)
    t, last, coupled = call(
        first_kernel, "forward_r", [vectors, vector, vector], [VMEM] * 5, [VMEM] * 3
    )(r, *mats)
    from_below = lax.ppermute(coupled, "blk", up)
    z, above = call(second_kernel, "backward_r", [vectors] * 2, [VMEM] * 6, [VMEM] * 2)(t, last, *mats)
    from_above = lax.ppermute(z[0], "blk", down)
    image, t, value = call(
        third_kernel, "image_and_forward", [vectors, vectors, vector], [VMEM] * 9, [VMEM] * 3
    )(r, z, above, from_below, diagonal, *mats)
    image_last, y = call(
        fourth_kernel,
        "backward_image",
        [vector, S((blocks, SPAN, 3, each, cells), F32)],
        [VMEM] * 9,
        [VMEM] * 2,
        [pltpu.VMEM((SPAN, each, cells), F32)],
    )(r, image[7], from_above, t, value, *mats)
    image = jnp.concatenate([image[:7], image_last[None]], axis=0)

    dq = lax.all_to_all(jnp.stack([z, image], axis=1), "pos", 0, 0, tiled=True)
    dq_pieces = [dq] + [swapped(dq, "rhs", t) for t in range(1, parts)]
    full, two = S((total, cells), F32), S((2, total, total), F32)
    r_full, d_full, q_full, early = call(
        functools.partial(early_kernel, parts),
        "products_d",
        [full, full, full, two],
        [VMEM] * (2 * parts),
        [VMEM] * 4,
    )(*r_pieces, *dq_pieces)
    early = summed(early)
    inverted = call(invert_kernel, "invert", S((total, total), F32), [VMEM])(early)

    y = lax.all_to_all(
        y.reshape(blocks * SPAN, 3, each, cells), ("blk", "pos"), 0, 0, tiled=True
    ).reshape(blocks, SPAN, 3, each, cells)
    y_pieces = [y] + [swapped(y, "rhs", t) for t in range(1, parts)]
    e_full, w_full, late = call(
        functools.partial(late_kernel, parts),
        "products_e",
        [full, full, two],
        [VMEM] * (parts + 3),
        [VMEM] * 3,
        [pltpu.VMEM((total, 3 * cells), F32)],
    )(*y_pieces, q_full, band_high, band_low)
    late = summed(late)
    return call(
        last_kernel, "update", [S((count, cells), F32)] * 2, [VMEM] * 8, [VMEM] * 2
    )(early, late, inverted, r_full, d_full, q_full, e_full, w_full)


def solution(mesh):
    devices = mesh.devices
    split = Mesh(
        devices.reshape(devices.shape[0] // SPAN, SPAN, devices.shape[1]), ("blk", "pos", "rhs")
    )
    rows = ("blk", "pos")
    return jax.shard_map(
        shards,
        mesh=split,
        in_specs=(
            P("rhs", rows),
            P(rows, None, None, None),
            P(rows, None, None),
            P(rows, None),
        ),
        out_specs=(P("rhs", rows), P("rhs", rows)),
        check_vma=False,
    )
```

time: 948 us -> 200 us (0.21)
  the two profiles are of different devices: /device:TPU:14 before, /device:TPU:0 now
where the time goes in v1:
time: 200 us; the launch traced here: 199 us
  Pallas kernels  55 us (28%)
  waiting for transfers between devices  53.1 us (27%)
  local copies, waits for them, and re-layouts  40.9 us (20%)
  starting transfers between devices  27.1 us (14%)
  between operations  14.3 us (7%)
  blocking collectives  8.73 us (4%)
    unnamed x40, local copies, waits for them, and re-layouts  39.4 us
    all_gather x1, waiting for transfers between devices, shards(): packed = lax.all_gather(packed, ('pos', 'rhs'), axis=0, tiled=True)  29.8 us
    pallas_call x1, Pallas kernels, shards(): call(factor_kernel, 'block_factors', [square, square, single, single], [S...  15.3 us
    all_to_all x1, waiting for transfers between devices, shards(): lax.all_to_all(y.reshape(blocks * SPAN, 3, each, cells), ('blk', 'pos'),...  12.4 us
    ppermute x11, waiting for transfers between devices, swapped(): lax.ppermute(value, axis, [(i, i ^ bit) for i in range(lax.axis_size(axis...  10.1 us
    ppermute x11, starting transfers between devices, swapped(): lax.ppermute(value, axis, [(i, i ^ bit) for i in range(lax.axis_size(axis...  9.28 us
    all_to_all x1, blocking collectives, shards(): dq = lax.all_to_all(jnp.stack([z, image], axis=1), 'pos', 0, 0, tiled=True)  8.73 us
    pallas_call x1, Pallas kernels, shards(): call(last_kernel, 'update', [S((count, cells), F32)] * 2, [VMEM] * 8, [VM...  7.54 us
  transfers between devices with their start and end apart: 17, of which 8 were waited for; matrix products, arithmetic and copies ran while one was open for 1% of the time, Pallas kernels for 20%

profile of v1, /device:TPU:0, one launch (start us, length us, event | category | flops | bytes accessed | tf_op | source)
XLA Modules:
  0.0 199.2 jit_solution(11010381502168255073)
XLA Ops:
  14.3 6.2 %all-to-all-start = ((f32[8,4,512]{2,1,0:T(4,128)}), f32[8,4,512]{2,1,0:T(4,128)S(1)}, u32[]{:S(2)}, u32[]{:S(2)}) async-start(f32[8,4,512]{2,1,0:T(4,128)} %reshape.13), calls=%async_computation | async-start | bytes 131072 | tf_op jit(solution)/shard_map/all_to_all | solution.py:395
  20.5 29.8 %all-gather.3.cloned.1.call-done.packed = f32[64,2,64,128]{3,2,1,0:T(8,128)} async-done(((f32[4,2,64,128]{3,2,1,0:T(8,128)}), f32[64,2,64,128]{3,2,1,0:T(8,128)}) %all-gather.3.cloned.1.call-update) | async-done | bytes 4194320 | tf_op jit(solution)/shard_map/all_gather | solution.py:393
  52.5 15.3 %block_factors.1 = (bf16[8,2,512,512]{3,2,1,0:T(8,128)(2,1)S(1)}, bf16[8,2,512,512]{3,2,1,0:T(8,128)(2,1)S(1)}, bf16[8,512,512]{2,1,0:T(8,128)(2,1)S(1)}, bf16[8,512,512]{2,1,0:T(8,128)(2,1)S(1)}) custom-call(s32[1,3]{1,0:T(1,128)S(1)} %get-tuple-element.28.offsets, f32[64,2,64,128]{3,2,1,0:T(8,128)S(1)} %copy-done.14), custom_call_target="tpu_custom_call" | custom-call | tf_op jit(solution)/shard_map/block_factors/pallas_call | solution.py:408
  67.8 3.3 %copy-done = bf16[8,2,512,512]{3,2,1,0:T(8,128)(2,1)} copy-done((bf16[8,2,512,512]{3,2,1,0:T(8,128)(2,1)}, bf16[8,2,512,512]{3,2,1,0:T(8,128)(2,1)S(1)}, u32[]{:S(2)}) %copy-start) | copy-done | bytes 8388632
  71.1 3.3 %copy-done.3 = bf16[8,2,512,512]{3,2,1,0:T(8,128)(2,1)} copy-done((bf16[8,2,512,512]{3,2,1,0:T(8,128)(2,1)}, bf16[8,2,512,512]{3,2,1,0:T(8,128)(2,1)S(1)}, u32[]{:S(2)}) %copy-start.3) | copy-done | bytes 8388632
  78.3 3.4 %copy-done.1 = bf16[8,2,512,512]{3,2,1,0:T(8,128)(2,1)S(1)} copy-done((bf16[8,2,512,512]{3,2,1,0:T(8,128)(2,1)S(1)}, bf16[8,2,512,512]{3,2,1,0:T(8,128)(2,1)}, u32[]{:S(2)}) %copy-start.1) | copy-done | bytes 8388632
  81.8 3.4 %copy-done.4 = bf16[8,2,512,512]{3,2,1,0:T(8,128)(2,1)S(1)} copy-done((bf16[8,2,512,512]{3,2,1,0:T(8,128)(2,1)S(1)}, bf16[8,2,512,512]{3,2,1,0:T(8,128)(2,1)}, u32[]{:S(2)}) %copy-start.4) | copy-done | bytes 8388632
  85.1 2.2 %copy-done.7 = bf16[8,512,512]{2,1,0:T(8,128)(2,1)S(1)} copy-done((bf16[8,512,512]{2,1,0:T(8,128)(2,1)S(1)}, bf16[8,512,512]{2,1,0:T(8,128)(2,1)}, u32[]{:S(2)}) %copy-start.7) | copy-done | bytes 4194328
  87.3 2.2 %copy-done.10 = bf16[8,512,512]{2,1,0:T(8,128)(2,1)S(1)} copy-done((bf16[8,512,512]{2,1,0:T(8,128)(2,1)S(1)}, bf16[8,512,512]{2,1,0:T(8,128)(2,1)}, u32[]{:S(2)}) %copy-start.10) | copy-done | bytes 4194328
  89.5 4.1 %forward_r.1 = (f32[8,4,512]{2,1,0:T(4,128)S(1)}, f32[4,512]{1,0:T(4,128)S(1)}, f32[4,512]{1,0:T(4,128)S(1)}) custom-call(f32[8,4,512]{2,1,0:T(4,128)S(1)} %all-to-all-done.r, bf16[8,2,512,512]{3,2,1,0:T(8,128)(2,1)S(1)} %copy-done.1, bf16[8,2,512,512]{3,2,1,0:T(8,128)(2,1)S(1)} %copy-done.4, bf16[8,512,512]{2,1,0:T(8,128)(2,1)S(1)} %copy-done.7, ...), custom_call_target="tpu_custom_call" | custom-call | tf_op jit(solution)/shard_map/forward_r/pallas_call | solution.py:416
  93.6 4.1 %collective-permute-start.1 = (f32[4,512]{1,0:T(4,128)S(1)}, f32[4,512]{1,0:T(4,128)S(1)}, u32[]{:S(2)}, u32[]{:S(2)}) collective-permute-start(f32[4,512]{1,0:T(4,128)S(1)} %get-tuple-element.38), channel_id=1, source_target_pairs={{0,16},{1,17},{2,18},{3,19},{4,20},{5,21},{6,22},{7,23},{8,24},{9,... | collective-permute-start | bytes 24584 | tf_op jit(solution)/shard_map/ppermute | solution.py:419
  97.7 4.1 %backward_r.1 = (f32[8,4,512]{2,1,0:T(4,128)S(1)}, f32[8,4,512]{2,1,0:T(4,128)S(1)}) custom-call(f32[8,4,512]{2,1,0:T(4,128)S(1)} %get-tuple-element.34.t, f32[4,512]{1,0:T(4,128)S(1)} %get-tuple-element.35.last, bf16[8,2,512,512]{3,2,1,0:T(8,128)(2,1)S(1)} %copy-done.1, bf16[8,2,512,512]{3,2,1,0:T(8,128)(2,1)S(1)} %copy-done.4, ...), custom_call_target="tpu_custom_call" | custom-call | tf_op jit(solution)/shard_map/backward_r/pallas_call | solution.py:420
  103.4 3.4 %copy-done.2 = bf16[8,2,512,512]{3,2,1,0:T(8,128)(2,1)S(1)} copy-done((bf16[8,2,512,512]{3,2,1,0:T(8,128)(2,1)S(1)}, bf16[8,2,512,512]{3,2,1,0:T(8,128)(2,1)}, u32[]{:S(2)}) %copy-start.2) | copy-done | bytes 8388632
  106.8 3.4 %copy-done.5 = bf16[8,2,512,512]{3,2,1,0:T(8,128)(2,1)S(1)} copy-done((bf16[8,2,512,512]{3,2,1,0:T(8,128)(2,1)S(1)}, bf16[8,2,512,512]{3,2,1,0:T(8,128)(2,1)}, u32[]{:S(2)}) %copy-start.5) | copy-done | bytes 8388632
  115.8 6.9 %image_and_forward.1 = (f32[8,4,512]{2,1,0:T(4,128)S(1)}, f32[8,4,512]{2,1,0:T(4,128)S(1)}, f32[4,512]{1,0:T(4,128)S(1)}) custom-call(f32[8,4,512]{2,1,0:T(4,128)S(1)} %all-to-all-done.r, f32[8,4,512]{2,1,0:T(4,128)S(1)} %get-tuple-element.36.z, f32[8,4,512]{2,1,0:T(4,128)S(1)} %get-tuple-element.37.above, f32[4,512]{1,0:T(4,128)S(1)} %collective-permute-done.1.arrived, ...), custom_call_target="tpu_custom_call" | custom-call | tf_op jit(solution)/shard_map/image_and_forward/pallas_call | solution.py:422
  122.7 6.0 %backward_image.1 = (f32[4,512]{1,0:T(4,128)S(1)}, f32[2,8,3,4,512]{4,3,2,1,0:T(4,128)}) custom-call(f32[8,4,512]{2,1,0:T(4,128)S(1)} %all-to-all-done.r, f32[4,512]{1,0:T(4,128)S(1)} %slice_bitcast_fusion.1.partial, f32[4,512]{1,0:T(4,128)S(1)} %collective-permute-done.2.arrived, f32[8,4,512]{2,1,0:T(4,128)S(1)} %get-tuple-element.41.t, ...), custom_call_target="tpu_custom_call" | custom-call | tf_op jit(solution)/shard_map/backward_image/pallas_call | solution.py:425
  128.7 6.0 %all-to-all-start.2 = ((f32[16,3,4,512]{3,2,1,0:T(4,128)}), f32[16,3,4,512]{3,2,1,0:T(4,128)S(1)}, u32[]{:S(2)}, u32[]{:S(2)}) async-start(f32[16,3,4,512]{3,2,1,0:T(4,128)} %bitcast.5), calls=%async_computation.2 | async-start | bytes 786432 | tf_op jit(solution)/shard_map/all_to_all | solution.py:448
  134.7 12.4 %all-to-all-done.2 = f32[16,3,4,512]{3,2,1,0:T(4,128)S(1)} async-done(((f32[16,3,4,512]{3,2,1,0:T(4,128)}), f32[16,3,4,512]{3,2,1,0:T(4,128)S(1)}, u32[]{:S(2)}, u32[]{:S(2)}) %all-to-all-start.2) | async-done | bytes 393248 | tf_op jit(solution)/shard_map/all_to_all | solution.py:448
  147.1 8.7 %all_to_all.15.refs_2_ = f32[8,2,4,512]{3,2,1,0:T(4,128)S(1)} all-to-all(f32[8,2,4,512]{3,2,1,0:T(4,128)S(1)} %pad_maximum_fusion), channel_id=1, replica_groups=mesh['blk'=2,'pos'=8,'rhs'=2] {'pos'}, dimensions={0} | all-to-all | bytes 262144 | tf_op jit(solution)/shard_map/all_to_all | solution.py:435
  156.4 2.6 %row_band.1 = (bf16[1536,512]{1,0:T(8,128)(2,1)S(1)}, bf16[1536,512]{1,0:T(8,128)(2,1)S(1)}) custom-call(s32[8,7]{1,0:T(8,128)S(1)} %copy-done.19, f32[8,7,64,64]{3,2,1,0:T(8,128)S(1)} %copy-done.13), custom_call_target="tpu_custom_call" | custom-call | tf_op jit(solution)/shard_map/row_band/pallas_call | solution.py:397
  170.9 2.5 %collective-permute-done.6 = f32[2,64,64]{2,1,0:T(8,128)S(1)} collective-permute-done((f32[2,64,64]{2,1,0:T(8,128)S(1)}, f32[2,64,64]{2,1,0:T(8,128)S(1)}, u32[]{:S(2)}, u32[]{:S(2)}) %collective-permute-start.6) | collective-permute-done | bytes 32800 | tf_op jit(solution)/shard_map/ppermute | solution.py:358
  176.4 2.9 %collective-permute-done.7 = f32[2,64,64]{2,1,0:T(8,128)S(1)} collective-permute-done((f32[2,64,64]{2,1,0:T(8,128)S(1)}, f32[2,64,64]{2,1,0:T(8,128)S(1)}, u32[]{:S(2)}, u32[]{:S(2)}) %collective-permute-start.7) | collective-permute-done | bytes 32800 | tf_op jit(solution)/shard_map/ppermute | solution.py:358
  179.3 5.4 %invert.1.inverted = f32[64,64]{1,0:T(8,128)S(1)} custom-call(f32[2,64,64]{2,1,0:T(8,128)S(1)} %add.27.sums.early), custom_call_target="tpu_custom_call" | custom-call | tf_op jit(solution)/shard_map/invert/pallas_call | solution.py:446
  184.8 7.5 %update.1 = (f32[32,512]{1,0:T(8,128)}, f32[32,512]{1,0:T(8,128)}) custom-call(f32[2,64,64]{2,1,0:T(8,128)S(1)} %add.27.sums.early, f32[2,64,64]{2,1,0:T(8,128)S(1)} %add.31.late, f32[64,64]{1,0:T(8,128)S(1)} %invert.1.inverted, f32[64,512]{1,0:T(8,128)S(1)} %get-tuple-element.50.r, f32[64,512]{1,0:T(8,128)S(1)} %get-tuple-element.51.d, ...), custom_call_target="tpu_custom_call" | custom-call | tf_op jit(solution)/shard_map/update/pallas_call | solution.py:461
  (78 shorter events, 36.0 us)
Async XLA Ops:
  7.2 43.2 %all-gather.3.cloned.1.call-start = ((), (), s32[]{:S(2)}) async-start(), calls=%async_computation.3 | async-start | bytes 4456448 | tf_op jit(solution)/shard_map/all_gather | solution.py:393
  12.1 91.3 %all-gather.5.cloned.1.call-start = ((), (), s32[]{:S(2)}) async-start(), calls=%async_computation.4 | async-start | bytes 1114112 | tf_op jit(solution)/shard_map/all_gather | solution.py:394
  14.3 64.0 %all-to-all-start = ((f32[8,4,512]{2,1,0:T(4,128)}), f32[8,4,512]{2,1,0:T(4,128)S(1)}, u32[]{:S(2)}, u32[]{:S(2)}) async-start(f32[8,4,512]{2,1,0:T(4,128)} %reshape.13), calls=%async_computation | async-start | bytes 131072 | tf_op jit(solution)/shard_map/all_to_all | solution.py:395
  78.3 3.4 %copy-start.1 = (bf16[8,2,512,512]{3,2,1,0:T(8,128)(2,1)S(1)}, bf16[8,2,512,512]{3,2,1,0:T(8,128)(2,1)}, u32[]{:S(2)}) copy-start(bf16[8,2,512,512]{3,2,1,0:T(8,128)(2,1)} %copy-done) | copy-start | bytes 25165828
  81.8 3.4 %copy-start.4 = (bf16[8,2,512,512]{3,2,1,0:T(8,128)(2,1)S(1)}, bf16[8,2,512,512]{3,2,1,0:T(8,128)(2,1)}, u32[]{:S(2)}) copy-start(bf16[8,2,512,512]{3,2,1,0:T(8,128)(2,1)} %copy-done.3) | copy-start | bytes 25165828
  93.6 9.8 %collective-permute-start.1 = (f32[4,512]{1,0:T(4,128)S(1)}, f32[4,512]{1,0:T(4,128)S(1)}, u32[]{:S(2)}, u32[]{:S(2)}) collective-permute-start(f32[4,512]{1,0:T(4,128)S(1)} %get-tuple-element.38), channel_id=1, source_target_pairs={{0,16},{1,17},{2,18},{3,19},{4,20},{5,21},{6,22},{7,23},{8,24},{9,... | collective-permute-start | bytes 24584 | tf_op jit(solution)/shard_map/ppermute | solution.py:419
  101.8 20.8 %collective-permute-start.2 = (f32[4,512]{1,0:T(4,128)S(1)}, f32[4,512]{1,0:T(4,128)S(1)}, u32[]{:S(2)}, u32[]{:S(2)}) collective-permute-start(f32[4,512]{1,0:T(4,128)S(1)} %slice_bitcast_fusion), channel_id=1, source_target_pairs={{16,0},{17,1},{18,2},{19,3},{20,4},{21,5},{22,6},{23,7},{24,8},{25... | collective-permute-start | bytes 24584 | tf_op jit(solution)/shard_map/ppermute | solution.py:421
  103.4 3.4 %copy-start.2 = (bf16[8,2,512,512]{3,2,1,0:T(8,128)(2,1)S(1)}, bf16[8,2,512,512]{3,2,1,0:T(8,128)(2,1)}, u32[]{:S(2)}) copy-start(bf16[8,2,512,512]{3,2,1,0:T(8,128)(2,1)} %copy-done) | copy-start | bytes 25165828
  106.8 3.4 %copy-start.5 = (bf16[8,2,512,512]{3,2,1,0:T(8,128)(2,1)S(1)}, bf16[8,2,512,512]{3,2,1,0:T(8,128)(2,1)}, u32[]{:S(2)}) copy-start(bf16[8,2,512,512]{3,2,1,0:T(8,128)(2,1)} %copy-done.3) | copy-start | bytes 25165828
  122.6 33.2 %copy-start.16 = (f32[32,512]{1,0:T(8,128)S(1)}, f32[32,512]{1,0:T(8,128)}, u32[]{:S(2)}) copy-start(f32[32,512]{1,0:T(8,128)} %refs_0_.1) | copy-start | bytes 196612
  122.6 33.7 %copy-start.13 = (f32[8,7,64,64]{3,2,1,0:T(8,128)S(1)}, f32[8,7,64,64]{3,2,1,0:T(8,128)}, u32[]{:S(2)}) copy-start(f32[8,7,64,64]{3,2,1,0:T(8,128)} %tiles.3) | copy-start | bytes 2752516
  122.7 33.7 %copy-start.19 = (s32[8,7]{1,0:T(8,128)S(1)}, s32[8,7]{1,0:T(8,128)}, u32[]{:S(2)}) copy-start(s32[8,7]{1,0:T(8,128)} %columns.3) | copy-start | bytes 676
  128.7 18.4 %all-to-all-start.2 = ((f32[16,3,4,512]{3,2,1,0:T(4,128)}), f32[16,3,4,512]{3,2,1,0:T(4,128)S(1)}, u32[]{:S(2)}, u32[]{:S(2)}) async-start(f32[16,3,4,512]{3,2,1,0:T(4,128)} %bitcast.5), calls=%async_computation.2 | async-start | bytes 786432 | tf_op jit(solution)/shard_map/all_to_all | solution.py:448
  147.1 12.8 %collective-permute-start.8 = (f32[2,8,3,4,512]{4,3,2,1,0:T(4,128)S(1)}, f32[2,8,3,4,512]{4,3,2,1,0:T(4,128)S(1)}, u32[]{:S(2)}, u32[]{:S(2)}) collective-permute-start(f32[2,8,3,4,512]{4,3,2,1,0:T(4,128)S(1)} %bitcast.10), channel_id=1, source_target_pairs={{0,1},{1,0},{2,3},{3,2},{4,5},{5,4},{6,7},{7,6},{8,9},{9,8},{10,11... | collective-permute-start | bytes 1179656 | tf_op jit(solution)/shard_map/ppermute | solution.py:358
  155.9 3.1 %collective-permute-start.3 = (f32[8,2,4,512]{3,2,1,0:T(4,128)S(1)}, f32[8,2,4,512]{3,2,1,0:T(4,128)S(1)}, u32[]{:S(2)}, u32[]{:S(2)}) collective-permute-start(f32[8,2,4,512]{3,2,1,0:T(4,128)S(1)} %all_to_all.15.refs_2_), channel_id=1, source_target_pairs={{0,1},{1,0},{2,3},{3,2},{4,5},{5,4},{6,7},{7,6},{8,9},{9,8},{10,11... | collective-permute-start | bytes 393224 | tf_op jit(solution)/shard_map/ppermute | solution.py:358
  155.9 3.1 %collective-permute-start = (f32[32,512]{1,0:T(8,128)S(1)}, f32[32,512]{1,0:T(8,128)S(1)}, u32[]{:S(2)}, u32[]{:S(2)}) collective-permute-start(f32[32,512]{1,0:T(8,128)S(1)} %copy-done.16), channel_id=1, source_target_pairs={{0,1},{1,0},{2,3},{3,2},{4,5},{5,4},{6,7},{7,6},{8,9},{9,8},{10,11... | collective-permute-start | bytes 196616 | tf_op jit(solution)/shard_map/ppermute | solution.py:358
  159.4 4.9 %collective-permute-start.4 = (f32[2,64,64]{2,1,0:T(8,128)S(1)}, f32[2,64,64]{2,1,0:T(8,128)S(1)}, u32[]{:S(2)}, u32[]{:S(2)}) collective-permute-start(f32[2,64,64]{2,1,0:T(8,128)S(1)} %get-tuple-element.44), channel_id=1, source_target_pairs={{0,2},{2,0},{4,6},{6,4},{8,10},{10,8},{12,14},{14,12},{1,3},{3,1},... | collective-permute-start | bytes 98312 | tf_op jit(solution)/shard_map/ppermute | solution.py:358
  160.8 4.4 %collective-permute-start.9 = (f32[2,64,64]{2,1,0:T(8,128)S(1)}, f32[2,64,64]{2,1,0:T(8,128)S(1)}, u32[]{:S(2)}, u32[]{:S(2)}) collective-permute-start(f32[2,64,64]{2,1,0:T(8,128)S(1)} %get-tuple-element.49), channel_id=1, source_target_pairs={{0,2},{2,0},{4,6},{6,4},{8,10},{10,8},{12,14},{14,12},{1,3},{3,1},... | collective-permute-start | bytes 98312 | tf_op jit(solution)/shard_map/ppermute | solution.py:358
  164.4 4.3 %collective-permute-start.5 = (f32[2,64,64]{2,1,0:T(8,128)S(1)}, f32[2,64,64]{2,1,0:T(8,128)S(1)}, u32[]{:S(2)}, u32[]{:S(2)}) collective-permute-start(f32[2,64,64]{2,1,0:T(8,128)S(1)} %add.24), channel_id=1, source_target_pairs={{0,4},{2,6},{4,0},{6,2},{8,12},{10,14},{12,8},{14,10},{1,5},{3,7},... | collective-permute-start | bytes 98312 | tf_op jit(solution)/shard_map/ppermute | solution.py:358
  165.2 4.3 %collective-permute-start.10 = (f32[2,64,64]{2,1,0:T(8,128)S(1)}, f32[2,64,64]{2,1,0:T(8,128)S(1)}, u32[]{:S(2)}, u32[]{:S(2)}) collective-permute-start(f32[2,64,64]{2,1,0:T(8,128)S(1)} %add.28), channel_id=1, source_target_pairs={{0,4},{2,6},{4,0},{6,2},{8,12},{10,14},{12,8},{14,10},{1,5},{3,7},... | collective-permute-start | bytes 98312 | tf_op jit(solution)/shard_map/ppermute | solution.py:358
  168.7 4.6 %collective-permute-start.6 = (f32[2,64,64]{2,1,0:T(8,128)S(1)}, f32[2,64,64]{2,1,0:T(8,128)S(1)}, u32[]{:S(2)}, u32[]{:S(2)}) collective-permute-start(f32[2,64,64]{2,1,0:T(8,128)S(1)} %add.25), channel_id=1, source_target_pairs={{0,8},{2,10},{4,12},{6,14},{8,0},{10,2},{12,4},{14,6},{1,9},{3,11}... | collective-permute-start | bytes 98312 | tf_op jit(solution)/shard_map/ppermute | solution.py:358
  169.5 5.4 %collective-permute-start.11 = (f32[2,64,64]{2,1,0:T(8,128)S(1)}, f32[2,64,64]{2,1,0:T(8,128)S(1)}, u32[]{:S(2)}, u32[]{:S(2)}) collective-permute-start(f32[2,64,64]{2,1,0:T(8,128)S(1)} %add.29), channel_id=1, source_target_pairs={{0,8},{2,10},{4,12},{6,14},{8,0},{10,2},{12,4},{14,6},{1,9},{3,11}... | collective-permute-start | bytes 98312 | tf_op jit(solution)/shard_map/ppermute | solution.py:358
  173.4 5.9 %collective-permute-start.7 = (f32[2,64,64]{2,1,0:T(8,128)S(1)}, f32[2,64,64]{2,1,0:T(8,128)S(1)}, u32[]{:S(2)}, u32[]{:S(2)}) collective-permute-start(f32[2,64,64]{2,1,0:T(8,128)S(1)} %add.26), channel_id=1, source_target_pairs={{0,16},{16,0},{1,17},{17,1},{2,18},{18,2},{3,19},{19,3},{4,20},{20... | collective-permute-start | bytes 98312 | tf_op jit(solution)/shard_map/ppermute | solution.py:358
  175.0 9.8 %collective-permute-start.12 = (f32[2,64,64]{2,1,0:T(8,128)S(1)}, f32[2,64,64]{2,1,0:T(8,128)S(1)}, u32[]{:S(2)}, u32[]{:S(2)}) collective-permute-start(f32[2,64,64]{2,1,0:T(8,128)S(1)} %add.30), channel_id=1, source_target_pairs={{0,16},{16,0},{1,17},{17,1},{2,18},{18,2},{3,19},{19,3},{4,20},{20... | collective-permute-start | bytes 98312 | tf_op jit(solution)/shard_map/ppermute | solution.py:358
  (13 other events, 25.8 us)
Sparse Core Ops, SparseCore 0:
  12.2 38.1 all-gather.2
  52.5 28.9 all-gather.4

commit v2 on v1

v2 whole, which is shorter than its diff:
```python
import functools
import jax
import jax.numpy as jnp
from jax import lax
from jax.experimental import pallas as pl
from jax.experimental.pallas import tpu as pltpu
from jax.sharding import Mesh, PartitionSpec as P

SPAN = 8
F32 = jnp.float32
BF16 = jnp.bfloat16
HIGHEST = lax.Precision.HIGHEST
NN = (((1,), (0,)), ((), ()))
NT = (((1,), (1,)), ((), ()))
VMEM = pl.BlockSpec(memory_space=pltpu.VMEM)
SMEM = pl.BlockSpec(memory_space=pltpu.SMEM)


def call(kernel, name, out_shape, in_specs, out_specs=VMEM, scratch=(), aliases=None, cost=1):
    return pl.pallas_call(
        kernel,
        out_shape=out_shape,
        in_specs=in_specs,
        out_specs=out_specs,
        scratch_shapes=list(scratch),
        input_output_aliases=aliases or {},
        cost_estimate=pl.CostEstimate(flops=int(cost * 1e9), bytes_accessed=0, transcendentals=0),
        compiler_params=pltpu.CompilerParams(vmem_limit_bytes=16 * 2**20),
        name=name,
    )


def two_parts(x):
    high = x.astype(BF16).astype(F32)
    return jnp.concatenate([high, x - high], axis=0).astype(BF16)


def halves(x):
    high = x.astype(BF16)
    return high, (x - high.astype(F32)).astype(BF16)


def product(x, high, low, dims):
    parts = two_parts(x)
    both = lax.dot_general(parts, high, dims, preferred_element_type=F32)
    both = both + lax.dot_general(parts, low, dims, preferred_element_type=F32)
    rows = x.shape[0]
    return both[:rows] + both[rows:]


def offsets_of(columns, start):
    found = []
    for offset in range(1, 8):
        hit = jnp.int32(0)
        for slot in range(7):
            away = columns[0, slot] - start
            hit = hit | jnp.where((away == offset) | (away == -offset), 1, 0)
        found.append(hit * 16 + offset)
    first = functools.reduce(jnp.maximum, found)
    second = functools.reduce(jnp.maximum, [jnp.where(f == first, 0, f) for f in found])
    first, second = (first & 15, second & 15)
    return (jnp.minimum(first, second), jnp.maximum(first, second), jnp.int32(8))


def pack_kernel(rows_part, columns, tiles, pivots, own, part, offsets):
    shard_rows, slots, order, _ = tiles.shape
    start = (lax.axis_index("blk") * SPAN + lax.axis_index("pos")) * shard_rows
    offs = offsets_of(columns, start)
    for k in range(3):
        offsets[0, k] = offs[k]
    at = [lax.broadcasted_iota(jnp.int32, (order, order), d) for d in range(2)]
    for row in range(shard_rows):
        sums = [jnp.zeros((order, order), F32) for _ in range(4)]
        for slot in range(slots):
            away = columns[row, slot] - (start + row)
            tile = tiles[row, slot]
            for k, want in enumerate((*offs, 0)):
                sums[k] = sums[k] + tile * jnp.where(away == want, 1.0, 0.0)
        both = jnp.where(at[0] <= at[1], pivots[row], sums[3])
        line = jnp.sum(jnp.where(at[0] == at[1], sums[3], 0.0), axis=0, keepdims=True)
        own[row, :order] = jnp.concatenate([sums[0], sums[1]], axis=1)
        own[row, order : 2 * order] = jnp.concatenate([sums[2], both], axis=1)
        own[row, 2 * order :] = jnp.broadcast_to(jnp.concatenate([line, line], axis=1), (8, 2 * order))
    for r in range(rows_part):
        part[r] = own[lax.axis_index("rhs") * rows_part + r]


def band_kernel(columns, tiles, band_high, band_low, band):
    shard_rows, slots, order, _ = tiles.shape
    start = (lax.axis_index("blk") * SPAN + lax.axis_index("pos")) * shard_rows
    band[...] = jnp.zeros_like(band)
    for row in range(shard_rows):
        for slot in range(slots):
            away = columns[row, slot] - start + shard_rows
            where = pl.ds(pl.multiple_of(away * order, order), order)
            lanes = pl.ds(row * order, order)
            band[where, lanes] = band[where, lanes] + tiles[row, slot].T
    high, low = halves(band[...])
    band_high[...] = high
    band_low[...] = low


def stage_rows(stage, t, pieces):
    rows_part = pieces[0][0].shape[0]
    base = (lax.axis_index("rhs") ^ t) * rows_part
    for r in range(rows_part):
        top = 0
        for ref, first, rows in pieces:
            stage[base + r, top : top + rows] = ref[r, first : first + rows]
            top += rows


def factors(offsets, stages, groups, m_high, m_low, w_high, w_low, g_high, g_low):
    order = 64
    cells = 8 * order
    o = [offsets[0, k] for k in range(3)]
    at = [lax.broadcasted_iota(jnp.int32, (order, order), d) for d in range(2)]
    lane = lax.broadcasted_iota(jnp.int32, (order, 2 * order), 1)
    pivots = {}
    for n, (stage, s) in enumerate(zip(stages, groups)):
        for i in range(8):
            for k in range(3):
                from_row = (i - o[k]) & 7
                kind = jnp.where(o[k] > i, 0, 1)
                tile = stage[
                    from_row,
                    k // 2 * order : (k // 2 + 1) * order,
                    k % 2 * order : (k % 2 + 1) * order,
                ]
                high, low = halves(tile)
                where = pl.ds(pl.multiple_of(from_row * order, order), order)
                lanes = slice(i * order, (i + 1) * order)
                m_high[s, kind, where, lanes] = high
                m_low[s, kind, where, lanes] = low
            both = stage[i, order : 2 * order, order:]
            turned = both.T
            pivots[n, i] = jnp.where(at[0] <= at[1], both, turned)
            line = stage[i, 2 * order : 2 * order + 1, :order]
            tile = jnp.where(at[0] > at[1], both, jnp.where(at[0] < at[1], turned, line))
            high, low = halves(tile)
            where = slice(i % 2 * order, (i % 2 + 1) * order)
            g_high[s, i // 2, where, where] = high
            g_low[s, i // 2, where, where] = low
    lefts = {}
    for n, stage in enumerate(stages):
        for j in range(7):
            inside = [jnp.where(o[k] + j <= 7, 1.0, 0.0) for k in range(2)]
            pair = stage[j, :order] * jnp.where(lane < order, inside[0], inside[1])
            left = two_parts(product(pivots[n, j], *halves(pair), NN))
            lefts[n, j] = jnp.concatenate([left, left], axis=1)
    for j in range(7, -1, -1):
        for n, s in enumerate(groups):
            row = jnp.pad(pivots[n, j], ((0, 0), (j * order, cells - (j + 1) * order)))
            if j < 7:
                where = [
                    pl.ds(pl.multiple_of(jnp.minimum(o[k] + j, 7) * order, order), order)
                    for k in range(2)
                ]
                first = (j + 1) // 4 * 256
                right = jnp.concatenate(
                    [w[s, where[k], first:] for w in (w_high, w_low) for k in range(2)], axis=0
                )
                both = lax.dot_general(lefts[n, j], right, NN, preferred_element_type=F32)
                away = both[:order] + both[order:]
                if first:
                    away = jnp.pad(away, ((0, 0), (first, 0)))
                row = row - away
            high, low = halves(row)
            w_high[s, j * order : (j + 1) * order] = high
            w_low[s, j * order : (j + 1) * order] = low


def own_factor_kernel(offsets, own, m_high, m_low, w_high, w_low, g_high, g_low):
    for ref in (m_high, m_low, g_high, g_low):
        ref[...] = jnp.zeros_like(ref)
    mats = (m_high, m_low, w_high, w_low, g_high, g_low)
    factors(offsets, [own], [lax.axis_index("pos")], *mats)


def factor_kernel(layout, count, ins, mats, outs, scratch):
    offsets, given = ins[0], ins[1:]
    staged, groups = [], []
    for n, (mask, pieces) in enumerate(layout):
        stage = scratch[0].at[n]
        for t in range(count):
            stage_rows(stage, t, [(given[i * count + t], first, rows) for i, first, rows in pieces])
        staged.append(stage)
        groups.append(lax.axis_index("pos") ^ mask)
    factors(offsets, staged, groups, *mats)


def upper(x, high, low):
    half = high.shape[0] // 2
    return jnp.concatenate(
        [
            product(x[:, :half], high[:half, :half], low[:half, :half], NN),
            product(x, high[:, half:], low[:, half:], NN),
        ],
        axis=1,
    )


def upper_t(x, high, low):
    half = high.shape[0] // 2
    return jnp.concatenate(
        [
            product(x, high[:half], low[:half], NT),
            product(x[:, half:], high[half:, half:], low[half:, half:], NT),
        ],
        axis=1,
    )


def lower(x, high, low):
    half = high.shape[0] // 2
    return jnp.concatenate(
        [
            product(x, high[:, :half], low[:, :half], NN),
            product(x[:, half:], high[half:, half:], low[half:, half:], NN),
        ],
        axis=1,
    )


def lower_t(x, high, low):
    half = high.shape[0] // 2
    return jnp.concatenate(
        [
            product(x[:, :half], high[:half, :half], low[:half, :half], NT),
            product(x, high[half:], low[half:], NT),
        ],
        axis=1,
    )


def forward_step(s, source, before, m, w):
    if before is not None:
        source = source - lower(before, m[0].at[s - 1, 0], m[1].at[s - 1, 0])
    value = upper(source, w[0].at[s], w[1].at[s])
    return value, source - upper(value, m[0].at[s, 1], m[1].at[s, 1])


def first_kernel(mats, r, t, top):
    m, w = mats[:2], mats[2:4]
    value = None
    for s in range(8):
        value, t[s] = forward_step(s, r[s], value, m, w)
    z = upper_t(t[7], w[0][7], w[1][7])
    top[0] = z
    top[1] = lower(z, m[0][7, 0], m[1][7, 0])


def spread(out, values):
    zero = jnp.zeros_like(values[0])
    for s in range(8):
        for side in range(3):
            out[s, side] = values[s + side - 1] if 0 <= s + side - 1 < 8 else zero


def second_kernel(mats, t, top, z, above, out, ends):
    m, w = mats[:2], mats[2:4]
    value = top[0]
    values = {7: value}
    for s in range(6, -1, -1):
        above[s] = lower_t(value, m[0][s, 0], m[1][s, 0])
        value = upper_t(t[s] - above[s], w[0][s], w[1][s])
        values[s] = value
    above[7] = jnp.zeros_like(value)
    for s in range(8):
        z[s] = values[s]
    spread(out, values)
    ends[:2] = top[...]
    ends[2] = value


def third_kernel(mats, r, t, z, above, source, t_left):
    m, g = mats[:2], mats[4:]
    for s in range(8):
        x = z[s]
        ahead = upper_t(x, m[0][s, 1], m[1][s, 1]) + above[s]
        own = [
            product(x[:, i * 128 : (i + 1) * 128], g[0][s, i], g[1][s, i], NN) for i in range(4)
        ]
        t_left[s] = t[s] - ahead
        source[s] = jnp.concatenate(own, axis=1) + ahead - t_left[s] - r[s]


def fourth_kernel(mats, source, t_left, from_below, from_above, t, last):
    m, w = mats[:2], mats[2:4]
    before = None
    for s in range(8):
        start = source[s]
        if s == 0:
            start = start + from_below[1]
        if s == 7:
            start = start + lower_t(from_above[2], m[0][7, 0], m[1][7, 0])
        before, more = forward_step(s, start, before, m, w)
        t[s] = t_left[s] + more
    last[...] = upper_t(t[7], w[0][7], w[1][7])


def fifth_kernel(mats, t, last, out):
    m, w = mats[:2], mats[2:4]
    value = last[...]
    values = {7: value}
    for s in range(6, -1, -1):
        ahead = lower_t(value, m[0][s, 0], m[1][s, 0])
        value = upper_t(t[s] - ahead, w[0][s], w[1][s])
        values[s] = value
    spread(out, values)


def place_rows(place, t, rhs, rows, lanes=slice(None)):
    count = rows.shape[0]
    place[pl.ds(pl.multiple_of((rhs ^ t) * count, count), count), lanes] = rows


def image_of(pieces, wide, band_high, band_low):
    rhs, cells = lax.axis_index("rhs"), pieces[0].shape[3]
    for t, piece in enumerate(pieces):
        for side in range(3):
            rows = jnp.concatenate([piece[j, side] for j in range(SPAN)], axis=0)
            place_rows(wide, t, rhs, rows, slice(side * cells, (side + 1) * cells))
    below = product(wide[:, :cells], band_high[:cells], band_low[:cells], NN)
    image = below + product(wide[:, cells:], band_high[cells:], band_low[cells:], NN)
    twice = image + below * jnp.where(lax.axis_index("pos") == 0, 1.0, 0.0)
    return wide[:, cells : 2 * cells], image, twice


def inner(a, b):
    return lax.dot_general(a, b, NT, precision=HIGHEST, preferred_element_type=F32)


def early_kernel(n, *refs):
    r_pieces, pieces = refs[:n], refs[n : 2 * n]
    band_high, band_low, r, d, q, sums, wide = refs[2 * n :]
    for t in range(n):
        place_rows(r, t, lax.axis_index("rhs"), r_pieces[t][...])
    d[...], q[...], twice = image_of(pieces, wide, band_high, band_low)
    sums[0] = inner(d[...], r[...])
    sums[1] = inner(d[...], twice)


def late_kernel(n, *refs):
    pieces = refs[:n]
    q, band_high, band_low, e, w, sums, wide = refs[n:]
    e[...], w[...], twice = image_of(pieces, wide, band_high, band_low)
    sums[0] = inner(e[...], q[...])
    sums[1] = inner(e[...], twice)


def complete_kernel(value, arrived, band_high, band_low, out):
    cells = value.shape[1]
    above = slice(2 * cells, 3 * cells)
    out[...] = value[...] + product(arrived[...], band_high[above], band_low[above], NN)


def small(a, b):
    return lax.dot_general(a, b, NN, precision=HIGHEST, preferred_element_type=F32)


def inverse(a):
    size = a.shape[0]
    row_at = lax.broadcasted_iota(jnp.int32, a.shape, 0)
    col_at = lax.broadcasted_iota(jnp.int32, a.shape, 1)
    for k in range(size):
        scale = 1.0 / a[k : k + 1, k : k + 1]
        row = jnp.where(col_at[:1] == k, 1.0, a[k : k + 1, :]) * scale
        column = a[:, k : k + 1]
        rest = jnp.where(col_at == k, 0.0, a)
        a = jnp.where(row_at == k, row, rest - column * row)
    return a


def symmetric(a):
    return 0.5 * (a + a.T)


def invert_kernel(sums, inverted):
    inverted[...] = inverse(symmetric(sums[1]))


def last_kernel(early, late, inverted, r, d, q, e, w, solution, residual):
    count = solution.shape[0]
    rhs = lax.axis_index("rhs")
    s1, s2 = symmetric(early[0]), symmetric(early[1])
    s3, s4 = symmetric(late[0]), symmetric(late[1])
    inv = inverted[...]
    c = small(inv, s3)
    schur = symmetric(s4 - small(s3, c))
    h = small(s2 - s1 - small(s1, c), inverse(schur))
    f = small(s1 - small(h, s3), inv)
    pick = lax.broadcasted_iota(jnp.int32, (count, s1.shape[0]), 0) + rhs * count
    pick = jnp.where(pick == lax.broadcasted_iota(jnp.int32, pick.shape, 1), 1.0, 0.0)
    f, h = small(pick, f), small(pick, h)
    solution[...] = small(f, d[...]) + small(h, e[...])
    own = r[pl.ds(pl.multiple_of(rhs * count, count), count), :]
    residual[...] = own - small(f, q[...]) - small(h, w[...])


def swapped(value, axis, bit):
    return lax.ppermute(value, axis, [(i, i ^ bit) for i in range(lax.axis_size(axis))])


def summed(value):
    axes = ("blk", "pos")
    size = lax.axis_size(axes)
    bit = 1
    while bit < size:
        near = value + swapped(value, axes, bit)
        if 2 * bit < size:
            near = near + (swapped(value, axes, 2 * bit) + swapped(value, axes, 3 * bit))
        value = near
        bit *= 4
    return value


def both_ways(value):
    blocks = lax.axis_size("blk")
    low = high = None
    for first in range(min(2, blocks - 1)):
        pairs = [(i, i + 1) for i in range(first, blocks - 1, 2)]
        got = lax.ppermute(value, "blk", pairs + [(b, a) for a, b in pairs])
        even = lax.axis_index("blk") % 2 == first
        up, down = jnp.where(even, 0.0, got), jnp.where(even, got, 0.0)
        low, high = (up, down) if low is None else (low + up, high + down)
    return low, high


def shards(right_side, tiles, pivots, columns):
    count, cells = right_side.shape
    shard_rows, slots, order, _ = tiles.shape
    parts = lax.axis_size("rhs")
    blocks = lax.axis_size("blk")
    rows_part = shard_rows // parts
    each = count // SPAN
    total = count * parts
    S = jax.ShapeDtypeStruct
    up = [(i, i + 1) for i in range(blocks - 1)]
    down_rows = [(SPAN * (i + 1), SPAN * (i + 1) - 1) for i in range(blocks - 1)]

    def others(value):
        return [value] + [swapped(value, "rhs", t) for t in range(1, parts)]

    tall = 2 * order + 8
    own, part, offsets = call(
        functools.partial(pack_kernel, rows_part),
        "pack_tiles",
        [
            S((shard_rows, tall, 2 * order), F32),
            S((rows_part, tall, 2 * order), F32),
            S((1, 3), jnp.int32),
        ],
        [SMEM, VMEM, VMEM],
        [VMEM, VMEM, SMEM],
        cost=2,
    )(columns, tiles, pivots)

    x, y, z = (swapped(part, "pos", bit) for bit in (1, 2, 4))
    mat_shapes = [
        pltpu.VMEM((SPAN, 2, cells, cells), BF16),
        pltpu.VMEM((SPAN, 2, cells, cells), BF16),
        pltpu.VMEM((SPAN, cells, cells), BF16),
        pltpu.VMEM((SPAN, cells, cells), BF16),
        pltpu.VMEM((SPAN, 4, 2 * order, 2 * order), BF16),
        pltpu.VMEM((SPAN, 4, 2 * order, 2 * order), BF16),
    ]
    r = lax.all_to_all(right_side.reshape(SPAN, each, cells), "pos", 0, 0, tiled=True)
    own, r = lax.optimization_barrier((own, r))
    mats = call(own_factor_kernel, "factors_own", mat_shapes, [SMEM, VMEM], [VMEM] * 6, cost=4)(
        offsets, own
    )
    band_high, band_low = call(
        band_kernel,
        "row_band",
        [S((3 * cells, cells), BF16)] * 2,
        [SMEM, VMEM],
        [VMEM] * 2,
        [pltpu.VMEM((3 * cells, cells), F32)],
        cost=3,
    )(columns, tiles)

    def with_mats(kernel, name, specs, out_shapes, given, scratch=(), cost=1):
        nonlocal mats
        first, outs = len(given), len(out_shapes)

        def body(*refs):
            ins, rest = refs[:first], refs[first + 6 :]
            kernel(ins, rest[outs : outs + 6], rest[:outs], rest[outs + 6 :])

        *results, m0, m1, w0, w1, g0, g1 = call(
            body,
            name,
            [*out_shapes, *mat_shapes],
            [*specs, *[VMEM] * 6],
            [VMEM] * (outs + 6),
            scratch,
            {first + i: outs + i for i in range(6)},
            cost,
        )(*given, *mats)
        mats = [m0, m1, w0, w1, g0, g1]
        return results

    def add_factors(name, layout, operands, cost):
        given = [offsets] + [piece for operand in operands for piece in others(operand)]
        with_mats(
            functools.partial(factor_kernel, layout, parts),
            name,
            [SMEM] + [VMEM] * (len(given) - 1),
            [],
            given,
            [pltpu.VMEM((len(layout), shard_rows, tall, 2 * order), F32)],
            cost,
        )

    def sweep(kernel, name, out_shapes, *given, cost=1):
        def body(ins, held, outs, scratch):
            kernel(held, *ins, *outs)

        return with_mats(body, name, [VMEM] * len(given), out_shapes, given, cost=cost)

    join = lambda *pieces: jnp.concatenate(pieces, axis=1)
    xs = swapped(join(y[:, :order], z[:, :order]), "pos", 1)
    ys = swapped(join(x[:, order:], z[:, :order]), "pos", 2)
    zs = swapped(join(x[:, order:], y[:, order:]), "pos", 4)
    rest = tall - order
    far_top = swapped(ys[:, rest:], "pos", 1)
    far_low = swapped(ys[:, :rest], "pos", 4)
    add_factors(
        "factors_near", [(bit, [(i, 0, tall)]) for i, bit in enumerate((1, 2, 4))], [x, y, z], 6
    )
    add_factors(
        "factors_mid",
        [
            (3, [(0, 0, order), (1, 0, rest)]),
            (5, [(0, order, order), (2, 0, rest)]),
            (6, [(1, rest, order), (2, rest, rest)]),
        ],
        [xs, ys, zs],
        6,
    )
    add_factors("factors_far", [(7, [(0, 0, order), (1, 0, rest)])], [far_top, far_low], 3)

    r_pieces = others(right_side)
    vectors, vector = S((SPAN, each, cells), F32), S((each, cells), F32)
    ends_shape, spread_shape = S((3, each, cells), F32), S((SPAN, 3, each, cells), F32)
    t, top = sweep(first_kernel, "forward_r", [vectors, S((2, each, cells), F32)], r, cost=4)
    z, above, spread_z, ends = sweep(
        second_kernel, "backward_r", [vectors, vectors, spread_shape, ends_shape], t, top, cost=4
    )
    from_below, from_above = both_ways(ends)
    source, t_left = sweep(third_kernel, "residue_of_z", [vectors] * 2, r, t, z, above, cost=2)
    spread_z = (spread_z.at[0, 0].set(from_below[0]))
    t, last = sweep(
        fourth_kernel, "forward_v", [vectors, vector], source, t_left, from_below, from_above, cost=4
    )
    from_below = lax.ppermute(last, "blk", up)
    (spread_e,) = sweep(fifth_kernel, "backward_v", [spread_shape], t, last, cost=4)
    both = jnp.stack([spread_z, spread_e.at[0, 0].set(from_below)], axis=1)
    both = lax.all_to_all(both, "pos", 0, 0, tiled=True)
    spread_z, spread_e = both[:, 0], both[:, 1]

    full, two = S((total, cells), F32), S((2, total, total), F32)
    wide = pltpu.VMEM((total, 3 * cells), F32)
    r_full, d_full, q_part, early = call(
        functools.partial(early_kernel, parts),
        "products_d",
        [full, full, full, two],
        [VMEM] * (2 * parts + 2),
        [VMEM] * 4,
        [wide],
    )(*r_pieces, *others(spread_z), band_high, band_low)
    d_above = lax.ppermute(d_full, ("blk", "pos"), down_rows)
    early = summed(early)
    inverted = call(invert_kernel, "invert", S((total, total), F32), [VMEM])(early)
    complete = call(complete_kernel, "complete", full, [VMEM] * 4)
    q_full = complete(q_part, d_above, band_high, band_low)

    e_full, w_part, late = call(
        functools.partial(late_kernel, parts),
        "products_e",
        [full, full, two],
        [VMEM] * (parts + 3),
        [VMEM] * 3,
        [wide],
    )(*others(spread_e), q_full, band_high, band_low)
    late = summed(late)
    e_above = lax.ppermute(e_full, ("blk", "pos"), down_rows)
    w_full = complete(w_part, e_above, band_high, band_low)
    return call(
        last_kernel, "update", [S((count, cells), F32)] * 2, [VMEM] * 8, [VMEM] * 2
    )(early, late, inverted, r_full, d_full, q_full, e_full, w_full)


def solution(mesh):
    devices = mesh.devices
    split = Mesh(
        devices.reshape(devices.shape[0] // SPAN, SPAN, devices.shape[1]), ("blk", "pos", "rhs")
    )
    rows = ("blk", "pos")
    return jax.shard_map(
        shards,
        mesh=split,
        in_specs=(
            P("rhs", rows),
            P(rows, None, None, None),
            P(rows, None, None),
            P(rows, None),
        ),
        out_specs=(P("rhs", rows), P("rhs", rows)),
        check_vma=False,
    )
```

time: 200 us -> 132 us (0.66)
  the two profiles are of different devices: /device:TPU:0 before, /device:TPU:14 now
where the time goes in v2:
time: 132 us
  Pallas kernels  56.1 us (42%)
  starting transfers between devices  44.9 us (34%)
  waiting for transfers between devices  25 us (19%)
  local copies, waits for them, and re-layouts  4.69 us (4%)
    pallas_call x8, Pallas kernels, with_mats(): call(body, name, [*out_shapes, *mat_shapes], [*specs, *[VMEM] * 6], [VMEM...  32.6 us
    ppermute x31, starting transfers between devices, swapped(): lax.ppermute(value, axis, [(i, i ^ bit) for i in range(lax.axis_size(axis...  22.9 us
    pallas_call x1, Pallas kernels, shards(): call(last_kernel, 'update', [S((count, cells), F32)] * 2, [VMEM] * 8, [VM...  7.54 us
    ppermute x1, waiting for transfers between devices, shards(): e_above = lax.ppermute(e_full, ('blk', 'pos'), down_rows)  7.3 us
    all_to_all x1, starting transfers between devices, shards(): lax.all_to_all(right_side.reshape(SPAN, each, cells), 'pos', 0, 0, tiled=...  7.13 us
    ppermute x31, waiting for transfers between devices, swapped(): lax.ppermute(value, axis, [(i, i ^ bit) for i in range(lax.axis_size(axis...  6.56 us
    pallas_call x1, Pallas kernels, shards(): call(invert_kernel, 'invert', S((total, total), F32), [VMEM])(early)  5.45 us
    all_to_all x1, starting transfers between devices, shards(): both = lax.all_to_all(both, 'pos', 0, 0, tiled=True)  5.11 us
  transfers between devices with their start and end apart: 37, of which 10 were waited for; matrix products, arithmetic and copies ran while one was open for 1% of the time, Pallas kernels for 23%

profile of v2, /device:TPU:14, one launch (start us, length us, event | category | flops | bytes accessed | tf_op | source)
XLA Modules:
  0.0 132.0 jit_solution(15531991293075687916)
XLA Ops:
  7.4 7.1 %all-to-all-start = ((f32[8,4,512]{2,1,0:T(4,128)}), f32[8,4,512]{2,1,0:T(4,128)S(1)}, u32[]{:S(2)}, u32[]{:S(2)}) async-start(f32[8,4,512]{2,1,0:T(4,128)} %reshape.84), calls=%async_computation | async-start | bytes 131072 | tf_op jit(solution)/shard_map/all_to_all | solution.py:468
  15.2 2.1 %all-to-all-done.refs_0_ = f32[8,4,512]{2,1,0:T(4,128)S(1)} async-done(((f32[8,4,512]{2,1,0:T(4,128)}), f32[8,4,512]{2,1,0:T(4,128)S(1)}, u32[]{:S(2)}, u32[]{:S(2)}) %all-to-all-start) | async-done | bytes 65568 | tf_op jit(solution)/shard_map/all_to_all | solution.py:468
  21.9 3.7 %factors_own.1 = (bf16[8,2,512,512]{3,2,1,0:T(8,128)(2,1)S(1)}, bf16[8,2,512,512]{3,2,1,0:T(8,128)(2,1)S(1)}, bf16[8,512,512]{2,1,0:T(8,128)(2,1)S(1)}, bf16[8,5...) custom-call(s32[1,3]{1,0:T(1,128)S(1)} %get-tuple-element.101.offsets.refs_0_, ...), custom_call_target="tpu_custom_call" | custom-call | flops 4000000000 | tf_op jit(solution)/shard_map/factors_own/pallas_call | solution.py:470
  28.7 5.6 %factors_near.1 = (bf16[8,2,512,512]{3,2,1,0:T(8,128)(2,1)S(1)}, bf16[8,2,512,512]{3,2,1,0:T(8,128)(2,1)S(1)}, bf16[8,512,512]{2,1,0:T(8,128)(2,1)S(1)}, bf16[8,...) custom-call(s32[1,3]{1,0:T(1,128)S(1)} %get-tuple-element.101.offset, ...), custom_call_target="tpu_custom_call", output_to_operand_aliasing={{0}: (7, {}), {1}: (8, {}), {2}: (9, {}), {3}: (10, {}), {4... | custom-call | flops 6000000000 | tf_op jit(solution)/shard_map/factors_near/pallas_call | solution.py:491
  34.9 5.6 %factors_mid.1 = (bf16[8,2,512,512]{3,2,1,0:T(8,128)(2,1)S(1)}, bf16[8,2,512,512]{3,2,1,0:T(8,128)(2,1)S(1)}, bf16[8,512,512]{2,1,0:T(8,128)(2,1)S(1)}, bf16[8,5...) custom-call(s32[1,3]{1,0:T(1,128)S(1)} %get-tuple-element.101.offset, ...), custom_call_target="tpu_custom_call", output_to_operand_aliasing={{0}: (7, {}), {1}: (8, {}), {2}: (9, {}), {3}: (10, {}), {4... | custom-call | flops 6000000000 | tf_op jit(solution)/shard_map/factors_mid/pallas_call | solution.py:491
  40.5 2.5 %factors_far.1 = (bf16[8,2,512,512]{3,2,1,0:T(8,128)(2,1)S(1)}, bf16[8,2,512,512]{3,2,1,0:T(8,128)(2,1)S(1)}, bf16[8,512,512]{2,1,0:T(8,128)(2,1)S(1)}, bf16[8,5...) custom-call(s32[1,3]{1,0:T(1,128)S(1)} %get-tuple-element.101.offset, ...), custom_call_target="tpu_custom_call", output_to_operand_aliasing={{0}: (5, {}), {1}: (6, {}), {2}: (7, {}), {3}: (8, {}), {4}... | custom-call | flops 3000000000 | tf_op jit(solution)/shard_map/factors_far/pallas_call | solution.py:491
  43.0 4.3 %forward_r.1 = (f32[8,4,512]{2,1,0:T(4,128)S(1)}, f32[2,4,512]{2,1,0:T(4,128)S(1)}, bf16[8,2,512,512]{3,2,1,0:T(8,128)(2,1)S(1)}, bf16[8,2,512,512]{3,2,1,0:T(8,...) custom-call(f32[8,4,512]{2,1,0:T(4,128)S(1)} %all-to-all-done.refs_0, ...), custom_call_target="tpu_custom_call", output_to_operand_aliasing={{2}: (1, {}), {3}: (2, {}), {4}: (3, {}), {5}: (4, {}), {6}... | custom-call | flops 4000000000 | tf_op jit(solution)/shard_map/forward_r/pallas_call | solution.py:491
  47.3 4.2 %backward_r.1 = (f32[8,4,512]{2,1,0:T(4,128)S(1)}, f32[8,4,512]{2,1,0:T(4,128)S(1)}, f32[8,3,4,512]{3,2,1,0:T(4,128)S(1)}, f32[3,4,512]{2,1,0:T(4,128)S(1)}, bf1...) custom-call(f32[8,4,512]{2,1,0:T(4,128)S(1)} %get-tuple-element.128., ...), custom_call_target="tpu_custom_call", output_to_operand_aliasing={{4}: (2, {}), {5}: (3, {}), {6}: (4, {}), {7}: (5, {}), {8}... | custom-call | flops 4000000000 | tf_op jit(solution)/shard_map/backward_r/pallas_call | solution.py:491
  51.4 2.6 %collective-permute-start.17 = (f32[3,4,512]{2,1,0:T(4,128)S(1)}, f32[3,4,512]{2,1,0:T(4,128)S(1)}, u32[]{:S(2)}, u32[]{:S(2)}) collective-permute-start(f32[3,4,512]{2,1,0:T(4,128)S(1)} %get-tuple-element.137), channel_id=1, source_target_pairs={{0,16},{16,0},{1,17},{17,1},{2,18},{18,2},{3,19},{19,3},{4,20},{20... | collective-permute-start | bytes 73736 | tf_op jit(solution)/shard_map/ppermute | solution.py:423
  54.1 2.3 %residue_of_z.1 = (f32[8,4,512]{2,1,0:T(4,128)S(1)}, f32[8,4,512]{2,1,0:T(4,128)S(1)}, bf16[8,2,512,512]{3,2,1,0:T(8,128)(2,1)S(1)}, bf16[8,2,512,512]{3,2,1,0:T...) custom-call(f32[8,4,512]{2,1,0:T(4,128)S(1)} %all-to-all-done.refs_0, ...), custom_call_target="tpu_custom_call", output_to_operand_aliasing={{2}: (4, {}), {3}: (5, {}), {4}: (6, {}), {5}: (7, {}), {6}... | custom-call | flops 2000000000 | tf_op jit(solution)/shard_map/residue_of_z/pallas_call | solution.py:491
  56.4 4.1 %forward_v.1 = (f32[8,4,512]{2,1,0:T(4,128)S(1)}, f32[4,512]{1,0:T(4,128)S(1)}, bf16[8,2,512,512]{3,2,1,0:T(8,128)(2,1)S(1)}, bf16[8,2,512,512]{3,2,1,0:T(8,128)...) custom-call(f32[8,4,512]{2,1,0:T(4,128)S(1)} %get-tuple-element.146., ...), custom_call_target="tpu_custom_call", output_to_operand_aliasing={{2}: (4, {}), {3}: (5, {}), {4}: (6, {}), {5}: (7, {}), {6}... | custom-call | flops 4000000000 | tf_op jit(solution)/shard_map/forward_v/pallas_call | solution.py:491
  60.5 4.3 %collective-permute-start.18 = (f32[4,512]{1,0:T(4,128)S(1)}, f32[4,512]{1,0:T(4,128)S(1)}, u32[]{:S(2)}, u32[]{:S(2)}) collective-permute-start(f32[4,512]{1,0:T(4,128)S(1)} %get-tuple-element.155.refs_1_), channel_id=1, source_target_pairs={{0,16},{1,17},{2,18},{3,19},{4,20},{5,21},{6,22},{7,23},{8,24},{9,... | collective-permute-start | bytes 24584 | tf_op jit(solution)/shard_map/ppermute | solution.py:557
  64.8 4.1 %backward_v.1 = (f32[8,3,4,512]{3,2,1,0:T(4,128)S(1)}, bf16[8,2,512,512]{3,2,1,0:T(8,128)(2,1)S(1)}, bf16[8,2,512,512]{3,2,1,0:T(8,128)(2,1)S(1)}, bf16[8,512,51...) custom-call(f32[8,4,512]{2,1,0:T(4,128)S(1)} %get-tuple-element.154., ...), custom_call_target="tpu_custom_call", output_to_operand_aliasing={{1}: (2, {}), {2}: (3, {}), {3}: (4, {}), {4}: (5, {}), {5}... | custom-call | flops 4000000000 | tf_op jit(solution)/shard_map/backward_v/pallas_call | solution.py:491
  69.9 5.1 %all-to-all-start.1 = ((f32[8,2,3,4,512]{4,3,2,1,0:T(4,128)}), f32[8,2,3,4,512]{4,3,2,1,0:T(4,128)S(1)}, u32[]{:S(2)}, u32[]{:S(2)}) async-start(f32[8,2,3,4,512]{4,3,2,1,0:T(4,128)} %copy.54), calls=%async_computation.1 | async-start | bytes 786432 | tf_op jit(solution)/shard_map/all_to_all | solution.py:560
  75.0 4.4 %all-to-all-done.1 = f32[8,2,3,4,512]{4,3,2,1,0:T(4,128)S(1)} async-done(((f32[8,2,3,4,512]{4,3,2,1,0:T(4,128)}), f32[8,2,3,4,512]{4,3,2,1,0:T(4,128)S(1)}, u32[]{:S(2)}, u32[]{:S(2)}) %all-to-all-start.1) | async-done | bytes 393248 | tf_op jit(solution)/shard_map/all_to_all | solution.py:560
  79.6 2.6 %row_band.1 = (bf16[1536,512]{1,0:T(8,128)(2,1)S(1)}, bf16[1536,512]{1,0:T(8,128)(2,1)S(1)}) custom-call(s32[8,7]{1,0:T(8,128)S(1)} %copy-done.5, f32[8,7,64,64]{3,2,1,0:T(8,128)S(1)} %copy-done.2), custom_call_target="tpu_custom_call" | custom-call | flops 3000000000 | tf_op jit(solution)/shard_map/row_band/pallas_call | solution.py:473
  88.9 2.4 %collective-permute-done.22 = f32[2,64,64]{2,1,0:T(8,128)S(1)} collective-permute-done((f32[2,64,64]{2,1,0:T(8,128)S(1)}, f32[2,64,64]{2,1,0:T(8,128)S(1)}, u32[]{:S(2)}, u32[]{:S(2)}) %collective-permute-start.22) | collective-permute-done | bytes 32800 | tf_op jit(solution)/shard_map/ppermute | solution.py:402
  92.6 2.2 %collective-permute-start.25 = (f32[2,64,64]{2,1,0:T(8,128)S(1)}, f32[2,64,64]{2,1,0:T(8,128)S(1)}, u32[]{:S(2)}, u32[]{:S(2)}) collective-permute-start(f32[2,64,64]{2,1,0:T(8,128)S(1)} %add_add_fusion.3), channel_id=1, source_target_pairs={{0,24},{2,26},{4,28},{6,30},{8,16},{10,18},{12,20},{14,22},{16,8},... | collective-permute-start | bytes 98312 | tf_op jit(solution)/shard_map/ppermute | solution.py:402
  94.8 4.6 %collective-permute-done.27.arrived = f32[64,512]{1,0:T(8,128)S(1)} collective-permute-done((f32[64,512]{1,0:T(8,128)S(1)}, f32[64,512]{1,0:T(8,128)S(1)}, u32[]{:S(2)}, u32[]{:S(2)}) %collective-permute-start.27) | collective-permute-done | bytes 131104 | tf_op jit(solution)/shard_map/ppermute | solution.py:573
  100.8 3.4 %collective-permute-start.30 = (f32[2,64,64]{2,1,0:T(8,128)S(1)}, f32[2,64,64]{2,1,0:T(8,128)S(1)}, u32[]{:S(2)}, u32[]{:S(2)}) collective-permute-start(f32[2,64,64]{2,1,0:T(8,128)S(1)} %get-tuple-element.168), channel_id=1, source_target_pairs={{0,6},{2,4},{4,2},{6,0},{8,14},{10,12},{12,10},{14,8},{16,22},{18,... | collective-permute-start | bytes 98312 | tf_op jit(solution)/shard_map/ppermute | solution.py:402
  106.6 3.4 %collective-permute-start.33 = (f32[2,64,64]{2,1,0:T(8,128)S(1)}, f32[2,64,64]{2,1,0:T(8,128)S(1)}, u32[]{:S(2)}, u32[]{:S(2)}) collective-permute-start(f32[2,64,64]{2,1,0:T(8,128)S(1)} %add_add_fusion.1), channel_id=1, source_target_pairs={{0,24},{2,26},{4,28},{6,30},{8,16},{10,18},{12,20},{14,22},{16,8},... | collective-permute-start | bytes 98312 | tf_op jit(solution)/shard_map/ppermute | solution.py:402
  110.0 5.4 %invert.1.inverted = f32[64,64]{1,0:T(8,128)S(1)} custom-call(f32[2,64,64]{2,1,0:T(8,128)S(1)} %add_add_fusion.2.sums.early), custom_call_target="tpu_custom_call" | custom-call | flops 1000000000 | tf_op jit(solution)/shard_map/invert/pallas_call | solution.py:575
  116.9 7.3 %collective-permute-done.34.arrived = f32[64,512]{1,0:T(8,128)S(1)} collective-permute-done((f32[64,512]{1,0:T(8,128)S(1)}, f32[64,512]{1,0:T(8,128)S(1)}, u32[]{:S(2)}, u32[]{:S(2)}) %collective-permute-start.34) | collective-permute-done | bytes 131104 | tf_op jit(solution)/shard_map/ppermute | solution.py:588
  124.5 7.5 %update.1 = (f32[32,512]{1,0:T(8,128)}, f32[32,512]{1,0:T(8,128)}) custom-call(f32[2,64,64]{2,1,0:T(8,128)S(1)} %add_add_fusion.2.sums.early, f32[2,64,64]{2,1,0:T(8,128)S(1)} %add_add_fusion.late, f32[64,64]{1,0:T(8,128)S(1)} %invert.1.inverted, f32[64,512]{1,0:T(8,128)S(1)} %get-tuple-element.169.r, f32[64,512]{1,0:T(8,128)S(1)} %get-tuple-element.167.d, ...), custom_call_target="tpu_custom_call" | custom-call | flops 1000000000 | tf_op jit(solution)/shard_map/update/pallas_call | solution.py:590
  (99 shorter events, 30.1 us)
Async XLA Ops:
  5.6 9.0 %collective-permute-start.2 = (f32[4,136,128]{2,1,0:T(8,128)S(1)}, f32[4,136,128]{2,1,0:T(8,128)S(1)}, u32[]{:S(2)}, u32[]{:S(2)}) collective-permute-start(f32[4,136,128]{2,1,0:T(8,128)S(1)} %get-tuple-element.102), channel_id=1, source_target_pairs={{0,8},{2,10},{4,12},{6,14},{8,0},{10,2},{12,4},{14,6},{1,9},{3,11}... | collective-permute-start | bytes 835592 | tf_op jit(solution)/shard_map/ppermute | solution.py:402
  6.1 8.5 %collective-permute-start.8 = (f32[4,136,128]{2,1,0:T(8,128)S(1)}, f32[4,136,128]{2,1,0:T(8,128)S(1)}, u32[]{:S(2)}, u32[]{:S(2)}) collective-permute-start(f32[4,136,128]{2,1,0:T(8,128)S(1)} %get-tuple-element.102), channel_id=1, source_target_pairs={{0,4},{2,6},{4,0},{6,2},{8,12},{10,14},{12,8},{14,10},{1,5},{3,7},... | collective-permute-start | bytes 835592 | tf_op jit(solution)/shard_map/ppermute | solution.py:402
  6.6 10.7 %collective-permute-start.1 = (f32[4,136,128]{2,1,0:T(8,128)S(1)}, f32[4,136,128]{2,1,0:T(8,128)S(1)}, u32[]{:S(2)}, u32[]{:S(2)}) collective-permute-start(f32[4,136,128]{2,1,0:T(8,128)S(1)} %get-tuple-element.102), channel_id=1, source_target_pairs={{0,2},{2,0},{4,6},{6,4},{8,10},{10,8},{12,14},{14,12},{1,3},{3,1},... | collective-permute-start | bytes 835592 | tf_op jit(solution)/shard_map/ppermute | solution.py:402
  7.4 9.9 %all-to-all-start = ((f32[8,4,512]{2,1,0:T(4,128)}), f32[8,4,512]{2,1,0:T(4,128)S(1)}, u32[]{:S(2)}, u32[]{:S(2)}) async-start(f32[8,4,512]{2,1,0:T(4,128)} %reshape.84), calls=%async_computation | async-start | bytes 131072 | tf_op jit(solution)/shard_map/all_to_all | solution.py:468
  14.6 7.3 %collective-permute-start.9 = (f32[4,128,128]{2,1,0:T(8,128)S(1)}, f32[4,128,128]{2,1,0:T(8,128)S(1)}, u32[]{:S(2)}, u32[]{:S(2)}) collective-permute-start(f32[4,128,128]{2,1,0:T(8,128)S(1)} %pad_maximum_fusion.3), channel_id=1, source_target_pairs={{0,2},{2,0},{4,6},{6,4},{8,10},{10,8},{12,14},{14,12},{1,3},{3,1},... | collective-permute-start | bytes 786440 | tf_op jit(solution)/shard_map/ppermute | solution.py:402
  17.4 8.2 %collective-permute-start.3 = (f32[4,136,128]{2,1,0:T(8,128)S(1)}, f32[4,136,128]{2,1,0:T(8,128)S(1)}, u32[]{:S(2)}, u32[]{:S(2)}) collective-permute-start(f32[4,136,128]{2,1,0:T(8,128)S(1)} %pad_maximum_fusion.2), channel_id=1, source_target_pairs={{0,4},{2,6},{4,0},{6,2},{8,12},{10,14},{12,8},{14,10},{1,5},{3,7},... | collective-permute-start | bytes 835592 | tf_op jit(solution)/shard_map/ppermute | solution.py:402
  18.8 9.4 %collective-permute-start.12 = (f32[4,144,128]{2,1,0:T(8,128)S(1)}, f32[4,144,128]{2,1,0:T(8,128)S(1)}, u32[]{:S(2)}, u32[]{:S(2)}) collective-permute-start(f32[4,144,128]{2,1,0:T(8,128)S(1)} %pad_maximum_fusion.1), channel_id=1, source_target_pairs={{0,8},{2,10},{4,12},{6,14},{8,0},{10,2},{12,4},{14,6},{1,9},{3,11}... | collective-permute-start | bytes 884744 | tf_op jit(solution)/shard_map/ppermute | solution.py:402
  20.2 7.2 %collective-permute-start.14 = (f32[4,136,128]{2,1,0:T(8,128)S(1)}, f32[4,136,128]{2,1,0:T(8,128)S(1)}, u32[]{:S(2)}, u32[]{:S(2)}) collective-permute-start(f32[4,136,128]{2,1,0:T(8,128)S(1)} %collective-permute-done.1.refs_1_), channel_id=1, source_target_pairs={{0,1},{1,0},{2,3},{3,2},{4,5},{5,4},{6,7},{7,6},{8,9},{9,8},{10,11... | collective-permute-start | bytes 835592 | tf_op jit(solution)/shard_map/ppermute | solution.py:402
  25.6 9.3 %collective-permute-start.10 = (f32[4,128,128]{2,1,0:T(8,128)S(1)}, f32[4,128,128]{2,1,0:T(8,128)S(1)}, u32[]{:S(2)}, u32[]{:S(2)}) collective-permute-start(f32[4,128,128]{2,1,0:T(8,128)S(1)} %collective-permute-done.9.refs_1_), channel_id=1, source_target_pairs={{0,1},{1,0},{2,3},{3,2},{4,5},{5,4},{6,7},{7,6},{8,9},{9,8},{10,11... | collective-permute-start | bytes 786440 | tf_op jit(solution)/shard_map/ppermute | solution.py:402
  26.2 8.2 %collective-permute-start.6 = (f32[4,72,128]{2,1,0:T(8,128)S(1)}, f32[4,72,128]{2,1,0:T(8,128)S(1)}, u32[]{:S(2)}, u32[]{:S(2)}) collective-permute-start(f32[4,72,128]{2,1,0:T(8,128)S(1)} %slice.95), channel_id=1, source_target_pairs={{0,8},{2,10},{4,12},{6,14},{8,0},{10,2},{12,4},{14,6},{1,9},{3,11}... | collective-permute-start | bytes 442376 | tf_op jit(solution)/shard_map/ppermute | solution.py:402
  27.4 6.8 %collective-permute-start.4 = (f32[4,64,128]{2,1,0:T(8,128)S(1)}, f32[4,64,128]{2,1,0:T(8,128)S(1)}, u32[]{:S(2)}, u32[]{:S(2)}) collective-permute-start(f32[4,64,128]{2,1,0:T(8,128)S(1)} %slice.94), channel_id=1, source_target_pairs={{0,2},{2,0},{4,6},{6,4},{8,10},{10,8},{12,14},{14,12},{1,3},{3,1},... | collective-permute-start | bytes 393224 | tf_op jit(solution)/shard_map/ppermute | solution.py:402
  28.2 6.7 %collective-permute-start.11 = (f32[4,136,128]{2,1,0:T(8,128)S(1)}, f32[4,136,128]{2,1,0:T(8,128)S(1)}, u32[]{:S(2)}, u32[]{:S(2)}) collective-permute-start(f32[4,136,128]{2,1,0:T(8,128)S(1)} %collective-permute-done.3.refs_3_), channel_id=1, source_target_pairs={{0,1},{1,0},{2,3},{3,2},{4,5},{5,4},{6,7},{7,6},{8,9},{9,8},{10,11... | collective-permute-start | bytes 835592 | tf_op jit(solution)/shard_map/ppermute | solution.py:402
  60.5 8.5 %collective-permute-start.18 = (f32[4,512]{1,0:T(4,128)S(1)}, f32[4,512]{1,0:T(4,128)S(1)}, u32[]{:S(2)}, u32[]{:S(2)}) collective-permute-start(f32[4,512]{1,0:T(4,128)S(1)} %get-tuple-element.155.refs_1_), channel_id=1, source_target_pairs={{0,16},{1,17},{2,18},{3,19},{4,20},{5,21},{6,22},{7,23},{8,24},{9,... | collective-permute-start | bytes 24584 | tf_op jit(solution)/shard_map/ppermute | solution.py:557
  69.9 9.5 %all-to-all-start.1 = ((f32[8,2,3,4,512]{4,3,2,1,0:T(4,128)}), f32[8,2,3,4,512]{4,3,2,1,0:T(4,128)S(1)}, u32[]{:S(2)}, u32[]{:S(2)}) async-start(f32[8,2,3,4,512]{4,3,2,1,0:T(4,128)} %copy.54), calls=%async_computation.1 | async-start | bytes 786432 | tf_op jit(solution)/shard_map/all_to_all | solution.py:560
  75.0 7.1 %collective-permute-start = (f32[32,512]{1,0:T(8,128)S(1)}, f32[32,512]{1,0:T(8,128)S(1)}, u32[]{:S(2)}, u32[]{:S(2)}) collective-permute-start(f32[32,512]{1,0:T(8,128)S(1)} %copy-done), channel_id=1, source_target_pairs={{0,1},{1,0},{2,3},{3,2},{4,5},{5,4},{6,7},{7,6},{8,9},{9,8},{10,11... | collective-permute-start | bytes 196616 | tf_op jit(solution)/shard_map/ppermute | solution.py:402
  86.6 13.1 %collective-permute-start.26 = (f32[8,3,4,512]{3,2,1,0:T(4,128)S(1)}, f32[8,3,4,512]{3,2,1,0:T(4,128)S(1)}, u32[]{:S(2)}, u32[]{:S(2)}) collective-permute-start(f32[8,3,4,512]{3,2,1,0:T(4,128)S(1)} %get-tuple-element.172.refs_0_), channel_id=1, source_target_pairs={{0,1},{1,0},{2,3},{3,2},{4,5},{5,4},{6,7},{7,6},{8,9},{9,8},{10,11... | collective-permute-start | bytes 589832 | tf_op jit(solution)/shard_map/ppermute | solution.py:402
  86.6 12.8 %collective-permute-start.27 = (f32[64,512]{1,0:T(8,128)S(1)}, f32[64,512]{1,0:T(8,128)S(1)}, u32[]{:S(2)}, u32[]{:S(2)}) collective-permute-start(f32[64,512]{1,0:T(8,128)S(1)} %get-tuple-element.167.d), channel_id=1, source_target_pairs={{16,14},{17,15}} | collective-permute-start | bytes 393224 | tf_op jit(solution)/shard_map/ppermute | solution.py:573
  91.3 9.6 %collective-permute-start.23 = (f32[2,64,64]{2,1,0:T(8,128)S(1)}, f32[2,64,64]{2,1,0:T(8,128)S(1)}, u32[]{:S(2)}, u32[]{:S(2)}) collective-permute-start(f32[2,64,64]{2,1,0:T(8,128)S(1)} %add_add_fusion.3), channel_id=1, source_target_pairs={{0,8},{2,10},{4,12},{6,14},{8,0},{10,2},{12,4},{14,6},{16,24},{18,... | collective-permute-start | bytes 98312 | tf_op jit(solution)/shard_map/ppermute | solution.py:402
  92.3 11.9 %collective-permute-start.24 = (f32[2,64,64]{2,1,0:T(8,128)S(1)}, f32[2,64,64]{2,1,0:T(8,128)S(1)}, u32[]{:S(2)}, u32[]{:S(2)}) collective-permute-start(f32[2,64,64]{2,1,0:T(8,128)S(1)} %add_add_fusion.3), channel_id=1, source_target_pairs={{0,16},{2,18},{4,20},{6,22},{8,24},{10,26},{12,28},{14,30},{16,0},... | collective-permute-start | bytes 98312 | tf_op jit(solution)/shard_map/ppermute | solution.py:402
  92.6 11.6 %collective-permute-start.25 = (f32[2,64,64]{2,1,0:T(8,128)S(1)}, f32[2,64,64]{2,1,0:T(8,128)S(1)}, u32[]{:S(2)}, u32[]{:S(2)}) collective-permute-start(f32[2,64,64]{2,1,0:T(8,128)S(1)} %add_add_fusion.3), channel_id=1, source_target_pairs={{0,24},{2,26},{4,28},{6,30},{8,16},{10,18},{12,20},{14,22},{16,8},... | collective-permute-start | bytes 98312 | tf_op jit(solution)/shard_map/ppermute | solution.py:402
  106.5 10.3 %collective-permute-start.31 = (f32[2,64,64]{2,1,0:T(8,128)S(1)}, f32[2,64,64]{2,1,0:T(8,128)S(1)}, u32[]{:S(2)}, u32[]{:S(2)}) collective-permute-start(f32[2,64,64]{2,1,0:T(8,128)S(1)} %add_add_fusion.1), channel_id=1, source_target_pairs={{0,8},{2,10},{4,12},{6,14},{8,0},{10,2},{12,4},{14,6},{16,24},{18,... | collective-permute-start | bytes 98312 | tf_op jit(solution)/shard_map/ppermute | solution.py:402
  106.6 10.3 %collective-permute-start.32 = (f32[2,64,64]{2,1,0:T(8,128)S(1)}, f32[2,64,64]{2,1,0:T(8,128)S(1)}, u32[]{:S(2)}, u32[]{:S(2)}) collective-permute-start(f32[2,64,64]{2,1,0:T(8,128)S(1)} %add_add_fusion.1), channel_id=1, source_target_pairs={{0,16},{2,18},{4,20},{6,22},{8,24},{10,26},{12,28},{14,30},{16,0},... | collective-permute-start | bytes 98312 | tf_op jit(solution)/shard_map/ppermute | solution.py:402
  106.6 10.2 %collective-permute-start.33 = (f32[2,64,64]{2,1,0:T(8,128)S(1)}, f32[2,64,64]{2,1,0:T(8,128)S(1)}, u32[]{:S(2)}, u32[]{:S(2)}) collective-permute-start(f32[2,64,64]{2,1,0:T(8,128)S(1)} %add_add_fusion.1), channel_id=1, source_target_pairs={{0,24},{2,26},{4,28},{6,30},{8,16},{10,18},{12,20},{14,22},{16,8},... | collective-permute-start | bytes 98312 | tf_op jit(solution)/shard_map/ppermute | solution.py:402
  115.5 8.7 %collective-permute-start.34 = (f32[64,512]{1,0:T(8,128)S(1)}, f32[64,512]{1,0:T(8,128)S(1)}, u32[]{:S(2)}, u32[]{:S(2)}) collective-permute-start(f32[64,512]{1,0:T(8,128)S(1)} %get-tuple-element.170.e), channel_id=1, source_target_pairs={{16,14},{17,15}} | collective-permute-start | bytes 393224 | tf_op jit(solution)/shard_map/ppermute | solution.py:588
  (19 other events, 103.1 us)

commit v3 on v2

--- a/solution.py
+++ b/solution.py
@@ -85,19 +85,26 @@
         part[r] = own[lax.axis_index("rhs") * rows_part + r]
 
 
-def band_kernel(columns, tiles, band_high, band_low, band):
+def band_kernel(first_row, columns, tiles, band_high, band_low, band):
     shard_rows, slots, order, _ = tiles.shape
     start = (lax.axis_index("blk") * SPAN + lax.axis_index("pos")) * shard_rows
     band[...] = jnp.zeros_like(band)
-    for row in range(shard_rows):
+    for row in range(shard_rows // 2):
         for slot in range(slots):
-            away = columns[row, slot] - start + shard_rows
+            away = columns[first_row + row, slot] - start + shard_rows
             where = pl.ds(pl.multiple_of(away * order, order), order)
             lanes = pl.ds(row * order, order)
-            band[where, lanes] = band[where, lanes] + tiles[row, slot].T
+            band[where, lanes] = band[where, lanes] + tiles[first_row + row, slot].T
     high, low = halves(band[...])
     band_high[...] = high
     band_low[...] = low
+
+
+def along(x, bands, first, last):
+    return jnp.concatenate(
+        [product(x, high[first:last], low[first:last], NN) for high, low in zip(bands[::2], bands[1::2])],
+        axis=1,
+    )
 
 
 def stage_rows(stage, t, pieces):
@@ -110,28 +117,19 @@
             top += rows
 
 
-def factors(offsets, stages, groups, m_high, m_low, w_high, w_low, g_high, g_low):
+def factors(offsets, stages, split, groups, m_high, m_low, w_high, w_low, g_high, g_low):
     order = 64
-    cells = 8 * order
     o = [offsets[0, k] for k in range(3)]
     at = [lax.broadcasted_iota(jnp.int32, (order, order), d) for d in range(2)]
     lane = lax.broadcasted_iota(jnp.int32, (order, 2 * order), 1)
-    pivots = {}
+    pivots, lefts = {}, {}
     for n, (stage, s) in enumerate(zip(stages, groups)):
         for i in range(8):
-            for k in range(3):
-                from_row = (i - o[k]) & 7
-                kind = jnp.where(o[k] > i, 0, 1)
-                tile = stage[
-                    from_row,
-                    k // 2 * order : (k // 2 + 1) * order,
-                    k % 2 * order : (k % 2 + 1) * order,
-                ]
-                high, low = halves(tile)
-                where = pl.ds(pl.multiple_of(from_row * order, order), order)
-                lanes = slice(i * order, (i + 1) * order)
-                m_high[s, kind, where, lanes] = high
-                m_low[s, kind, where, lanes] = low
+            for p in range(2):
+                pair = stage[i, p * order : (p + 1) * order]
+                turned = jnp.concatenate([pair[:, order:], pair[:, :order]], axis=1)
+                for version, tiles in enumerate((pair, turned)):
+                    split[n, 0, i, version, p], split[n, 1, i, version, p] = halves(tiles)
             both = stage[i, order : 2 * order, order:]
             turned = both.T
             pivots[n, i] = jnp.where(at[0] <= at[1], both, turned)
@@ -141,40 +139,45 @@
             where = slice(i % 2 * order, (i % 2 + 1) * order)
             g_high[s, i // 2, where, where] = high
             g_low[s, i // 2, where, where] = low
-    lefts = {}
-    for n, stage in enumerate(stages):
         for j in range(7):
             inside = [jnp.where(o[k] + j <= 7, 1.0, 0.0) for k in range(2)]
             pair = stage[j, :order] * jnp.where(lane < order, inside[0], inside[1])
             left = two_parts(product(pivots[n, j], *halves(pair), NN))
             lefts[n, j] = jnp.concatenate([left, left], axis=1)
+        for i in range(8):
+            lanes = slice(i * order, (i + 1) * order)
+            side = slice(i % 2 * order, (i % 2 + 1) * order)
+            for k in range(3):
+                from_row = (i - o[k]) & 7 if k < 2 else i
+                kind = jnp.where(o[k] > i, 0, 1) if k < 2 else 0
+                where = pl.ds(pl.multiple_of(from_row * order, order), order)
+                for part, m in enumerate((m_high, m_low)):
+                    m[s, kind, where, lanes] = split[n, part, from_row, (i + k) % 2, k // 2, :, side]
     for j in range(7, -1, -1):
+        first = j // 2 * 128
         for n, s in enumerate(groups):
-            row = jnp.pad(pivots[n, j], ((0, 0), (j * order, cells - (j + 1) * order)))
+            after = 8 * order - first - (j % 2 + 1) * order
+            row = jnp.pad(pivots[n, j], ((0, 0), (j % 2 * order, after)))
             if j < 7:
                 where = [
                     pl.ds(pl.multiple_of(jnp.minimum(o[k] + j, 7) * order, order), order)
                     for k in range(2)
                 ]
-                first = (j + 1) // 4 * 256
                 right = jnp.concatenate(
                     [w[s, where[k], first:] for w in (w_high, w_low) for k in range(2)], axis=0
                 )
                 both = lax.dot_general(lefts[n, j], right, NN, preferred_element_type=F32)
-                away = both[:order] + both[order:]
-                if first:
-                    away = jnp.pad(away, ((0, 0), (first, 0)))
-                row = row - away
+                row = row - (both[:order] + both[order:])
             high, low = halves(row)
-            w_high[s, j * order : (j + 1) * order] = high
-            w_low[s, j * order : (j + 1) * order] = low
-
-
-def own_factor_kernel(offsets, own, m_high, m_low, w_high, w_low, g_high, g_low):
-    for ref in (m_high, m_low, g_high, g_low):
+            w_high[s, j * order : (j + 1) * order, first:] = high
+            w_low[s, j * order : (j + 1) * order, first:] = low
+
+
+def own_factor_kernel(offsets, own, m_high, m_low, w_high, w_low, g_high, g_low, split):
+    mats = (m_high, m_low, w_high, w_low, g_high, g_low)
+    for ref in mats:
         ref[...] = jnp.zeros_like(ref)
-    mats = (m_high, m_low, w_high, w_low, g_high, g_low)
-    factors(offsets, [own], [lax.axis_index("pos")], *mats)
+    factors(offsets, [own], split, [lax.axis_index("pos")], *mats)
 
 
 def factor_kernel(layout, count, ins, mats, outs, scratch):
@@ -186,7 +189,7 @@
             stage_rows(stage, t, [(given[i * count + t], first, rows) for i, first, rows in pieces])
         staged.append(stage)
         groups.append(lax.axis_index("pos") ^ mask)
-    factors(offsets, staged, groups, *mats)
+    factors(offsets, staged, scratch[1], groups, *mats)
 
 
 def upper(x, high, low):
@@ -250,14 +253,14 @@
     top[1] = lower(z, m[0][7, 0], m[1][7, 0])
 
 
-def spread(out, values):
-    zero = jnp.zeros_like(values[0])
+def spread(out, kind, values, below, above):
+    values = [below, *values, above]
     for s in range(8):
         for side in range(3):
-            out[s, side] = values[s + side - 1] if 0 <= s + side - 1 < 8 else zero
-
-
-def second_kernel(mats, t, top, z, above, out, ends):
+            out[s, kind, side] = values[s + side]
+
+
+def second_kernel(mats, t, top, z, above, ends):
     m, w = mats[:2], mats[2:4]
     value = top[0]
     values = {7: value}
@@ -268,7 +271,6 @@
     above[7] = jnp.zeros_like(value)
     for s in range(8):
         z[s] = values[s]
-    spread(out, values)
     ends[:2] = top[...]
     ends[2] = value
 
@@ -299,15 +301,21 @@
     last[...] = upper_t(t[7], w[0][7], w[1][7])
 
 
-def fifth_kernel(mats, t, last, out):
+def fifth_kernel(mats, t, last, z, from_below, from_above, out):
     m, w = mats[:2], mats[2:4]
     value = last[...]
-    values = {7: value}
+    values = [value]
     for s in range(6, -1, -1):
         ahead = lower_t(value, m[0][s, 0], m[1][s, 0])
         value = upper_t(t[s] - ahead, w[0][s], w[1][s])
-        values[s] = value
-    spread(out, values)
+        values.insert(0, value)
+    zero = jnp.zeros_like(value)
+    spread(out, 0, [z[s] for s in range(8)], from_below[0], from_above[2])
+    spread(out, 1, values, zero, zero)
+
+
+def halo_kernel(rows, arrived, out):
+    out[0, 1, 0] = arrived[...]
 
 
 def place_rows(place, t, rhs, rows, lanes=slice(None)):
@@ -315,44 +323,37 @@
     place[pl.ds(pl.multiple_of((rhs ^ t) * count, count), count), lanes] = rows
 
 
-def image_of(pieces, wide, band_high, band_low):
-    rhs, cells = lax.axis_index("rhs"), pieces[0].shape[3]
-    for t, piece in enumerate(pieces):
-        for side in range(3):
-            rows = jnp.concatenate([piece[j, side] for j in range(SPAN)], axis=0)
-            place_rows(wide, t, rhs, rows, slice(side * cells, (side + 1) * cells))
-    below = product(wide[:, :cells], band_high[:cells], band_low[:cells], NN)
-    image = below + product(wide[:, cells:], band_high[cells:], band_low[cells:], NN)
-    twice = image + below * jnp.where(lax.axis_index("pos") == 0, 1.0, 0.0)
-    return wide[:, cells : 2 * cells], image, twice
-
-
 def inner(a, b):
     return lax.dot_general(a, b, NT, precision=HIGHEST, preferred_element_type=F32)
 
 
-def early_kernel(n, *refs):
-    r_pieces, pieces = refs[:n], refs[n : 2 * n]
-    band_high, band_low, r, d, q, sums, wide = refs[2 * n :]
+def products_kernel(n, *refs):
+    r_pieces, pieces, bands = refs[:n], refs[n : 2 * n], refs[2 * n : 2 * n + 4]
+    r, d, q, e, w, sums, wide = refs[2 * n + 4 :]
+    rhs, cells, total = lax.axis_index("rhs"), pieces[0].shape[4], r.shape[0]
     for t in range(n):
-        place_rows(r, t, lax.axis_index("rhs"), r_pieces[t][...])
-    d[...], q[...], twice = image_of(pieces, wide, band_high, band_low)
-    sums[0] = inner(d[...], r[...])
-    sums[1] = inner(d[...], twice)
-
-
-def late_kernel(n, *refs):
-    pieces = refs[:n]
-    q, band_high, band_low, e, w, sums, wide = refs[n:]
-    e[...], w[...], twice = image_of(pieces, wide, band_high, band_low)
-    sums[0] = inner(e[...], q[...])
-    sums[1] = inner(e[...], twice)
-
-
-def complete_kernel(value, arrived, band_high, band_low, out):
+        place_rows(r, t, rhs, r_pieces[t][...])
+        for kind in range(2):
+            for side in range(3):
+                rows = jnp.concatenate([pieces[t][j, kind, side] for j in range(SPAN)], axis=0)
+                lanes = slice(side * cells, (side + 1) * cells)
+                place_rows(wide.at[pl.ds(kind * total, total)], t, rhs, rows, lanes)
+    below = along(wide[:, :cells], bands, 0, cells)
+    image = below + along(wide[:, cells:], bands, cells, 3 * cells)
+    first = jnp.where(lax.axis_index("pos") == 0, 1.0, 0.0)
+    below_e = below[total:] * first
+    own = slice(cells, 2 * cells)
+    d[...], e[...] = wide[:total, own], wide[total:, own]
+    q[...], w[...] = image[:total], image[total:]
+    odd = rhs % 2 == 1
+    left = jnp.where(odd, e[...], d[...])
+    rights = jnp.where(odd, q[...], r[...]), jnp.where(odd, w[...] + below_e, q[...])
+    sums[...] = jnp.concatenate([inner(left, right) for right in rights], axis=1)
+
+
+def complete_kernel(value, arrived, *refs):
     cells = value.shape[1]
-    above = slice(2 * cells, 3 * cells)
-    out[...] = value[...] + product(arrived[...], band_high[above], band_low[above], NN)
+    refs[4][...] = value[...] + along(arrived[...], refs[:4], 2 * cells, 3 * cells)
 
 
 def small(a, b):
@@ -360,37 +361,56 @@
 
 
 def inverse(a):
-    size = a.shape[0]
-    row_at = lax.broadcasted_iota(jnp.int32, a.shape, 0)
-    col_at = lax.broadcasted_iota(jnp.int32, a.shape, 1)
-    for k in range(size):
-        scale = 1.0 / a[k : k + 1, k : k + 1]
-        row = jnp.where(col_at[:1] == k, 1.0, a[k : k + 1, :]) * scale
-        column = a[:, k : k + 1]
-        rest = jnp.where(col_at == k, 0.0, a)
-        a = jnp.where(row_at == k, row, rest - column * row)
-    return a
+    at = [lax.broadcasted_iota(jnp.int32, a.shape, d) for d in range(2)]
+    same = at[0] == at[1]
+    eye = jnp.where(same, 1.0, 0.0)
+    kept = jnp.where(same, a, 0.0)
+    by_row = lax.rsqrt(jnp.sum(kept, axis=1, keepdims=True))
+    by_column = lax.rsqrt(jnp.sum(kept, axis=0, keepdims=True))
+    a = a * by_row * by_column
+    scale = 1.0 / jnp.max(jnp.sum(jnp.abs(a), axis=0, keepdims=True), axis=1, keepdims=True)
+    rest = eye - a * scale
+    total = eye + rest
+
+    def step(total, rest):
+        rest = product(rest, *halves(rest), NN)
+        return total + product(total, *halves(rest), NN), rest
+
+    for _ in range(5):
+        total, rest = step(total, rest)
+
+    def going(carry):
+        turn, _, rest = carry
+        return (turn < 40) & (jnp.max(jnp.abs(rest)) > 1e-7)
+
+    def more(carry):
+        turn, total, rest = carry
+        return (turn + 1, *step(total, rest))
+
+    _, total, _ = lax.while_loop(going, more, (jnp.int32(0), total, rest))
+    total = total * scale
+    total = total + small(total, eye - small(a, total))
+    return total * by_row * by_column
 
 
 def symmetric(a):
     return 0.5 * (a + a.T)
 
 
-def invert_kernel(sums, inverted):
-    inverted[...] = inverse(symmetric(sums[1]))
-
-
-def last_kernel(early, late, inverted, r, d, q, e, w, solution, residual):
-    count = solution.shape[0]
+def last_kernel(own_sums, other_sums, r, d, q, e, w, solution, residual):
+    count, total = solution.shape[0], r.shape[0]
     rhs = lax.axis_index("rhs")
-    s1, s2 = symmetric(early[0]), symmetric(early[1])
-    s3, s4 = symmetric(late[0]), symmetric(late[1])
-    inv = inverted[...]
+    odd = rhs % 2 == 1
+    sums = jnp.where(odd, other_sums[...], own_sums[...]), jnp.where(odd, own_sums[...], other_sums[...])
+    s1, s2, s3, s4 = [
+        symmetric(sums[k // 2][:, k % 2 * total : (k % 2 + 1) * total]) for k in range(4)
+    ]
+    inv = inverse(s2)
     c = small(inv, s3)
     schur = symmetric(s4 - small(s3, c))
     h = small(s2 - s1 - small(s1, c), inverse(schur))
     f = small(s1 - small(h, s3), inv)
-    pick = lax.broadcasted_iota(jnp.int32, (count, s1.shape[0]), 0) + rhs * count
+    pick = lax.broadcasted_iota(jnp.int32, (count, total), 0) + rhs * count
     pick = jnp.where(pick == lax.broadcasted_iota(jnp.int32, pick.shape, 1), 1.0, 0.0)
     f, h = small(pick, f), small(pick, h)
     solution[...] = small(f, d[...]) + small(h, e[...])
@@ -456,6 +476,8 @@
         cost=2,
     )(columns, tiles, pivots)
 
+    vectors, vector = S((SPAN, each, cells), F32), S((each, cells), F32)
+    r = lax.all_to_all(right_side.reshape(SPAN, each, cells), "pos", 0, 0, tiled=True)
     x, y, z = (swapped(part, "pos", bit) for bit in (1, 2, 4))
     mat_shapes = [
         pltpu.VMEM((SPAN, 2, cells, cells), BF16),
@@ -465,21 +487,29 @@
         pltpu.VMEM((SPAN, 4, 2 * order, 2 * order), BF16),
         pltpu.VMEM((SPAN, 4, 2 * order, 2 * order), BF16),
     ]
-    r = lax.all_to_all(right_side.reshape(SPAN, each, cells), "pos", 0, 0, tiled=True)
+    splits = lambda groups: pltpu.VMEM((groups, 2, 8, 2, 2, order, 2 * order), BF16)
+    bands = []
+    for half in range(2):
+        bands += call(
+            functools.partial(band_kernel, half * shard_rows // 2),
+            "row_band",
+            [S((3 * cells, cells // 2), BF16)] * 2,
+            [SMEM, VMEM],
+            [VMEM] * 2,
+            [pltpu.VMEM((3 * cells, cells // 2), F32)],
+            cost=2,
+        )(columns, tiles)
+
     own, r = lax.optimization_barrier((own, r))
-    mats = call(own_factor_kernel, "factors_own", mat_shapes, [SMEM, VMEM], [VMEM] * 6, cost=4)(
-        offsets, own
-    )
-    band_high, band_low = call(
-        band_kernel,
-        "row_band",
-        [S((3 * cells, cells), BF16)] * 2,
+    mats = call(
+        own_factor_kernel,
+        "factors_own",
+        mat_shapes,
         [SMEM, VMEM],
-        [VMEM] * 2,
-        [pltpu.VMEM((3 * cells, cells), F32)],
-        cost=3,
-    )(columns, tiles)
-
+        [VMEM] * 6,
+        [splits(1)],
+        cost=4,
+    )(offsets, own)
     def with_mats(kernel, name, specs, out_shapes, given, scratch=(), cost=1):
         nonlocal mats
         first, outs = len(given), len(out_shapes)
@@ -509,7 +539,7 @@
             [SMEM] + [VMEM] * (len(given) - 1),
             [],
             given,
-            [pltpu.VMEM((len(layout), shard_rows, tall, 2 * order), F32)],
+            [pltpu.VMEM((len(layout), shard_rows, tall, 2 * order), F32), splits(len(layout))],
             cost,
         )
 
@@ -542,54 +572,39 @@
     add_factors("factors_far", [(7, [(0, 0, order), (1, 0, rest)])], [far_top, far_low], 3)
 
     r_pieces = others(right_side)
-    vectors, vector = S((SPAN, each, cells), F32), S((each, cells), F32)
-    ends_shape, spread_shape = S((3, each, cells), F32), S((SPAN, 3, each, cells), F32)
+    ends_shape, spread_shape = S((3, each, cells), F32), S((SPAN, 2, 3, each, cells), F32)
     t, top = sweep(first_kernel, "forward_r", [vectors, S((2, each, cells), F32)], r, cost=4)
-    z, above, spread_z, ends = sweep(
-        second_kernel, "backward_r", [vectors, vectors, spread_shape, ends_shape], t, top, cost=4
+    z, above, ends = sweep(
+        second_kernel, "backward_r", [vectors, vectors, ends_shape], t, top, cost=4
     )
     from_below, from_above = both_ways(ends)
     source, t_left = sweep(third_kernel, "residue_of_z", [vectors] * 2, r, t, z, above, cost=2)
-    spread_z = (spread_z.at[0, 0].set(from_below[0]))
     t, last = sweep(
         fourth_kernel, "forward_v", [vectors, vector], source, t_left, from_below, from_above, cost=4
     )
-    from_below = lax.ppermute(last, "blk", up)
-    (spread_e,) = sweep(fifth_kernel, "backward_v", [spread_shape], t, last, cost=4)
-    both = jnp.stack([spread_z, spread_e.at[0, 0].set(from_below)], axis=1)
-    both = lax.all_to_all(both, "pos", 0, 0, tiled=True)
-    spread_z, spread_e = both[:, 0], both[:, 1]
-
-    full, two = S((total, cells), F32), S((2, total, total), F32)
-    wide = pltpu.VMEM((total, 3 * cells), F32)
-    r_full, d_full, q_part, early = call(
-        functools.partial(early_kernel, parts),
-        "products_d",
-        [full, full, full, two],
-        [VMEM] * (2 * parts + 2),
-        [VMEM] * 4,
-        [wide],
-    )(*r_pieces, *others(spread_z), band_high, band_low)
-    d_above = lax.ppermute(d_full, ("blk", "pos"), down_rows)
-    early = summed(early)
-    inverted = call(invert_kernel, "invert", S((total, total), F32), [VMEM])(early)
-    complete = call(complete_kernel, "complete", full, [VMEM] * 4)
-    q_full = complete(q_part, d_above, band_high, band_low)
-
-    e_full, w_part, late = call(
-        functools.partial(late_kernel, parts),
-        "products_e",
-        [full, full, two],
-        [VMEM] * (parts + 3),
-        [VMEM] * 3,
-        [wide],
-    )(*others(spread_e), q_full, band_high, band_low)
-    late = summed(late)
-    e_above = lax.ppermute(e_full, ("blk", "pos"), down_rows)
-    w_full = complete(w_part, e_above, band_high, band_low)
-    return call(
-        last_kernel, "update", [S((count, cells), F32)] * 2, [VMEM] * 8, [VMEM] * 2
-    )(early, late, inverted, r_full, d_full, q_full, e_full, w_full)
+    last_below = lax.ppermute(last, "blk", up)
+    (rows,) = sweep(
+        fifth_kernel, "backward_v", [spread_shape], t, last, z, from_below, from_above, cost=4
+    )
+    rows = call(halo_kernel, "halo", spread_shape, [VMEM] * 2, aliases={0: 0})(rows, last_below)
+    rows = lax.all_to_all(rows, "pos", 0, 0, tiled=True)
+
+    full, sums_shape = S((total, cells), F32), S((total, 2 * total), F32)
+    r_full, d, q, e, w_part, sums = call(
+        functools.partial(products_kernel, parts),
+        "products",
+        [full] * 5 + [sums_shape],
+        [VMEM] * (2 * parts + 4),
+        [VMEM] * 6,
+        [pltpu.VMEM((2 * total, 3 * cells), F32)],
+        cost=2,
+    )(*r_pieces, *others(rows), *bands)
+    sums = summed(sums)
+    e_above = lax.ppermute(e, ("blk", "pos"), down_rows)
+    w = call(complete_kernel, "complete", full, [VMEM] * 6)(w_part, e_above, *bands)
+    return call(last_kernel, "update", [S((count, cells), F32)] * 2, [VMEM] * 7, [VMEM] * 2, cost=8)(
+        sums, swapped(sums, "rhs", 1), r_full, d, q, e, w
+    )
 
 
 def solution(mesh):

time: 132 us -> 116 us (0.88)
  starting transfers between devices: 44.9 us -> 31.8 us
  waiting for transfers between devices: 25 us -> 14.9 us
  blocking collectives: 0 us -> 9.44 us
  Pallas kernels: 56.1 us -> 54.2 us
    all_to_all x0 -> x1, blocking collectives: none -> 9.44 us  [shards(): rows = lax.all_to_all(rows, 'pos', 0, 0, tiled=True)]
    ppermute x31 -> x25, starting transfers between devices: 22.9 us -> 16.4 us  [swapped(): lax.ppermute(value, axis, [(i, i ^ bit) for i in range(lax.axis_size(axis...]
    ppermute x3 -> x2, waiting for transfers between devices: 11.9 us -> 5.97 us  [the longest x1 5.93 us: shards(): e_above = lax.ppermute(e, ('blk', 'pos'), down_rows)]
    all_to_all x1 -> x0, starting transfers between devices: 5.11 us -> none  [shards(): both = lax.all_to_all(both, 'pos', 0, 0, tiled=True)]
    all_to_all x1 -> x0, waiting for transfers between devices: 4.4 us -> none  [shards(): both = lax.all_to_all(both, 'pos', 0, 0, tiled=True)]
    pallas_call x7 -> x6, Pallas kernels: 18.1 us -> 14.4 us  [the longest x1 9.21 us: shards(): call(last_kernel, 'update', [S((count, cells), F32)] * 2, [VMEM] * 7, [VM...]
    ppermute x3 -> x2, starting transfers between devices: 7.15 us -> 5.61 us  [the longest x1 4.33 us: shards(): last_below = lax.ppermute(last, 'blk', up)]
    ppermute x31 -> x25, waiting for transfers between devices: 6.56 us -> 6.82 us  [swapped(): lax.ppermute(value, axis, [(i, i ^ bit) for i in range(lax.axis_size(axis...]
  transfers between devices with their start and end apart: 37 -> 29, of which waited for: 10 -> 7; matrix products, arithmetic and copies ran while one was open for 1% -> 1% of each run, Pallas kernels for 23% -> 23%
where the time goes in v3:
time: 116 us; the launch traced here: 115 us
  Pallas kernels  54.2 us (47%)
  starting transfers between devices  31.8 us (27%)
  waiting for transfers between devices  14.9 us (13%)
  blocking collectives  9.44 us (8%)
  local copies, waits for them, and re-layouts  3.85 us (3%)
    pallas_call x8, Pallas kernels, with_mats(): call(body, name, [*out_shapes, *mat_shapes], [*specs, *[VMEM] * 6], [VMEM...  33.8 us
    ppermute x25, starting transfers between devices, swapped(): lax.ppermute(value, axis, [(i, i ^ bit) for i in range(lax.axis_size(axis...  16.4 us
    all_to_all x1, blocking collectives, shards(): rows = lax.all_to_all(rows, 'pos', 0, 0, tiled=True)  9.44 us
    pallas_call x1, Pallas kernels, shards(): call(last_kernel, 'update', [S((count, cells), F32)] * 2, [VMEM] * 7, [VM...  9.21 us
    all_to_all x1, starting transfers between devices, shards(): lax.all_to_all(right_side.reshape(SPAN, each, cells), 'pos', 0, 0, tiled=...  7.13 us
    ppermute x25, waiting for transfers between devices, swapped(): lax.ppermute(value, axis, [(i, i ^ bit) for i in range(lax.axis_size(axis...  6.82 us
    ppermute x1, waiting for transfers between devices, shards(): e_above = lax.ppermute(e, ('blk', 'pos'), down_rows)  5.93 us
    ppermute x1, starting transfers between devices, shards(): last_below = lax.ppermute(last, 'blk', up)  4.33 us
  transfers between devices with their start and end apart: 29, of which 7 were waited for; matrix products, arithmetic and copies ran while one was open for 1% of the time, Pallas kernels for 23%

profile of v3, /device:TPU:14, one launch (start us, length us, event | category | flops | bytes accessed | tf_op | source)
XLA Modules:
  0.0 115.2 jit_solution(8275484127097080820)
XLA Ops:
  0.6 1.5 %copy-done.1 = f32[8,7,64,64]{3,2,1,0:T(8,128)S(1)} copy-done((f32[8,7,64,64]{3,2,1,0:T(8,128)S(1)}, f32[8,7,64,64]{3,2,1,0:T(8,128)}, u32[]{:S(2)}) %copy-start.1) | copy-done | bytes 917528
  3.8 1.8 %pack_tiles.1 = (f32[8,136,128]{2,1,0:T(8,128)S(1)}, f32[4,136,128]{2,1,0:T(8,128)S(1)}, s32[1,3]{1,0:T(1,128)S(1)}) custom-call(s32[8,7]{1,0:T(8,128)S(1)} %copy-done.4, f32[8,7,64,64]{3,2,1,0:T(8,128)S(1)} %copy-done.1, f32[8,64,64]{2,1,0:T(8,128)S(1)} %copy-done.3), custom_call_target="tpu_custom_call" | custom-call | flops 2000000000 | tf_op jit(solution)/shard_map/pack_tiles/pallas_call | solution.py:466
  7.4 7.1 %all-to-all-start = ((f32[8,4,512]{2,1,0:T(4,128)}), f32[8,4,512]{2,1,0:T(4,128)S(1)}, u32[]{:S(2)}, u32[]{:S(2)}) async-start(f32[8,4,512]{2,1,0:T(4,128)} %reshape.7), calls=%async_computation | async-start | bytes 131072 | tf_op jit(solution)/shard_map/all_to_all | solution.py:480
  15.2 2.1 %all-to-all-done.refs_0_ = f32[8,4,512]{2,1,0:T(4,128)S(1)} async-done(((f32[8,4,512]{2,1,0:T(4,128)}), f32[8,4,512]{2,1,0:T(4,128)S(1)}, u32[]{:S(2)}, u32[]{:S(2)}) %all-to-all-start) | async-done | bytes 65568 | tf_op jit(solution)/shard_map/all_to_all | solution.py:480
  21.9 4.2 %factors_own.1 = (bf16[8,2,512,512]{3,2,1,0:T(8,128)(2,1)S(1)}, bf16[8,2,512,512]{3,2,1,0:T(8,128)(2,1)S(1)}, bf16[8,512,512]{2,1,0:T(8,128)(2,1)S(1)}, bf16[8,5...) custom-call(s32[1,3]{1,0:T(1,128)S(1)} %get-tuple-element.77.offsets.refs_0_, ...), custom_call_target="tpu_custom_call" | custom-call | flops 4000000000 | tf_op jit(solution)/shard_map/factors_own/pallas_call | solution.py:504
  29.3 6.1 %factors_near.1 = (bf16[8,2,512,512]{3,2,1,0:T(8,128)(2,1)S(1)}, bf16[8,2,512,512]{3,2,1,0:T(8,128)(2,1)S(1)}, bf16[8,512,512]{2,1,0:T(8,128)(2,1)S(1)}, bf16[8,...) custom-call(s32[1,3]{1,0:T(1,128)S(1)} %get-tuple-element.77.offsets, ...), custom_call_target="tpu_custom_call", output_to_operand_aliasing={{0}: (7, {}), {1}: (8, {}), {2}: (9, {}), {3}: (10, {}), {4... | custom-call | flops 6000000000 | tf_op jit(solution)/shard_map/factors_near/pallas_call | solution.py:521
  36.0 6.2 %factors_mid.1 = (bf16[8,2,512,512]{3,2,1,0:T(8,128)(2,1)S(1)}, bf16[8,2,512,512]{3,2,1,0:T(8,128)(2,1)S(1)}, bf16[8,512,512]{2,1,0:T(8,128)(2,1)S(1)}, bf16[8,5...) custom-call(s32[1,3]{1,0:T(1,128)S(1)} %get-tuple-element.77.offsets, ...), custom_call_target="tpu_custom_call", output_to_operand_aliasing={{0}: (7, {}), {1}: (8, {}), {2}: (9, {}), {3}: (10, {}), {4... | custom-call | flops 6000000000 | tf_op jit(solution)/shard_map/factors_mid/pallas_call | solution.py:521
  42.2 2.7 %factors_far.1 = (bf16[8,2,512,512]{3,2,1,0:T(8,128)(2,1)S(1)}, bf16[8,2,512,512]{3,2,1,0:T(8,128)(2,1)S(1)}, bf16[8,512,512]{2,1,0:T(8,128)(2,1)S(1)}, bf16[8,5...) custom-call(s32[1,3]{1,0:T(1,128)S(1)} %get-tuple-element.77.offsets, ...), custom_call_target="tpu_custom_call", output_to_operand_aliasing={{0}: (5, {}), {1}: (6, {}), {2}: (7, {}), {3}: (8, {}), {4}... | custom-call | flops 3000000000 | tf_op jit(solution)/shard_map/factors_far/pallas_call | solution.py:521
  44.9 4.1 %forward_r.1 = (f32[8,4,512]{2,1,0:T(4,128)S(1)}, f32[2,4,512]{2,1,0:T(4,128)S(1)}, bf16[8,2,512,512]{3,2,1,0:T(8,128)(2,1)S(1)}, bf16[8,2,512,512]{3,2,1,0:T(8,...) custom-call(f32[8,4,512]{2,1,0:T(4,128)S(1)} %all-to-all-done.refs_0, ...), custom_call_target="tpu_custom_call", output_to_operand_aliasing={{2}: (1, {}), {3}: (2, {}), {4}: (3, {}), {5}: (4, {}), {6}... | custom-call | flops 4000000000 | tf_op jit(solution)/shard_map/forward_r/pallas_call | solution.py:521
  49.0 4.1 %backward_r.1 = (f32[8,4,512]{2,1,0:T(4,128)S(1)}, f32[8,4,512]{2,1,0:T(4,128)S(1)}, f32[3,4,512]{2,1,0:T(4,128)S(1)}, bf16[8,2,512,512]{3,2,1,0:T(8,128)(2,1)S(...) custom-call(f32[8,4,512]{2,1,0:T(4,128)S(1)} %get-tuple-element.104., ...), custom_call_target="tpu_custom_call", output_to_operand_aliasing={{3}: (2, {}), {4}: (3, {}), {5}: (4, {}), {6}: (5, {}), {7}... | custom-call | flops 4000000000 | tf_op jit(solution)/shard_map/backward_r/pallas_call | solution.py:521
  53.2 2.6 %collective-permute-start.17 = (f32[3,4,512]{2,1,0:T(4,128)S(1)}, f32[3,4,512]{2,1,0:T(4,128)S(1)}, u32[]{:S(2)}, u32[]{:S(2)}) collective-permute-start(f32[3,4,512]{2,1,0:T(4,128)S(1)} %get-tuple-element.122), channel_id=1, source_target_pairs={{0,16},{16,0},{1,17},{17,1},{2,18},{18,2},{3,19},{19,3},{4,20},{20... | collective-permute-start | bytes 73736 | tf_op jit(solution)/shard_map/ppermute | solution.py:443
  55.8 2.3 %residue_of_z.1 = (f32[8,4,512]{2,1,0:T(4,128)S(1)}, f32[8,4,512]{2,1,0:T(4,128)S(1)}, bf16[8,2,512,512]{3,2,1,0:T(8,128)(2,1)S(1)}, bf16[8,2,512,512]{3,2,1,0:T...) custom-call(f32[8,4,512]{2,1,0:T(4,128)S(1)} %all-to-all-done.refs_0, ...), custom_call_target="tpu_custom_call", output_to_operand_aliasing={{2}: (4, {}), {3}: (5, {}), {4}: (6, {}), {5}: (7, {}), {6}... | custom-call | flops 2000000000 | tf_op jit(solution)/shard_map/residue_of_z/pallas_call | solution.py:521
  58.2 4.1 %forward_v.1 = (f32[8,4,512]{2,1,0:T(4,128)S(1)}, f32[4,512]{1,0:T(4,128)S(1)}, bf16[8,2,512,512]{3,2,1,0:T(8,128)(2,1)S(1)}, bf16[8,2,512,512]{3,2,1,0:T(8,128)...) custom-call(f32[8,4,512]{2,1,0:T(4,128)S(1)} %get-tuple-element.120., ...), custom_call_target="tpu_custom_call", output_to_operand_aliasing={{2}: (4, {}), {3}: (5, {}), {4}: (6, {}), {5}: (7, {}), {6}... | custom-call | flops 4000000000 | tf_op jit(solution)/shard_map/forward_v/pallas_call | solution.py:521
  62.3 4.3 %collective-permute-start.18 = (f32[4,512]{1,0:T(4,128)S(1)}, f32[4,512]{1,0:T(4,128)S(1)}, u32[]{:S(2)}, u32[]{:S(2)}) collective-permute-start(f32[4,512]{1,0:T(4,128)S(1)} %get-tuple-element.130.refs_1_), channel_id=1, source_target_pairs={{0,16},{1,17},{2,18},{3,19},{4,20},{5,21},{6,22},{7,23},{8,24},{9,... | collective-permute-start | bytes 24584 | tf_op jit(solution)/shard_map/ppermute | solution.py:585
  66.6 4.1 %backward_v.1 = (f32[8,2,3,4,512]{4,3,2,1,0:T(4,128)S(1)}, bf16[8,2,512,512]{3,2,1,0:T(8,128)(2,1)S(1)}, bf16[8,2,512,512]{3,2,1,0:T(8,128)(2,1)S(1)}, bf16[8,51...) custom-call(f32[8,4,512]{2,1,0:T(4,128)S(1)} %get-tuple-element.129., ...), custom_call_target="tpu_custom_call", output_to_operand_aliasing={{1}: (5, {}), {2}: (6, {}), {3}: (7, {}), {4}: (8, {}), {5}... | custom-call | flops 4000000000 | tf_op jit(solution)/shard_map/backward_v/pallas_call | solution.py:521
  70.8 9.4 %all_to_all.10.refs_2_ = f32[8,2,3,4,512]{4,3,2,1,0:T(4,128)S(1)} all-to-all(f32[8,2,3,4,512]{4,3,2,1,0:T(4,128)S(1)} %halo.1), channel_id=1, replica_groups=mesh['blk'=2,'pos'=8,'rhs'=2] {'pos'}, dimensions={0} | all-to-all | bytes 786432 | tf_op jit(solution)/shard_map/all_to_all | solution.py:590
  80.7 1.7 %row_band.2 = (bf16[1536,256]{1,0:T(8,128)(2,1)S(1)}, bf16[1536,256]{1,0:T(8,128)(2,1)S(1)}) custom-call(s32[8,7]{1,0:T(8,128)S(1)} %copy-done.5, f32[8,7,64,64]{3,2,1,0:T(8,128)S(1)} %copy-done.2), custom_call_target="tpu_custom_call" | custom-call | flops 2000000000 | tf_op jit(solution)/shard_map/row_band/pallas_call | solution.py:493
  82.4 1.7 %row_band.3 = (bf16[1536,256]{1,0:T(8,128)(2,1)S(1)}, bf16[1536,256]{1,0:T(8,128)(2,1)S(1)}) custom-call(s32[8,7]{1,0:T(8,128)S(1)} %copy-done.5, f32[8,7,64,64]{3,2,1,0:T(8,128)S(1)} %copy-done.2), custom_call_target="tpu_custom_call" | custom-call | flops 2000000000 | tf_op jit(solution)/shard_map/row_band/pallas_call | solution.py:493
  85.6 1.5 %collective-permute-start.20 = (f32[64,128]{1,0:T(8,128)S(1)}, f32[64,128]{1,0:T(8,128)S(1)}, u32[]{:S(2)}, u32[]{:S(2)}) collective-permute-start(f32[64,128]{1,0:T(8,128)S(1)} %get-tuple-element.142), channel_id=1, source_target_pairs={{0,2},{2,0},{4,6},{6,4},{8,10},{10,8},{12,14},{14,12},{16,18},{18,... | collective-permute-start | bytes 98312 | tf_op jit(solution)/shard_map/ppermute | solution.py:422
  87.1 1.5 %collective-permute-start.21 = (f32[64,128]{1,0:T(8,128)S(1)}, f32[64,128]{1,0:T(8,128)S(1)}, u32[]{:S(2)}, u32[]{:S(2)}) collective-permute-start(f32[64,128]{1,0:T(8,128)S(1)} %get-tuple-element.142), channel_id=1, source_target_pairs={{0,4},{2,6},{4,0},{6,2},{8,12},{10,14},{12,8},{14,10},{16,20},{18,... | collective-permute-start | bytes 98312 | tf_op jit(solution)/shard_map/ppermute | solution.py:422
  91.1 2.4 %collective-permute-done.22 = f32[64,128]{1,0:T(8,128)S(1)} collective-permute-done((f32[64,128]{1,0:T(8,128)S(1)}, f32[64,128]{1,0:T(8,128)S(1)}, u32[]{:S(2)}, u32[]{:S(2)}) %collective-permute-start.22) | collective-permute-done | bytes 32800 | tf_op jit(solution)/shard_map/ppermute | solution.py:422
  95.0 2.0 %collective-permute-start.25 = (f32[64,128]{1,0:T(8,128)S(1)}, f32[64,128]{1,0:T(8,128)S(1)}, u32[]{:S(2)}, u32[]{:S(2)}) collective-permute-start(f32[64,128]{1,0:T(8,128)S(1)} %add_add_fusion.1), channel_id=1, source_target_pairs={{0,24},{2,26},{4,28},{6,30},{8,16},{10,18},{12,20},{14,22},{16,8},... | collective-permute-start | bytes 98312 | tf_op jit(solution)/shard_map/ppermute | solution.py:422
  99.7 5.9 %collective-permute-done.27.arrived = f32[64,512]{1,0:T(8,128)S(1)} collective-permute-done((f32[64,512]{1,0:T(8,128)S(1)}, f32[64,512]{1,0:T(8,128)S(1)}, u32[]{:S(2)}, u32[]{:S(2)}) %collective-permute-start.27) | collective-permute-done | bytes 131104 | tf_op jit(solution)/shard_map/ppermute | solution.py:603
  106.0 9.2 %update.1 = (f32[32,512]{1,0:T(8,128)}, f32[32,512]{1,0:T(8,128)}) custom-call(f32[64,128]{1,0:T(8,128)S(1)} %add_add_fusion.own_sums, f32[64,128]{1,0:T(8,128)S(1)} %collective-permute-done.26.other_sums, f32[64,512]{1,0:T(8,128)S(1)} %get-tuple-element.143.r, f32[64,512]{1,0:T(8,128)S(1)} %get-tuple-element.144.d, f32[64,512]{1,0:T(8,128)S(1)} %get-tuple-element.145.q, ...), custom_call_target="tpu_custom_call" | custom-call | flops 8000000000 | tf_op jit(solution)/shard_map/update/pallas_call | solution.py:605
  (76 shorter events, 21.4 us)
Async XLA Ops:
  5.6 9.0 %collective-permute-start.2 = (f32[4,136,128]{2,1,0:T(8,128)S(1)}, f32[4,136,128]{2,1,0:T(8,128)S(1)}, u32[]{:S(2)}, u32[]{:S(2)}) collective-permute-start(f32[4,136,128]{2,1,0:T(8,128)S(1)} %get-tuple-element.78), channel_id=1, source_target_pairs={{0,8},{2,10},{4,12},{6,14},{8,0},{10,2},{12,4},{14,6},{1,9},{3,11}... | collective-permute-start | bytes 835592 | tf_op jit(solution)/shard_map/ppermute | solution.py:422
  6.1 8.5 %collective-permute-start.8 = (f32[4,136,128]{2,1,0:T(8,128)S(1)}, f32[4,136,128]{2,1,0:T(8,128)S(1)}, u32[]{:S(2)}, u32[]{:S(2)}) collective-permute-start(f32[4,136,128]{2,1,0:T(8,128)S(1)} %get-tuple-element.78), channel_id=1, source_target_pairs={{0,4},{2,6},{4,0},{6,2},{8,12},{10,14},{12,8},{14,10},{1,5},{3,7},... | collective-permute-start | bytes 835592 | tf_op jit(solution)/shard_map/ppermute | solution.py:422
  6.6 10.7 %collective-permute-start.1 = (f32[4,136,128]{2,1,0:T(8,128)S(1)}, f32[4,136,128]{2,1,0:T(8,128)S(1)}, u32[]{:S(2)}, u32[]{:S(2)}) collective-permute-start(f32[4,136,128]{2,1,0:T(8,128)S(1)} %get-tuple-element.78), channel_id=1, source_target_pairs={{0,2},{2,0},{4,6},{6,4},{8,10},{10,8},{12,14},{14,12},{1,3},{3,1},... | collective-permute-start | bytes 835592 | tf_op jit(solution)/shard_map/ppermute | solution.py:422
  7.4 9.9 %all-to-all-start = ((f32[8,4,512]{2,1,0:T(4,128)}), f32[8,4,512]{2,1,0:T(4,128)S(1)}, u32[]{:S(2)}, u32[]{:S(2)}) async-start(f32[8,4,512]{2,1,0:T(4,128)} %reshape.7), calls=%async_computation | async-start | bytes 131072 | tf_op jit(solution)/shard_map/all_to_all | solution.py:480
  14.6 7.3 %collective-permute-start.9 = (f32[4,128,128]{2,1,0:T(8,128)S(1)}, f32[4,128,128]{2,1,0:T(8,128)S(1)}, u32[]{:S(2)}, u32[]{:S(2)}) collective-permute-start(f32[4,128,128]{2,1,0:T(8,128)S(1)} %pad_maximum_fusion.2), channel_id=1, source_target_pairs={{0,2},{2,0},{4,6},{6,4},{8,10},{10,8},{12,14},{14,12},{1,3},{3,1},... | collective-permute-start | bytes 786440 | tf_op jit(solution)/shard_map/ppermute | solution.py:422
  17.4 8.8 %collective-permute-start.3 = (f32[4,136,128]{2,1,0:T(8,128)S(1)}, f32[4,136,128]{2,1,0:T(8,128)S(1)}, u32[]{:S(2)}, u32[]{:S(2)}) collective-permute-start(f32[4,136,128]{2,1,0:T(8,128)S(1)} %pad_maximum_fusion.1), channel_id=1, source_target_pairs={{0,4},{2,6},{4,0},{6,2},{8,12},{10,14},{12,8},{14,10},{1,5},{3,7},... | collective-permute-start | bytes 835592 | tf_op jit(solution)/shard_map/ppermute | solution.py:422
  18.8 10.0 %collective-permute-start.12 = (f32[4,144,128]{2,1,0:T(8,128)S(1)}, f32[4,144,128]{2,1,0:T(8,128)S(1)}, u32[]{:S(2)}, u32[]{:S(2)}) collective-permute-start(f32[4,144,128]{2,1,0:T(8,128)S(1)} %pad_maximum_fusion), channel_id=1, source_target_pairs={{0,8},{2,10},{4,12},{6,14},{8,0},{10,2},{12,4},{14,6},{1,9},{3,11}... | collective-permute-start | bytes 884744 | tf_op jit(solution)/shard_map/ppermute | solution.py:422
  20.2 6.6 %collective-permute-start.15 = (f32[4,136,128]{2,1,0:T(8,128)S(1)}, f32[4,136,128]{2,1,0:T(8,128)S(1)}, u32[]{:S(2)}, u32[]{:S(2)}) collective-permute-start(f32[4,136,128]{2,1,0:T(8,128)S(1)} %collective-permute-done.8.refs_3_), channel_id=1, source_target_pairs={{0,1},{1,0},{2,3},{3,2},{4,5},{5,4},{6,7},{7,6},{8,9},{9,8},{10,11... | collective-permute-start | bytes 835592 | tf_op jit(solution)/shard_map/ppermute | solution.py:422
  20.2 7.8 %collective-permute-start.14 = (f32[4,136,128]{2,1,0:T(8,128)S(1)}, f32[4,136,128]{2,1,0:T(8,128)S(1)}, u32[]{:S(2)}, u32[]{:S(2)}) collective-permute-start(f32[4,136,128]{2,1,0:T(8,128)S(1)} %collective-permute-done.1.refs_1_), channel_id=1, source_target_pairs={{0,1},{1,0},{2,3},{3,2},{4,5},{5,4},{6,7},{7,6},{8,9},{9,8},{10,11... | collective-permute-start | bytes 835592 | tf_op jit(solution)/shard_map/ppermute | solution.py:422
  21.9 6.8 %collective-permute-start.16 = (f32[4,136,128]{2,1,0:T(8,128)S(1)}, f32[4,136,128]{2,1,0:T(8,128)S(1)}, u32[]{:S(2)}, u32[]{:S(2)}) collective-permute-start(f32[4,136,128]{2,1,0:T(8,128)S(1)} %collective-permute-done.2.refs_5_), channel_id=1, source_target_pairs={{0,1},{1,0},{2,3},{3,2},{4,5},{5,4},{6,7},{7,6},{8,9},{9,8},{10,11... | collective-permute-start | bytes 835592 | tf_op jit(solution)/shard_map/ppermute | solution.py:422
  26.2 9.8 %collective-permute-start.10 = (f32[4,128,128]{2,1,0:T(8,128)S(1)}, f32[4,128,128]{2,1,0:T(8,128)S(1)}, u32[]{:S(2)}, u32[]{:S(2)}) collective-permute-start(f32[4,128,128]{2,1,0:T(8,128)S(1)} %collective-permute-done.9.refs_1_), channel_id=1, source_target_pairs={{0,1},{1,0},{2,3},{3,2},{4,5},{5,4},{6,7},{7,6},{8,9},{9,8},{10,11... | collective-permute-start | bytes 786440 | tf_op jit(solution)/shard_map/ppermute | solution.py:422
  26.8 8.7 %collective-permute-start.6 = (f32[4,72,128]{2,1,0:T(8,128)S(1)}, f32[4,72,128]{2,1,0:T(8,128)S(1)}, u32[]{:S(2)}, u32[]{:S(2)}) collective-permute-start(f32[4,72,128]{2,1,0:T(8,128)S(1)} %slice.29), channel_id=1, source_target_pairs={{0,8},{2,10},{4,12},{6,14},{8,0},{10,2},{12,4},{14,6},{1,9},{3,11}... | collective-permute-start | bytes 442376 | tf_op jit(solution)/shard_map/ppermute | solution.py:422
  28.0 7.4 %collective-permute-start.4 = (f32[4,64,128]{2,1,0:T(8,128)S(1)}, f32[4,64,128]{2,1,0:T(8,128)S(1)}, u32[]{:S(2)}, u32[]{:S(2)}) collective-permute-start(f32[4,64,128]{2,1,0:T(8,128)S(1)} %slice.28), channel_id=1, source_target_pairs={{0,2},{2,0},{4,6},{6,4},{8,10},{10,8},{12,14},{14,12},{1,3},{3,1},... | collective-permute-start | bytes 393224 | tf_op jit(solution)/shard_map/ppermute | solution.py:422
  28.8 7.3 %collective-permute-start.11 = (f32[4,136,128]{2,1,0:T(8,128)S(1)}, f32[4,136,128]{2,1,0:T(8,128)S(1)}, u32[]{:S(2)}, u32[]{:S(2)}) collective-permute-start(f32[4,136,128]{2,1,0:T(8,128)S(1)} %collective-permute-done.3.refs_3_), channel_id=1, source_target_pairs={{0,1},{1,0},{2,3},{3,2},{4,5},{5,4},{6,7},{7,6},{8,9},{9,8},{10,11... | collective-permute-start | bytes 835592 | tf_op jit(solution)/shard_map/ppermute | solution.py:422
  28.8 7.3 %collective-permute-start.13 = (f32[4,144,128]{2,1,0:T(8,128)S(1)}, f32[4,144,128]{2,1,0:T(8,128)S(1)}, u32[]{:S(2)}, u32[]{:S(2)}) collective-permute-start(f32[4,144,128]{2,1,0:T(8,128)S(1)} %collective-permute-done.12.refs_5_), channel_id=1, source_target_pairs={{0,1},{1,0},{2,3},{3,2},{4,5},{5,4},{6,7},{7,6},{8,9},{9,8},{10,11... | collective-permute-start | bytes 884744 | tf_op jit(solution)/shard_map/ppermute | solution.py:422
  35.4 6.8 %collective-permute-start.5 = (f32[4,64,128]{2,1,0:T(8,128)S(1)}, f32[4,64,128]{2,1,0:T(8,128)S(1)}, u32[]{:S(2)}, u32[]{:S(2)}) collective-permute-start(f32[4,64,128]{2,1,0:T(8,128)S(1)} %collective-permute-done.4.refs_1_), channel_id=1, source_target_pairs={{0,1},{1,0},{2,3},{3,2},{4,5},{5,4},{6,7},{7,6},{8,9},{9,8},{10,11... | collective-permute-start | bytes 393224 | tf_op jit(solution)/shard_map/ppermute | solution.py:422
  35.6 6.6 %collective-permute-start.7 = (f32[4,72,128]{2,1,0:T(8,128)S(1)}, f32[4,72,128]{2,1,0:T(8,128)S(1)}, u32[]{:S(2)}, u32[]{:S(2)}) collective-permute-start(f32[4,72,128]{2,1,0:T(8,128)S(1)} %collective-permute-done.6.refs_3_), channel_id=1, source_target_pairs={{0,1},{1,0},{2,3},{3,2},{4,5},{5,4},{6,7},{7,6},{8,9},{9,8},{10,11... | collective-permute-start | bytes 442376 | tf_op jit(solution)/shard_map/ppermute | solution.py:422
  53.2 5.0 %collective-permute-start.17 = (f32[3,4,512]{2,1,0:T(4,128)S(1)}, f32[3,4,512]{2,1,0:T(4,128)S(1)}, u32[]{:S(2)}, u32[]{:S(2)}) collective-permute-start(f32[3,4,512]{2,1,0:T(4,128)S(1)} %get-tuple-element.122), channel_id=1, source_target_pairs={{0,16},{16,0},{1,17},{17,1},{2,18},{18,2},{3,19},{19,3},{4,20},{20... | collective-permute-start | bytes 73736 | tf_op jit(solution)/shard_map/ppermute | solution.py:443
  62.3 8.5 %collective-permute-start.18 = (f32[4,512]{1,0:T(4,128)S(1)}, f32[4,512]{1,0:T(4,128)S(1)}, u32[]{:S(2)}, u32[]{:S(2)}) collective-permute-start(f32[4,512]{1,0:T(4,128)S(1)} %get-tuple-element.130.refs_1_), channel_id=1, source_target_pairs={{0,16},{1,17},{2,18},{3,19},{4,20},{5,21},{6,22},{7,23},{8,24},{9,... | collective-permute-start | bytes 24584 | tf_op jit(solution)/shard_map/ppermute | solution.py:585
  88.6 4.8 %collective-permute-start.22 = (f32[64,128]{1,0:T(8,128)S(1)}, f32[64,128]{1,0:T(8,128)S(1)}, u32[]{:S(2)}, u32[]{:S(2)}) collective-permute-start(f32[64,128]{1,0:T(8,128)S(1)} %get-tuple-element.142), channel_id=1, source_target_pairs={{0,6},{2,4},{4,2},{6,0},{8,14},{10,12},{12,10},{14,8},{16,22},{18,... | collective-permute-start | bytes 98312 | tf_op jit(solution)/shard_map/ppermute | solution.py:422
  93.4 4.8 %collective-permute-start.23 = (f32[64,128]{1,0:T(8,128)S(1)}, f32[64,128]{1,0:T(8,128)S(1)}, u32[]{:S(2)}, u32[]{:S(2)}) collective-permute-start(f32[64,128]{1,0:T(8,128)S(1)} %add_add_fusion.1), channel_id=1, source_target_pairs={{0,8},{2,10},{4,12},{6,14},{8,0},{10,2},{12,4},{14,6},{16,24},{18,... | collective-permute-start | bytes 98312 | tf_op jit(solution)/shard_map/ppermute | solution.py:422
  94.8 4.8 %collective-permute-start.24 = (f32[64,128]{1,0:T(8,128)S(1)}, f32[64,128]{1,0:T(8,128)S(1)}, u32[]{:S(2)}, u32[]{:S(2)}) collective-permute-start(f32[64,128]{1,0:T(8,128)S(1)} %add_add_fusion.1), channel_id=1, source_target_pairs={{0,16},{2,18},{4,20},{6,22},{8,24},{10,26},{12,28},{14,30},{16,0},... | collective-permute-start | bytes 98312 | tf_op jit(solution)/shard_map/ppermute | solution.py:422
  97.0 8.6 %collective-permute-start.27 = (f32[64,512]{1,0:T(8,128)S(1)}, f32[64,512]{1,0:T(8,128)S(1)}, u32[]{:S(2)}, u32[]{:S(2)}) collective-permute-start(f32[64,512]{1,0:T(8,128)S(1)} %get-tuple-element.146.e), channel_id=1, source_target_pairs={{16,14},{17,15}} | collective-permute-start | bytes 393224 | tf_op jit(solution)/shard_map/ppermute | solution.py:603
  99.6 6.3 %collective-permute-start.26 = (f32[64,128]{1,0:T(8,128)S(1)}, f32[64,128]{1,0:T(8,128)S(1)}, u32[]{:S(2)}, u32[]{:S(2)}) collective-permute-start(f32[64,128]{1,0:T(8,128)S(1)} %add_add_fusion.own_sums), channel_id=1, source_target_pairs={{0,1},{1,0},{2,3},{3,2},{4,5},{5,4},{6,7},{7,6},{8,9},{9,8},{10,11... | collective-permute-start | bytes 98312 | tf_op jit(solution)/shard_map/ppermute | solution.py:422
  (11 other events, 46.5 us)

commit v4 on v3

--- a/solution.py
+++ b/solution.py
@@ -16,7 +16,7 @@
 SMEM = pl.BlockSpec(memory_space=pltpu.SMEM)
 
 
-def call(kernel, name, out_shape, in_specs, out_specs=VMEM, scratch=(), aliases=None, cost=1):
+def call(kernel, name, out_shape, in_specs, out_specs=VMEM, scratch=(), aliases=None, cost=1, limit=16):
     return pl.pallas_call(
         kernel,
         out_shape=out_shape,
@@ -25,7 +25,7 @@
         scratch_shapes=list(scratch),
         input_output_aliases=aliases or {},
         cost_estimate=pl.CostEstimate(flops=int(cost * 1e9), bytes_accessed=0, transcendentals=0),
-        compiler_params=pltpu.CompilerParams(vmem_limit_bytes=16 * 2**20),
+        compiler_params=pltpu.CompilerParams(vmem_limit_bytes=limit * 2**20),
         name=name,
     )
 
@@ -62,14 +62,26 @@
     return (jnp.minimum(first, second), jnp.maximum(first, second), jnp.int32(8))
 
 
-def pack_kernel(rows_part, columns, tiles, pivots, own, part, offsets):
+def pack_kernel(rows_part, columns_far, tiles_far, pivots_far, own, part, offsets, *scratch):
+    columns, tiles, pivots, sems = scratch
     shard_rows, slots, order, _ = tiles.shape
+    copies = [
+        pltpu.make_async_copy(far, near, sems.at[i])
+        for i, (far, near) in enumerate(((columns_far, columns), (pivots_far, pivots)))
+    ]
+    for row in range(shard_rows):
+        copies.append(pltpu.make_async_copy(tiles_far.at[row], tiles.at[row], sems.at[2 + row]))
+    for copy in copies:
+        copy.start()
+    copies[0].wait()
     start = (lax.axis_index("blk") * SPAN + lax.axis_index("pos")) * shard_rows
     offs = offsets_of(columns, start)
     for k in range(3):
         offsets[0, k] = offs[k]
     at = [lax.broadcasted_iota(jnp.int32, (order, order), d) for d in range(2)]
+    copies[1].wait()
     for row in range(shard_rows):
+        copies[2 + row].wait()
         sums = [jnp.zeros((order, order), F32) for _ in range(4)]
         for slot in range(slots):
             away = columns[row, slot] - (start + row)
@@ -81,8 +93,8 @@
         own[row, :order] = jnp.concatenate([sums[0], sums[1]], axis=1)
         own[row, order : 2 * order] = jnp.concatenate([sums[2], both], axis=1)
         own[row, 2 * order :] = jnp.broadcast_to(jnp.concatenate([line, line], axis=1), (8, 2 * order))
-    for r in range(rows_part):
-        part[r] = own[lax.axis_index("rhs") * rows_part + r]
+    for a in range(rows_part):
+        part[a] = own[lax.axis_index("rhs") * rows_part + a]
 
 
 def band_kernel(first_row, columns, tiles, band_high, band_low, band):
@@ -315,6 +327,7 @@
 
 
 def halo_kernel(rows, arrived, out):
+    out[...] = rows[...]
     out[0, 1, 0] = arrived[...]
 
 
@@ -376,7 +389,7 @@
         rest = product(rest, *halves(rest), NN)
         return total + product(total, *halves(rest), NN), rest
 
-    for _ in range(5):
+    for _ in range(7):
         total, rest = step(total, rest)
 
     def going(carry):
@@ -405,17 +418,16 @@
     s1, s2, s3, s4 = [
         symmetric(sums[k // 2][:, k % 2 * total : (k % 2 + 1) * total]) for k in range(4)
     ]
-    inv = inverse(s2)
-    c = small(inv, s3)
-    schur = symmetric(s4 - small(s3, c))
-    h = small(s2 - s1 - small(s1, c), inverse(schur))
-    f = small(s1 - small(h, s3), inv)
+    gram = jnp.concatenate(
+        [jnp.concatenate([s2, s3], axis=1), jnp.concatenate([s3, s4], axis=1)], axis=0
+    )
+    weights = small(jnp.concatenate([s1, s2 - s1], axis=1), inverse(gram))
     pick = lax.broadcasted_iota(jnp.int32, (count, total), 0) + rhs * count
     pick = jnp.where(pick == lax.broadcasted_iota(jnp.int32, pick.shape, 1), 1.0, 0.0)
-    f, h = small(pick, f), small(pick, h)
-    solution[...] = small(f, d[...]) + small(h, e[...])
+    weights = small(pick, weights)
     own = r[pl.ds(pl.multiple_of(rhs * count, count), count), :]
-    residual[...] = own - small(f, q[...]) - small(h, w[...])
+    solution[...] = small(weights, jnp.concatenate([d[...], e[...]], axis=0))
+    residual[...] = own - small(weights, jnp.concatenate([q[...], w[...]], axis=0))
 
 
 def swapped(value, axis, bit):
@@ -471,9 +483,16 @@
             S((rows_part, tall, 2 * order), F32),
             S((1, 3), jnp.int32),
         ],
-        [SMEM, VMEM, VMEM],
+        [pl.BlockSpec(memory_space=pl.ANY)] * 3,
         [VMEM, VMEM, SMEM],
+        [
+            pltpu.SMEM(columns.shape, jnp.int32),
+            pltpu.VMEM(tiles.shape, F32),
+            pltpu.VMEM(pivots.shape, F32),
+            pltpu.SemaphoreType.DMA((2 + shard_rows,)),
+        ],
         cost=2,
+        limit=60,
     )(columns, tiles, pivots)
 
     vectors, vector = S((SPAN, each, cells), F32), S((each, cells), F32)
@@ -497,7 +516,7 @@
             [SMEM, VMEM],
             [VMEM] * 2,
             [pltpu.VMEM((3 * cells, cells // 2), F32)],
-            cost=2,
+            cost=20,
         )(columns, tiles)
 
     own, r = lax.optimization_barrier((own, r))
@@ -586,7 +605,7 @@
     (rows,) = sweep(
         fifth_kernel, "backward_v", [spread_shape], t, last, z, from_below, from_above, cost=4
     )
-    rows = call(halo_kernel, "halo", spread_shape, [VMEM] * 2, aliases={0: 0})(rows, last_below)
+    rows = call(halo_kernel, "halo", spread_shape, [VMEM] * 2)(rows, last_below)
     rows = lax.all_to_all(rows, "pos", 0, 0, tiled=True)
 
     full, sums_shape = S((total, cells), F32), S((total, 2 * total), F32)

time: 116 us -> 111 us (0.957)
  blocking collectives: 9.44 us -> 0 us
  starting transfers between devices: 31.8 us -> 36.8 us
  Pallas kernels: 54.2 us -> 53 us
    all_to_all x1 -> x0, blocking collectives: 9.44 us -> none  [shards(): rows = lax.all_to_all(rows, 'pos', 0, 0, tiled=True)]
    all_to_all x0 -> x1, starting transfers between devices: none -> 5.1 us  [shards(): rows = lax.all_to_all(rows, 'pos', 0, 0, tiled=True)]
    pallas_call x1, Pallas kernels: 9.21 us -> 6.05 us  [shards(): call(last_kernel, 'update', [S((count, cells), F32)] * 2, [VMEM] * 7, [VM...]
    pallas_call x1, Pallas kernels: 1.78 us -> 3.06 us  [shards(): call(functools.partial(pack_kernel, rows_part), 'pack_tiles', [S((shard_r...]
    unnamed x12 -> x18, local copies, waits for them, and re-layouts: 3.14 us -> 3.5 us
  transfers between devices with their start and end apart: 29 -> 30, of which waited for: 7 -> 9; matrix products, arithmetic and copies ran while one was open for 1% -> 1% of each run, Pallas kernels for 23% -> 38%
where the time goes in v4:
time: 111 us
  Pallas kernels  53 us (48%)
  starting transfers between devices  36.8 us (33%)
  waiting for transfers between devices  15.8 us (14%)
  local copies, waits for them, and re-layouts  4.21 us (4%)
    pallas_call x8, Pallas kernels, with_mats(): call(body, name, [*out_shapes, *mat_shapes], [*specs, *[VMEM] * 6], [VMEM...  33.8 us
    ppermute x25, starting transfers between devices, swapped(): lax.ppermute(value, axis, [(i, i ^ bit) for i in range(lax.axis_size(axis...  16.1 us
    all_to_all x1, starting transfers between devices, shards(): lax.all_to_all(right_side.reshape(SPAN, each, cells), 'pos', 0, 0, tiled=...  7.13 us
    ppermute x25, waiting for transfers between devices, swapped(): lax.ppermute(value, axis, [(i, i ^ bit) for i in range(lax.axis_size(axis...  6.81 us
    pallas_call x1, Pallas kernels, shards(): call(last_kernel, 'update', [S((count, cells), F32)] * 2, [VMEM] * 7, [VM...  6.05 us
    ppermute x1, waiting for transfers between devices, shards(): e_above = lax.ppermute(e, ('blk', 'pos'), down_rows)  5.97 us
    all_to_all x1, starting transfers between devices, shards(): rows = lax.all_to_all(rows, 'pos', 0, 0, tiled=True)  5.1 us
    ppermute x1, starting transfers between devices, shards(): last_below = lax.ppermute(last, 'blk', up)  4.59 us
  transfers between devices with their start and end apart: 30, of which 9 were waited for; matrix products, arithmetic and copies ran while one was open for 1% of the time, Pallas kernels for 38%

profile of v4, /device:TPU:14, one launch (start us, length us, event | category | flops | bytes accessed | tf_op | source)
XLA Modules:
  0.0 111.0 jit_solution(460377672253999095)
XLA Ops:
  0.6 3.1 %pack_tiles.1 = (f32[8,136,128]{2,1,0:T(8,128)}, f32[4,136,128]{2,1,0:T(8,128)}, s32[1,3]{1,0:T(1,128)}) custom-call(s32[8,7]{1,0:T(8,128)} %columns.3, f32[8,7,64,64]{3,2,1,0:T(8,128)} %tiles.3, f32[8,64,64]{2,1,0:T(8,128)} %pivots_far.1), custom_call_target="tpu_custom_call" | custom-call | flops 2000000000 | tf_op jit(solution)/shard_map/pack_tiles/pallas_call | solution.py:478
  5.5 7.1 %all-to-all-start = ((f32[8,4,512]{2,1,0:T(4,128)}), f32[8,4,512]{2,1,0:T(4,128)S(1)}, u32[]{:S(2)}, u32[]{:S(2)}) async-start(f32[8,4,512]{2,1,0:T(4,128)} %reshape.7), calls=%async_computation | async-start | bytes 131072 | tf_op jit(solution)/shard_map/all_to_all | solution.py:499
  13.4 2.1 %all-to-all-done.refs_0_ = f32[8,4,512]{2,1,0:T(4,128)S(1)} async-done(((f32[8,4,512]{2,1,0:T(4,128)}), f32[8,4,512]{2,1,0:T(4,128)S(1)}, u32[]{:S(2)}, u32[]{:S(2)}) %all-to-all-start) | async-done | bytes 65568 | tf_op jit(solution)/shard_map/all_to_all | solution.py:499
  21.8 4.2 %factors_own.1 = (bf16[8,2,512,512]{3,2,1,0:T(8,128)(2,1)S(1)}, bf16[8,2,512,512]{3,2,1,0:T(8,128)(2,1)S(1)}, bf16[8,512,512]{2,1,0:T(8,128)(2,1)S(1)}, bf16[8,5...) custom-call(s32[1,3]{1,0:T(1,128)S(1)} %copy-done.1, ...), custom_call_target="tpu_custom_call" | custom-call | flops 4000000000 | tf_op jit(solution)/shard_map/factors_own/pallas_call | solution.py:523
  29.3 6.1 %factors_near.1 = (bf16[8,2,512,512]{3,2,1,0:T(8,128)(2,1)S(1)}, bf16[8,2,512,512]{3,2,1,0:T(8,128)(2,1)S(1)}, bf16[8,512,512]{2,1,0:T(8,128)(2,1)S(1)}, bf16[8,...) custom-call(s32[1,3]{1,0:T(1,128)S(1)} %copy-done.1, ...), custom_call_target="tpu_custom_call", output_to_operand_aliasing={{0}: (7, {}), {1}: (8, {}), {2}: (9, {}), {3}: (10, {}), {4... | custom-call | flops 6000000000 | tf_op jit(solution)/shard_map/factors_near/pallas_call | solution.py:540
  36.1 6.1 %factors_mid.1 = (bf16[8,2,512,512]{3,2,1,0:T(8,128)(2,1)S(1)}, bf16[8,2,512,512]{3,2,1,0:T(8,128)(2,1)S(1)}, bf16[8,512,512]{2,1,0:T(8,128)(2,1)S(1)}, bf16[8,5...) custom-call(s32[1,3]{1,0:T(1,128)S(1)} %copy-done.1, ...), custom_call_target="tpu_custom_call", output_to_operand_aliasing={{0}: (7, {}), {1}: (8, {}), {2}: (9, {}), {3}: (10, {}), {4... | custom-call | flops 6000000000 | tf_op jit(solution)/shard_map/factors_mid/pallas_call | solution.py:540
  42.3 2.7 %factors_far.1 = (bf16[8,2,512,512]{3,2,1,0:T(8,128)(2,1)S(1)}, bf16[8,2,512,512]{3,2,1,0:T(8,128)(2,1)S(1)}, bf16[8,512,512]{2,1,0:T(8,128)(2,1)S(1)}, bf16[8,5...) custom-call(s32[1,3]{1,0:T(1,128)S(1)} %copy-done.1, ...), custom_call_target="tpu_custom_call", output_to_operand_aliasing={{0}: (5, {}), {1}: (6, {}), {2}: (7, {}), {3}: (8, {}), {4}... | custom-call | flops 3000000000 | tf_op jit(solution)/shard_map/factors_far/pallas_call | solution.py:540
  45.0 4.1 %forward_r.1 = (f32[8,4,512]{2,1,0:T(4,128)S(1)}, f32[2,4,512]{2,1,0:T(4,128)S(1)}, bf16[8,2,512,512]{3,2,1,0:T(8,128)(2,1)S(1)}, bf16[8,2,512,512]{3,2,1,0:T(8,...) custom-call(f32[8,4,512]{2,1,0:T(4,128)S(1)} %all-to-all-done.refs_0, ...), custom_call_target="tpu_custom_call", output_to_operand_aliasing={{2}: (1, {}), {3}: (2, {}), {4}: (3, {}), {5}: (4, {}), {6}... | custom-call | flops 4000000000 | tf_op jit(solution)/shard_map/forward_r/pallas_call | solution.py:540
  49.1 4.1 %backward_r.1 = (f32[8,4,512]{2,1,0:T(4,128)S(1)}, f32[8,4,512]{2,1,0:T(4,128)S(1)}, f32[3,4,512]{2,1,0:T(4,128)S(1)}, bf16[8,2,512,512]{3,2,1,0:T(8,128)(2,1)S(...) custom-call(f32[8,4,512]{2,1,0:T(4,128)S(1)} %get-tuple-element.104., ...), custom_call_target="tpu_custom_call", output_to_operand_aliasing={{3}: (2, {}), {4}: (3, {}), {5}: (4, {}), {6}: (5, {}), {7}... | custom-call | flops 4000000000 | tf_op jit(solution)/shard_map/backward_r/pallas_call | solution.py:540
  53.3 2.6 %collective-permute-start.17 = (f32[3,4,512]{2,1,0:T(4,128)S(1)}, f32[3,4,512]{2,1,0:T(4,128)S(1)}, u32[]{:S(2)}, u32[]{:S(2)}) collective-permute-start(f32[3,4,512]{2,1,0:T(4,128)S(1)} %get-tuple-element.122), channel_id=1, source_target_pairs={{0,16},{16,0},{1,17},{17,1},{2,18},{18,2},{3,19},{19,3},{4,20},{20... | collective-permute-start | bytes 73736 | tf_op jit(solution)/shard_map/ppermute | solution.py:455
  55.9 2.3 %residue_of_z.1 = (f32[8,4,512]{2,1,0:T(4,128)S(1)}, f32[8,4,512]{2,1,0:T(4,128)S(1)}, bf16[8,2,512,512]{3,2,1,0:T(8,128)(2,1)S(1)}, bf16[8,2,512,512]{3,2,1,0:T...) custom-call(f32[8,4,512]{2,1,0:T(4,128)S(1)} %all-to-all-done.refs_0, ...), custom_call_target="tpu_custom_call", output_to_operand_aliasing={{2}: (4, {}), {3}: (5, {}), {4}: (6, {}), {5}: (7, {}), {6}... | custom-call | flops 2000000000 | tf_op jit(solution)/shard_map/residue_of_z/pallas_call | solution.py:540
  58.2 4.1 %forward_v.1 = (f32[8,4,512]{2,1,0:T(4,128)S(1)}, f32[4,512]{1,0:T(4,128)S(1)}, bf16[8,2,512,512]{3,2,1,0:T(8,128)(2,1)S(1)}, bf16[8,2,512,512]{3,2,1,0:T(8,128)...) custom-call(f32[8,4,512]{2,1,0:T(4,128)S(1)} %get-tuple-element.120., ...), custom_call_target="tpu_custom_call", output_to_operand_aliasing={{2}: (4, {}), {3}: (5, {}), {4}: (6, {}), {5}: (7, {}), {6}... | custom-call | flops 4000000000 | tf_op jit(solution)/shard_map/forward_v/pallas_call | solution.py:540
  62.3 4.6 %collective-permute-start.18 = (f32[4,512]{1,0:T(4,128)S(1)}, f32[4,512]{1,0:T(4,128)S(1)}, u32[]{:S(2)}, u32[]{:S(2)}) collective-permute-start(f32[4,512]{1,0:T(4,128)S(1)} %get-tuple-element.130.refs_1_), channel_id=1, source_target_pairs={{0,16},{1,17},{2,18},{3,19},{4,20},{5,21},{6,22},{7,23},{8,24},{9,... | collective-permute-start | bytes 24584 | tf_op jit(solution)/shard_map/ppermute | solution.py:604
  66.9 4.1 %backward_v.1 = (f32[8,2,3,4,512]{4,3,2,1,0:T(4,128)S(1)}, bf16[8,2,512,512]{3,2,1,0:T(8,128)(2,1)S(1)}, bf16[8,2,512,512]{3,2,1,0:T(8,128)(2,1)S(1)}, bf16[8,51...) custom-call(f32[8,4,512]{2,1,0:T(4,128)S(1)} %get-tuple-element.129., ...), custom_call_target="tpu_custom_call", output_to_operand_aliasing={{1}: (5, {}), {2}: (6, {}), {3}: (7, {}), {4}: (8, {}), {5}... | custom-call | flops 4000000000 | tf_op jit(solution)/shard_map/backward_v/pallas_call | solution.py:540
  71.9 5.1 %all-to-all-start.1 = ((f32[8,2,3,4,512]{4,3,2,1,0:T(4,128)}), f32[8,2,3,4,512]{4,3,2,1,0:T(4,128)S(1)}, u32[]{:S(2)}, u32[]{:S(2)}) async-start(f32[8,2,3,4,512]{4,3,2,1,0:T(4,128)} %halo.1), calls=%async_computation.1 | async-start | bytes 786432 | tf_op jit(solution)/shard_map/all_to_all | solution.py:609
  77.0 1.7 %row_band.2 = (bf16[1536,256]{1,0:T(8,128)(2,1)S(1)}, bf16[1536,256]{1,0:T(8,128)(2,1)S(1)}) custom-call(s32[8,7]{1,0:T(8,128)S(1)} %copy-done.3, f32[8,7,64,64]{3,2,1,0:T(8,128)S(1)} %copy-done.2), custom_call_target="tpu_custom_call" | custom-call | flops 20000000000 | tf_op jit(solution)/shard_map/row_band/pallas_call | solution.py:512
  81.4 1.7 %row_band.3 = (bf16[1536,256]{1,0:T(8,128)(2,1)S(1)}, bf16[1536,256]{1,0:T(8,128)(2,1)S(1)}) custom-call(s32[8,7]{1,0:T(8,128)S(1)} %copy-done.3, f32[8,7,64,64]{3,2,1,0:T(8,128)S(1)} %copy-done.2), custom_call_target="tpu_custom_call" | custom-call | flops 20000000000 | tf_op jit(solution)/shard_map/row_band/pallas_call | solution.py:512
  84.6 1.5 %collective-permute-start.20 = (f32[64,128]{1,0:T(8,128)S(1)}, f32[64,128]{1,0:T(8,128)S(1)}, u32[]{:S(2)}, u32[]{:S(2)}) collective-permute-start(f32[64,128]{1,0:T(8,128)S(1)} %get-tuple-element.142), channel_id=1, source_target_pairs={{0,2},{2,0},{4,6},{6,4},{8,10},{10,8},{12,14},{14,12},{16,18},{18,... | collective-permute-start | bytes 98312 | tf_op jit(solution)/shard_map/ppermute | solution.py:434
  86.1 1.5 %collective-permute-start.21 = (f32[64,128]{1,0:T(8,128)S(1)}, f32[64,128]{1,0:T(8,128)S(1)}, u32[]{:S(2)}, u32[]{:S(2)}) collective-permute-start(f32[64,128]{1,0:T(8,128)S(1)} %get-tuple-element.142), channel_id=1, source_target_pairs={{0,4},{2,6},{4,0},{6,2},{8,12},{10,14},{12,8},{14,10},{16,20},{18,... | collective-permute-start | bytes 98312 | tf_op jit(solution)/shard_map/ppermute | solution.py:434
  88.6 1.5 %collective-permute-done.21 = f32[64,128]{1,0:T(8,128)S(1)} collective-permute-done((f32[64,128]{1,0:T(8,128)S(1)}, f32[64,128]{1,0:T(8,128)S(1)}, u32[]{:S(2)}, u32[]{:S(2)}) %collective-permute-start.21) | collective-permute-done | bytes 32800 | tf_op jit(solution)/shard_map/ppermute | solution.py:434
  90.0 2.4 %collective-permute-done.22 = f32[64,128]{1,0:T(8,128)S(1)} collective-permute-done((f32[64,128]{1,0:T(8,128)S(1)}, f32[64,128]{1,0:T(8,128)S(1)}, u32[]{:S(2)}, u32[]{:S(2)}) %collective-permute-start.22) | collective-permute-done | bytes 32800 | tf_op jit(solution)/shard_map/ppermute | solution.py:434
  93.7 2.2 %collective-permute-start.25 = (f32[64,128]{1,0:T(8,128)S(1)}, f32[64,128]{1,0:T(8,128)S(1)}, u32[]{:S(2)}, u32[]{:S(2)}) collective-permute-start(f32[64,128]{1,0:T(8,128)S(1)} %add_add_fusion.1), channel_id=1, source_target_pairs={{0,24},{2,26},{4,28},{6,30},{8,16},{10,18},{12,20},{14,22},{16,8},... | collective-permute-start | bytes 98312 | tf_op jit(solution)/shard_map/ppermute | solution.py:434
  98.6 6.0 %collective-permute-done.27.arrived = f32[64,512]{1,0:T(8,128)S(1)} collective-permute-done((f32[64,512]{1,0:T(8,128)S(1)}, f32[64,512]{1,0:T(8,128)S(1)}, u32[]{:S(2)}, u32[]{:S(2)}) %collective-permute-start.27) | collective-permute-done | bytes 131104 | tf_op jit(solution)/shard_map/ppermute | solution.py:622
  104.9 6.1 %update.1 = (f32[32,512]{1,0:T(8,128)}, f32[32,512]{1,0:T(8,128)}) custom-call(f32[64,128]{1,0:T(8,128)S(1)} %add_add_fusion.own_sums, f32[64,128]{1,0:T(8,128)S(1)} %collective-permute-done.26.other_sums, f32[64,512]{1,0:T(8,128)S(1)} %get-tuple-element.143.r, f32[64,512]{1,0:T(8,128)S(1)} %get-tuple-element.144.d, f32[64,512]{1,0:T(8,128)S(1)} %get-tuple-element.145.q, ...), custom_call_target="tpu_custom_call" | custom-call | flops 8000000000 | tf_op jit(solution)/shard_map/update/pallas_call | solution.py:624
  (83 shorter events, 23.0 us)
Async XLA Ops:
  3.7 9.0 %collective-permute-start.2 = (f32[4,136,128]{2,1,0:T(8,128)}, f32[4,136,128]{2,1,0:T(8,128)S(1)}, u32[]{:S(2)}, u32[]{:S(2)}) collective-permute-start(f32[4,136,128]{2,1,0:T(8,128)} %get-tuple-element.78), channel_id=1, source_target_pairs={{0,8},{2,10},{4,12},{6,14},{8,0},{10,2},{12,4},{14,6},{1,9},{3,11}... | collective-permute-start | bytes 835592 | tf_op jit(solution)/shard_map/ppermute | solution.py:434
  4.2 8.5 %collective-permute-start.8 = (f32[4,136,128]{2,1,0:T(8,128)}, f32[4,136,128]{2,1,0:T(8,128)S(1)}, u32[]{:S(2)}, u32[]{:S(2)}) collective-permute-start(f32[4,136,128]{2,1,0:T(8,128)} %get-tuple-element.78), channel_id=1, source_target_pairs={{0,4},{2,6},{4,0},{6,2},{8,12},{10,14},{12,8},{14,10},{1,5},{3,7},... | collective-permute-start | bytes 835592 | tf_op jit(solution)/shard_map/ppermute | solution.py:434
  4.7 10.7 %collective-permute-start.1 = (f32[4,136,128]{2,1,0:T(8,128)}, f32[4,136,128]{2,1,0:T(8,128)S(1)}, u32[]{:S(2)}, u32[]{:S(2)}) collective-permute-start(f32[4,136,128]{2,1,0:T(8,128)} %get-tuple-element.78), channel_id=1, source_target_pairs={{0,2},{2,0},{4,6},{6,4},{8,10},{10,8},{12,14},{14,12},{1,3},{3,1},... | collective-permute-start | bytes 835592 | tf_op jit(solution)/shard_map/ppermute | solution.py:434
  5.5 9.9 %all-to-all-start = ((f32[8,4,512]{2,1,0:T(4,128)}), f32[8,4,512]{2,1,0:T(4,128)S(1)}, u32[]{:S(2)}, u32[]{:S(2)}) async-start(f32[8,4,512]{2,1,0:T(4,128)} %reshape.7), calls=%async_computation | async-start | bytes 131072 | tf_op jit(solution)/shard_map/all_to_all | solution.py:499
  12.7 7.3 %collective-permute-start.9 = (f32[4,128,128]{2,1,0:T(8,128)S(1)}, f32[4,128,128]{2,1,0:T(8,128)S(1)}, u32[]{:S(2)}, u32[]{:S(2)}) collective-permute-start(f32[4,128,128]{2,1,0:T(8,128)S(1)} %pad_maximum_fusion.2), channel_id=1, source_target_pairs={{0,2},{2,0},{4,6},{6,4},{8,10},{10,8},{12,14},{14,12},{1,3},{3,1},... | collective-permute-start | bytes 786440 | tf_op jit(solution)/shard_map/ppermute | solution.py:434
  15.5 10.6 %collective-permute-start.3 = (f32[4,136,128]{2,1,0:T(8,128)S(1)}, f32[4,136,128]{2,1,0:T(8,128)S(1)}, u32[]{:S(2)}, u32[]{:S(2)}) collective-permute-start(f32[4,136,128]{2,1,0:T(8,128)S(1)} %pad_maximum_fusion.1), channel_id=1, source_target_pairs={{0,4},{2,6},{4,0},{6,2},{8,12},{10,14},{12,8},{14,10},{1,5},{3,7},... | collective-permute-start | bytes 835592 | tf_op jit(solution)/shard_map/ppermute | solution.py:434
  16.9 11.8 %collective-permute-start.12 = (f32[4,144,128]{2,1,0:T(8,128)S(1)}, f32[4,144,128]{2,1,0:T(8,128)S(1)}, u32[]{:S(2)}, u32[]{:S(2)}) collective-permute-start(f32[4,144,128]{2,1,0:T(8,128)S(1)} %pad_maximum_fusion), channel_id=1, source_target_pairs={{0,8},{2,10},{4,12},{6,14},{8,0},{10,2},{12,4},{14,6},{1,9},{3,11}... | collective-permute-start | bytes 884744 | tf_op jit(solution)/shard_map/ppermute | solution.py:434
  18.4 8.3 %collective-permute-start.15 = (f32[4,136,128]{2,1,0:T(8,128)S(1)}, f32[4,136,128]{2,1,0:T(8,128)S(1)}, u32[]{:S(2)}, u32[]{:S(2)}) collective-permute-start(f32[4,136,128]{2,1,0:T(8,128)S(1)} %collective-permute-done.8.refs_3_), channel_id=1, source_target_pairs={{0,1},{1,0},{2,3},{3,2},{4,5},{5,4},{6,7},{7,6},{8,9},{9,8},{10,11... | collective-permute-start | bytes 835592 | tf_op jit(solution)/shard_map/ppermute | solution.py:434
  18.4 9.7 %collective-permute-start.14 = (f32[4,136,128]{2,1,0:T(8,128)S(1)}, f32[4,136,128]{2,1,0:T(8,128)S(1)}, u32[]{:S(2)}, u32[]{:S(2)}) collective-permute-start(f32[4,136,128]{2,1,0:T(8,128)S(1)} %collective-permute-done.1.refs_1_), channel_id=1, source_target_pairs={{0,1},{1,0},{2,3},{3,2},{4,5},{5,4},{6,7},{7,6},{8,9},{9,8},{10,11... | collective-permute-start | bytes 835592 | tf_op jit(solution)/shard_map/ppermute | solution.py:434
  20.1 8.7 %collective-permute-start.16 = (f32[4,136,128]{2,1,0:T(8,128)S(1)}, f32[4,136,128]{2,1,0:T(8,128)S(1)}, u32[]{:S(2)}, u32[]{:S(2)}) collective-permute-start(f32[4,136,128]{2,1,0:T(8,128)S(1)} %collective-permute-done.2.refs_5_), channel_id=1, source_target_pairs={{0,1},{1,0},{2,3},{3,2},{4,5},{5,4},{6,7},{7,6},{8,9},{9,8},{10,11... | collective-permute-start | bytes 835592 | tf_op jit(solution)/shard_map/ppermute | solution.py:434
  26.1 9.9 %collective-permute-start.10 = (f32[4,128,128]{2,1,0:T(8,128)S(1)}, f32[4,128,128]{2,1,0:T(8,128)S(1)}, u32[]{:S(2)}, u32[]{:S(2)}) collective-permute-start(f32[4,128,128]{2,1,0:T(8,128)S(1)} %collective-permute-done.9.refs_1_), channel_id=1, source_target_pairs={{0,1},{1,0},{2,3},{3,2},{4,5},{5,4},{6,7},{7,6},{8,9},{9,8},{10,11... | collective-permute-start | bytes 786440 | tf_op jit(solution)/shard_map/ppermute | solution.py:434
  26.7 8.9 %collective-permute-start.6 = (f32[4,72,128]{2,1,0:T(8,128)S(1)}, f32[4,72,128]{2,1,0:T(8,128)S(1)}, u32[]{:S(2)}, u32[]{:S(2)}) collective-permute-start(f32[4,72,128]{2,1,0:T(8,128)S(1)} %slice.29), channel_id=1, source_target_pairs={{0,8},{2,10},{4,12},{6,14},{8,0},{10,2},{12,4},{14,6},{1,9},{3,11}... | collective-permute-start | bytes 442376 | tf_op jit(solution)/shard_map/ppermute | solution.py:434
  28.1 7.3 %collective-permute-start.4 = (f32[4,64,128]{2,1,0:T(8,128)S(1)}, f32[4,64,128]{2,1,0:T(8,128)S(1)}, u32[]{:S(2)}, u32[]{:S(2)}) collective-permute-start(f32[4,64,128]{2,1,0:T(8,128)S(1)} %slice.28), channel_id=1, source_target_pairs={{0,2},{2,0},{4,6},{6,4},{8,10},{10,8},{12,14},{14,12},{1,3},{3,1},... | collective-permute-start | bytes 393224 | tf_op jit(solution)/shard_map/ppermute | solution.py:434
  28.8 7.3 %collective-permute-start.11 = (f32[4,136,128]{2,1,0:T(8,128)S(1)}, f32[4,136,128]{2,1,0:T(8,128)S(1)}, u32[]{:S(2)}, u32[]{:S(2)}) collective-permute-start(f32[4,136,128]{2,1,0:T(8,128)S(1)} %collective-permute-done.3.refs_3_), channel_id=1, source_target_pairs={{0,1},{1,0},{2,3},{3,2},{4,5},{5,4},{6,7},{7,6},{8,9},{9,8},{10,11... | collective-permute-start | bytes 835592 | tf_op jit(solution)/shard_map/ppermute | solution.py:434
  28.8 7.3 %collective-permute-start.13 = (f32[4,144,128]{2,1,0:T(8,128)S(1)}, f32[4,144,128]{2,1,0:T(8,128)S(1)}, u32[]{:S(2)}, u32[]{:S(2)}) collective-permute-start(f32[4,144,128]{2,1,0:T(8,128)S(1)} %collective-permute-done.12.refs_5_), channel_id=1, source_target_pairs={{0,1},{1,0},{2,3},{3,2},{4,5},{5,4},{6,7},{7,6},{8,9},{9,8},{10,11... | collective-permute-start | bytes 884744 | tf_op jit(solution)/shard_map/ppermute | solution.py:434
  35.4 47.7 %collective-permute-start = (f32[32,512]{1,0:T(8,128)S(1)}, f32[32,512]{1,0:T(8,128)S(1)}, u32[]{:S(2)}, u32[]{:S(2)}) collective-permute-start(f32[32,512]{1,0:T(8,128)S(1)} %copy-done), channel_id=1, source_target_pairs={{0,1},{1,0},{2,3},{3,2},{4,5},{5,4},{6,7},{7,6},{8,9},{9,8},{10,11... | collective-permute-start | bytes 196616 | tf_op jit(solution)/shard_map/ppermute | solution.py:434
  35.6 6.7 %collective-permute-start.5 = (f32[4,64,128]{2,1,0:T(8,128)S(1)}, f32[4,64,128]{2,1,0:T(8,128)S(1)}, u32[]{:S(2)}, u32[]{:S(2)}) collective-permute-start(f32[4,64,128]{2,1,0:T(8,128)S(1)} %collective-permute-done.4.refs_1_), channel_id=1, source_target_pairs={{0,1},{1,0},{2,3},{3,2},{4,5},{5,4},{6,7},{7,6},{8,9},{9,8},{10,11... | collective-permute-start | bytes 393224 | tf_op jit(solution)/shard_map/ppermute | solution.py:434
  36.0 6.3 %collective-permute-start.7 = (f32[4,72,128]{2,1,0:T(8,128)S(1)}, f32[4,72,128]{2,1,0:T(8,128)S(1)}, u32[]{:S(2)}, u32[]{:S(2)}) collective-permute-start(f32[4,72,128]{2,1,0:T(8,128)S(1)} %collective-permute-done.6.refs_3_), channel_id=1, source_target_pairs={{0,1},{1,0},{2,3},{3,2},{4,5},{5,4},{6,7},{7,6},{8,9},{9,8},{10,11... | collective-permute-start | bytes 442376 | tf_op jit(solution)/shard_map/ppermute | solution.py:434
  53.3 4.9 %collective-permute-start.17 = (f32[3,4,512]{2,1,0:T(4,128)S(1)}, f32[3,4,512]{2,1,0:T(4,128)S(1)}, u32[]{:S(2)}, u32[]{:S(2)}) collective-permute-start(f32[3,4,512]{2,1,0:T(4,128)S(1)} %get-tuple-element.122), channel_id=1, source_target_pairs={{0,16},{16,0},{1,17},{17,1},{2,18},{18,2},{3,19},{19,3},{4,20},{20... | collective-permute-start | bytes 73736 | tf_op jit(solution)/shard_map/ppermute | solution.py:455
  62.3 8.8 %collective-permute-start.18 = (f32[4,512]{1,0:T(4,128)S(1)}, f32[4,512]{1,0:T(4,128)S(1)}, u32[]{:S(2)}, u32[]{:S(2)}) collective-permute-start(f32[4,512]{1,0:T(4,128)S(1)} %get-tuple-element.130.refs_1_), channel_id=1, source_target_pairs={{0,16},{1,17},{2,18},{3,19},{4,20},{5,21},{6,22},{7,23},{8,24},{9,... | collective-permute-start | bytes 24584 | tf_op jit(solution)/shard_map/ppermute | solution.py:604
  71.9 9.5 %all-to-all-start.1 = ((f32[8,2,3,4,512]{4,3,2,1,0:T(4,128)}), f32[8,2,3,4,512]{4,3,2,1,0:T(4,128)S(1)}, u32[]{:S(2)}, u32[]{:S(2)}) async-start(f32[8,2,3,4,512]{4,3,2,1,0:T(4,128)} %halo.1), calls=%async_computation.1 | async-start | bytes 786432 | tf_op jit(solution)/shard_map/all_to_all | solution.py:609
  93.4 4.9 %collective-permute-start.24 = (f32[64,128]{1,0:T(8,128)S(1)}, f32[64,128]{1,0:T(8,128)S(1)}, u32[]{:S(2)}, u32[]{:S(2)}) collective-permute-start(f32[64,128]{1,0:T(8,128)S(1)} %add_add_fusion.1), channel_id=1, source_target_pairs={{0,16},{2,18},{4,20},{6,22},{8,24},{10,26},{12,28},{14,30},{16,0},... | collective-permute-start | bytes 98312 | tf_op jit(solution)/shard_map/ppermute | solution.py:434
  95.9 8.6 %collective-permute-start.27 = (f32[64,512]{1,0:T(8,128)S(1)}, f32[64,512]{1,0:T(8,128)S(1)}, u32[]{:S(2)}, u32[]{:S(2)}) collective-permute-start(f32[64,512]{1,0:T(8,128)S(1)} %get-tuple-element.146.e), channel_id=1, source_target_pairs={{16,14},{17,15}} | collective-permute-start | bytes 393224 | tf_op jit(solution)/shard_map/ppermute | solution.py:622
  98.6 6.4 %collective-permute-start.26 = (f32[64,128]{1,0:T(8,128)S(1)}, f32[64,128]{1,0:T(8,128)S(1)}, u32[]{:S(2)}, u32[]{:S(2)}) collective-permute-start(f32[64,128]{1,0:T(8,128)S(1)} %add_add_fusion.own_sums), channel_id=1, source_target_pairs={{0,1},{1,0},{2,3},{3,2},{4,5},{5,4},{6,7},{7,6},{8,9},{9,8},{10,11... | collective-permute-start | bytes 98312 | tf_op jit(solution)/shard_map/ppermute | solution.py:434
  (15 other events, 47.1 us)

commit v5 on v4

--- a/solution.py
+++ b/solution.py
@@ -187,7 +187,12 @@
 
 def own_factor_kernel(offsets, own, m_high, m_low, w_high, w_low, g_high, g_low, split):
     mats = (m_high, m_low, w_high, w_low, g_high, g_low)
-    for ref in mats:
+    half = m_high.shape[2] // 2
+    for ref in (m_high, m_low):
+        for kind in range(2):
+            ref[:, kind, :half, : half * (1 + kind)] = jnp.zeros((SPAN, half, half * (1 + kind)), BF16)
+            ref[:, kind, half:, half * kind :] = jnp.zeros((SPAN, half, half * (2 - kind)), BF16)
+    for ref in mats[2:]:
         ref[...] = jnp.zeros_like(ref)
     factors(offsets, [own], split, [lax.axis_index("pos")], *mats)
 
@@ -326,9 +331,11 @@
     spread(out, 1, values, zero, zero)
 
 
-def halo_kernel(rows, arrived, out):
+def halo_kernel(rows, *refs):
+    out, odd = refs[-1], lax.axis_index("blk") % 2
     out[...] = rows[...]
-    out[0, 1, 0] = arrived[...]
+    for n, got in enumerate(refs[:-1]):
+        out[0, 1, 0] += got[...] * jnp.where(odd == n, 0.0, 1.0)
 
 
 def place_rows(place, t, rhs, rows, lanes=slice(None)):
@@ -410,7 +417,7 @@
     return 0.5 * (a + a.T)
 
 
-def last_kernel(own_sums, other_sums, r, d, q, e, w, solution, residual):
+def last_kernel(own_sums, other_sums, r, d, q, e, w, solution, residual, all_weights):
     count, total = solution.shape[0], r.shape[0]
     rhs = lax.axis_index("rhs")
     odd = rhs % 2 == 1
@@ -422,9 +429,8 @@
         [jnp.concatenate([s2, s3], axis=1), jnp.concatenate([s3, s4], axis=1)], axis=0
     )
     weights = small(jnp.concatenate([s1, s2 - s1], axis=1), inverse(gram))
-    pick = lax.broadcasted_iota(jnp.int32, (count, total), 0) + rhs * count
-    pick = jnp.where(pick == lax.broadcasted_iota(jnp.int32, pick.shape, 1), 1.0, 0.0)
-    weights = small(pick, weights)
+    all_weights[...] = weights
+    weights = all_weights[pl.ds(pl.multiple_of(rhs * count, count), count), :]
     own = r[pl.ds(pl.multiple_of(rhs * count, count), count), :]
     solution[...] = small(weights, jnp.concatenate([d[...], e[...]], axis=0))
     residual[...] = own - small(weights, jnp.concatenate([q[...], w[...]], axis=0))
@@ -447,12 +453,17 @@
     return value
 
 
-def both_ways(value):
-    blocks = lax.axis_size("blk")
-    low = high = None
+def exchanged(value):
+    blocks, got = lax.axis_size("blk"), []
     for first in range(min(2, blocks - 1)):
         pairs = [(i, i + 1) for i in range(first, blocks - 1, 2)]
-        got = lax.ppermute(value, "blk", pairs + [(b, a) for a, b in pairs])
+        got.append(lax.ppermute(value, "blk", pairs + [(b, a) for a, b in pairs]))
+    return got
+
+
+def both_ways(value):
+    low = high = None
+    for first, got in enumerate(exchanged(value)):
         even = lax.axis_index("blk") % 2 == first
         up, down = jnp.where(even, 0.0, got), jnp.where(even, got, 0.0)
         low, high = (up, down) if low is None else (low + up, high + down)
@@ -468,7 +479,6 @@
     each = count // SPAN
     total = count * parts
     S = jax.ShapeDtypeStruct
-    up = [(i, i + 1) for i in range(blocks - 1)]
     down_rows = [(SPAN * (i + 1), SPAN * (i + 1) - 1) for i in range(blocks - 1)]
 
     def others(value):
@@ -479,7 +489,7 @@
         functools.partial(pack_kernel, rows_part),
         "pack_tiles",
         [
-            S((shard_rows, tall, 2 * order), F32),
+            pltpu.VMEM((shard_rows, tall, 2 * order), F32),
             S((rows_part, tall, 2 * order), F32),
             S((1, 3), jnp.int32),
         ],
@@ -601,11 +611,11 @@
     t, last = sweep(
         fourth_kernel, "forward_v", [vectors, vector], source, t_left, from_below, from_above, cost=4
     )
-    last_below = lax.ppermute(last, "blk", up)
+    halos = exchanged(last)
     (rows,) = sweep(
         fifth_kernel, "backward_v", [spread_shape], t, last, z, from_below, from_above, cost=4
     )
-    rows = call(halo_kernel, "halo", spread_shape, [VMEM] * 2)(rows, last_below)
+    rows = call(halo_kernel, "halo", spread_shape, [VMEM] * (1 + len(halos)))(rows, *halos)
     rows = lax.all_to_all(rows, "pos", 0, 0, tiled=True)
 
     full, sums_shape = S((total, cells), F32), S((total, 2 * total), F32)
@@ -621,9 +631,15 @@
     sums = summed(sums)
     e_above = lax.ppermute(e, ("blk", "pos"), down_rows)
     w = call(complete_kernel, "complete", full, [VMEM] * 6)(w_part, e_above, *bands)
-    return call(last_kernel, "update", [S((count, cells), F32)] * 2, [VMEM] * 7, [VMEM] * 2, cost=8)(
-        sums, swapped(sums, "rhs", 1), r_full, d, q, e, w
-    )
+    return call(
+        last_kernel,
+        "update",
+        [S((count, cells), F32)] * 2,
+        [VMEM] * 7,
+        [VMEM] * 2,
+        [pltpu.VMEM((total, 2 * total), F32)],
+        cost=5,
+    )(sums, swapped(sums, "rhs", 1), r_full, d, q, e, w)
 
 
 def solution(mesh):

time: 111 us -> 108 us (0.973)
  starting transfers between devices: 36.8 us -> 34.9 us
    ppermute x2, starting transfers between devices: 7.22 us -> 5.32 us  [exchanged(): got.append(lax.ppermute(value, 'blk', pairs + [(b, a) for a, b in pairs]))]
    unnamed x18 -> x16, local copies, waits for them, and re-layouts: 3.5 us -> 2.46 us
  transfers between devices with their start and end apart: 30 -> 30, of which waited for: 9 -> 9; matrix products, arithmetic and copies ran while one was open for 1% -> 1% of each run, Pallas kernels for 38% -> 39%
where the time goes in v5:
time: 108 us; the launch traced here: 107 us
  Pallas kernels  52.4 us (49%)
  starting transfers between devices  34.9 us (32%)
  waiting for transfers between devices  15.8 us (15%)
  local copies, waits for them, and re-layouts  3.17 us (3%)
    pallas_call x8, Pallas kernels, with_mats(): call(body, name, [*out_shapes, *mat_shapes], [*specs, *[VMEM] * 6], [VMEM...  33.8 us
    ppermute x25, starting transfers between devices, swapped(): lax.ppermute(value, axis, [(i, i ^ bit) for i in range(lax.axis_size(axis...  16.1 us
    all_to_all x1, starting transfers between devices, shards(): lax.all_to_all(right_side.reshape(SPAN, each, cells), 'pos', 0, 0, tiled=...  7.13 us
    ppermute x25, waiting for transfers between devices, swapped(): lax.ppermute(value, axis, [(i, i ^ bit) for i in range(lax.axis_size(axis...  6.83 us
    ppermute x1, waiting for transfers between devices, shards(): e_above = lax.ppermute(e, ('blk', 'pos'), down_rows)  5.94 us
    pallas_call x1, Pallas kernels, shards(): call(last_kernel, 'update', [S((count, cells), F32)] * 2, [VMEM] * 7, [VM...  5.86 us
    ppermute x2, starting transfers between devices, exchanged(): got.append(lax.ppermute(value, 'blk', pairs + [(b, a) for a, b in pairs]))  5.32 us
    all_to_all x1, starting transfers between devices, shards(): rows = lax.all_to_all(rows, 'pos', 0, 0, tiled=True)  5.1 us
  transfers between devices with their start and end apart: 30, of which 9 were waited for; matrix products, arithmetic and copies ran while one was open for 1% of the time, Pallas kernels for 39%

profile of v5, /device:TPU:14, one launch (start us, length us, event | category | flops | bytes accessed | tf_op | source)
XLA Modules:
  0.0 107.3 jit_solution(14207904033689370677)
XLA Ops:
  0.6 2.8 %pack_tiles.1 = (f32[8,136,128]{2,1,0:T(8,128)S(1)}, f32[4,136,128]{2,1,0:T(8,128)}, s32[1,3]{1,0:T(1,128)}) custom-call(s32[8,7]{1,0:T(8,128)} %columns.3, f32[8,7,64,64]{3,2,1,0:T(8,128)} %tiles.3, f32[8,64,64]{2,1,0:T(8,128)} %pivots_far.1), custom_call_target="tpu_custom_call" | custom-call | flops 2000000000 | tf_op jit(solution)/shard_map/pack_tiles/pallas_call | solution.py:488
  5.3 7.1 %all-to-all-start = ((f32[8,4,512]{2,1,0:T(4,128)}), f32[8,4,512]{2,1,0:T(4,128)S(1)}, u32[]{:S(2)}, u32[]{:S(2)}) async-start(f32[8,4,512]{2,1,0:T(4,128)} %reshape.7), calls=%async_computation | async-start | bytes 131072 | tf_op jit(solution)/shard_map/all_to_all | solution.py:509
  13.1 2.1 %all-to-all-done.refs_0_ = f32[8,4,512]{2,1,0:T(4,128)S(1)} async-done(((f32[8,4,512]{2,1,0:T(4,128)}), f32[8,4,512]{2,1,0:T(4,128)S(1)}, u32[]{:S(2)}, u32[]{:S(2)}) %all-to-all-start) | async-done | bytes 65568 | tf_op jit(solution)/shard_map/all_to_all | solution.py:509
  20.5 4.0 %factors_own.1 = (bf16[8,2,512,512]{3,2,1,0:T(8,128)(2,1)S(1)}, bf16[8,2,512,512]{3,2,1,0:T(8,128)(2,1)S(1)}, bf16[8,512,512]{2,1,0:T(8,128)(2,1)S(1)}, bf16[8,5...) custom-call(s32[1,3]{1,0:T(1,128)S(1)} %copy-done.1, ...), custom_call_target="tpu_custom_call" | custom-call | flops 4000000000 | tf_op jit(solution)/shard_map/factors_own/pallas_call | solution.py:533
  27.7 6.1 %factors_near.1 = (bf16[8,2,512,512]{3,2,1,0:T(8,128)(2,1)S(1)}, bf16[8,2,512,512]{3,2,1,0:T(8,128)(2,1)S(1)}, bf16[8,512,512]{2,1,0:T(8,128)(2,1)S(1)}, bf16[8,...) custom-call(s32[1,3]{1,0:T(1,128)S(1)} %copy-done.1, ...), custom_call_target="tpu_custom_call", output_to_operand_aliasing={{0}: (7, {}), {1}: (8, {}), {2}: (9, {}), {3}: (10, {}), {4... | custom-call | flops 6000000000 | tf_op jit(solution)/shard_map/factors_near/pallas_call | solution.py:550
  34.6 6.1 %factors_mid.1 = (bf16[8,2,512,512]{3,2,1,0:T(8,128)(2,1)S(1)}, bf16[8,2,512,512]{3,2,1,0:T(8,128)(2,1)S(1)}, bf16[8,512,512]{2,1,0:T(8,128)(2,1)S(1)}, bf16[8,5...) custom-call(s32[1,3]{1,0:T(1,128)S(1)} %copy-done.1, ...), custom_call_target="tpu_custom_call", output_to_operand_aliasing={{0}: (7, {}), {1}: (8, {}), {2}: (9, {}), {3}: (10, {}), {4... | custom-call | flops 6000000000 | tf_op jit(solution)/shard_map/factors_mid/pallas_call | solution.py:550
  40.7 2.7 %factors_far.1 = (bf16[8,2,512,512]{3,2,1,0:T(8,128)(2,1)S(1)}, bf16[8,2,512,512]{3,2,1,0:T(8,128)(2,1)S(1)}, bf16[8,512,512]{2,1,0:T(8,128)(2,1)S(1)}, bf16[8,5...) custom-call(s32[1,3]{1,0:T(1,128)S(1)} %copy-done.1, ...), custom_call_target="tpu_custom_call", output_to_operand_aliasing={{0}: (5, {}), {1}: (6, {}), {2}: (7, {}), {3}: (8, {}), {4}... | custom-call | flops 3000000000 | tf_op jit(solution)/shard_map/factors_far/pallas_call | solution.py:550
  43.5 4.1 %forward_r.1 = (f32[8,4,512]{2,1,0:T(4,128)S(1)}, f32[2,4,512]{2,1,0:T(4,128)S(1)}, bf16[8,2,512,512]{3,2,1,0:T(8,128)(2,1)S(1)}, bf16[8,2,512,512]{3,2,1,0:T(8,...) custom-call(f32[8,4,512]{2,1,0:T(4,128)S(1)} %all-to-all-done.refs_0, ...), custom_call_target="tpu_custom_call", output_to_operand_aliasing={{2}: (1, {}), {3}: (2, {}), {4}: (3, {}), {5}: (4, {}), {6}... | custom-call | flops 4000000000 | tf_op jit(solution)/shard_map/forward_r/pallas_call | solution.py:550
  47.6 4.1 %backward_r.1 = (f32[8,4,512]{2,1,0:T(4,128)S(1)}, f32[8,4,512]{2,1,0:T(4,128)S(1)}, f32[3,4,512]{2,1,0:T(4,128)S(1)}, bf16[8,2,512,512]{3,2,1,0:T(8,128)(2,1)S(...) custom-call(f32[8,4,512]{2,1,0:T(4,128)S(1)} %get-tuple-element.104., ...), custom_call_target="tpu_custom_call", output_to_operand_aliasing={{3}: (2, {}), {4}: (3, {}), {5}: (4, {}), {6}: (5, {}), {7}... | custom-call | flops 4000000000 | tf_op jit(solution)/shard_map/backward_r/pallas_call | solution.py:550
  51.7 2.6 %collective-permute-start.17 = (f32[3,4,512]{2,1,0:T(4,128)S(1)}, f32[3,4,512]{2,1,0:T(4,128)S(1)}, u32[]{:S(2)}, u32[]{:S(2)}) collective-permute-start(f32[3,4,512]{2,1,0:T(4,128)S(1)} %get-tuple-element.122), channel_id=1, source_target_pairs={{0,16},{16,0},{1,17},{17,1},{2,18},{18,2},{3,19},{19,3},{4,20},{20... | collective-permute-start | bytes 73736 | tf_op jit(solution)/shard_map/ppermute | solution.py:460
  54.4 2.3 %residue_of_z.1 = (f32[8,4,512]{2,1,0:T(4,128)S(1)}, f32[8,4,512]{2,1,0:T(4,128)S(1)}, bf16[8,2,512,512]{3,2,1,0:T(8,128)(2,1)S(1)}, bf16[8,2,512,512]{3,2,1,0:T...) custom-call(f32[8,4,512]{2,1,0:T(4,128)S(1)} %all-to-all-done.refs_0, ...), custom_call_target="tpu_custom_call", output_to_operand_aliasing={{2}: (4, {}), {3}: (5, {}), {4}: (6, {}), {5}: (7, {}), {6}... | custom-call | flops 2000000000 | tf_op jit(solution)/shard_map/residue_of_z/pallas_call | solution.py:550
  56.7 4.1 %forward_v.1 = (f32[8,4,512]{2,1,0:T(4,128)S(1)}, f32[4,512]{1,0:T(4,128)S(1)}, bf16[8,2,512,512]{3,2,1,0:T(8,128)(2,1)S(1)}, bf16[8,2,512,512]{3,2,1,0:T(8,128)...) custom-call(f32[8,4,512]{2,1,0:T(4,128)S(1)} %get-tuple-element.120., ...), custom_call_target="tpu_custom_call", output_to_operand_aliasing={{2}: (4, {}), {3}: (5, {}), {4}: (6, {}), {5}: (7, {}), {6}... | custom-call | flops 4000000000 | tf_op jit(solution)/shard_map/forward_v/pallas_call | solution.py:550
  60.8 2.7 %collective-permute-start.18 = (f32[4,512]{1,0:T(4,128)S(1)}, f32[4,512]{1,0:T(4,128)S(1)}, u32[]{:S(2)}, u32[]{:S(2)}) collective-permute-start(f32[4,512]{1,0:T(4,128)S(1)} %get-tuple-element.130.refs_1_), channel_id=1, source_target_pairs={{0,16},{16,0},{1,17},{17,1},{2,18},{18,2},{3,19},{19,3},{4,20},{20... | collective-permute-start | bytes 24584 | tf_op jit(solution)/shard_map/ppermute | solution.py:460
  63.5 4.1 %backward_v.1 = (f32[8,2,3,4,512]{4,3,2,1,0:T(4,128)S(1)}, bf16[8,2,512,512]{3,2,1,0:T(8,128)(2,1)S(1)}, bf16[8,2,512,512]{3,2,1,0:T(8,128)(2,1)S(1)}, bf16[8,51...) custom-call(f32[8,4,512]{2,1,0:T(4,128)S(1)} %get-tuple-element.129., ...), custom_call_target="tpu_custom_call", output_to_operand_aliasing={{1}: (5, {}), {2}: (6, {}), {3}: (7, {}), {4}: (8, {}), {5}... | custom-call | flops 4000000000 | tf_op jit(solution)/shard_map/backward_v/pallas_call | solution.py:550
  68.4 5.1 %all-to-all-start.1 = ((f32[8,2,3,4,512]{4,3,2,1,0:T(4,128)}), f32[8,2,3,4,512]{4,3,2,1,0:T(4,128)S(1)}, u32[]{:S(2)}, u32[]{:S(2)}) async-start(f32[8,2,3,4,512]{4,3,2,1,0:T(4,128)} %halo.1), calls=%async_computation.1 | async-start | bytes 786432 | tf_op jit(solution)/shard_map/all_to_all | solution.py:619
  73.5 1.7 %row_band.2 = (bf16[1536,256]{1,0:T(8,128)(2,1)S(1)}, bf16[1536,256]{1,0:T(8,128)(2,1)S(1)}) custom-call(s32[8,7]{1,0:T(8,128)S(1)} %copy-done.3, f32[8,7,64,64]{3,2,1,0:T(8,128)S(1)} %copy-done.2), custom_call_target="tpu_custom_call" | custom-call | flops 20000000000 | tf_op jit(solution)/shard_map/row_band/pallas_call | solution.py:522
  78.0 1.7 %row_band.3 = (bf16[1536,256]{1,0:T(8,128)(2,1)S(1)}, bf16[1536,256]{1,0:T(8,128)(2,1)S(1)}) custom-call(s32[8,7]{1,0:T(8,128)S(1)} %copy-done.3, f32[8,7,64,64]{3,2,1,0:T(8,128)S(1)} %copy-done.2), custom_call_target="tpu_custom_call" | custom-call | flops 20000000000 | tf_op jit(solution)/shard_map/row_band/pallas_call | solution.py:522
  81.1 1.5 %collective-permute-start.20 = (f32[64,128]{1,0:T(8,128)S(1)}, f32[64,128]{1,0:T(8,128)S(1)}, u32[]{:S(2)}, u32[]{:S(2)}) collective-permute-start(f32[64,128]{1,0:T(8,128)S(1)} %get-tuple-element.142), channel_id=1, source_target_pairs={{0,2},{2,0},{4,6},{6,4},{8,10},{10,8},{12,14},{14,12},{16,18},{18,... | collective-permute-start | bytes 98312 | tf_op jit(solution)/shard_map/ppermute | solution.py:440
  82.6 1.5 %collective-permute-start.21 = (f32[64,128]{1,0:T(8,128)S(1)}, f32[64,128]{1,0:T(8,128)S(1)}, u32[]{:S(2)}, u32[]{:S(2)}) collective-permute-start(f32[64,128]{1,0:T(8,128)S(1)} %get-tuple-element.142), channel_id=1, source_target_pairs={{0,4},{2,6},{4,0},{6,2},{8,12},{10,14},{12,8},{14,10},{16,20},{18,... | collective-permute-start | bytes 98312 | tf_op jit(solution)/shard_map/ppermute | solution.py:440
  85.1 1.5 %collective-permute-done.21 = f32[64,128]{1,0:T(8,128)S(1)} collective-permute-done((f32[64,128]{1,0:T(8,128)S(1)}, f32[64,128]{1,0:T(8,128)S(1)}, u32[]{:S(2)}, u32[]{:S(2)}) %collective-permute-start.21) | collective-permute-done | bytes 32800 | tf_op jit(solution)/shard_map/ppermute | solution.py:440
  86.6 2.4 %collective-permute-done.22 = f32[64,128]{1,0:T(8,128)S(1)} collective-permute-done((f32[64,128]{1,0:T(8,128)S(1)}, f32[64,128]{1,0:T(8,128)S(1)}, u32[]{:S(2)}, u32[]{:S(2)}) %collective-permute-start.22) | collective-permute-done | bytes 32800 | tf_op jit(solution)/shard_map/ppermute | solution.py:440
  91.0 1.5 %collective-permute-start.25 = (f32[64,128]{1,0:T(8,128)S(1)}, f32[64,128]{1,0:T(8,128)S(1)}, u32[]{:S(2)}, u32[]{:S(2)}) collective-permute-start(f32[64,128]{1,0:T(8,128)S(1)} %add_add_fusion.1), channel_id=1, source_target_pairs={{0,24},{2,26},{4,28},{6,30},{8,16},{10,18},{12,20},{14,22},{16,8},... | collective-permute-start | bytes 98312 | tf_op jit(solution)/shard_map/ppermute | solution.py:440
  95.2 5.9 %collective-permute-done.27.arrived = f32[64,512]{1,0:T(8,128)S(1)} collective-permute-done((f32[64,512]{1,0:T(8,128)S(1)}, f32[64,512]{1,0:T(8,128)S(1)}, u32[]{:S(2)}, u32[]{:S(2)}) %collective-permute-start.27) | collective-permute-done | bytes 131104 | tf_op jit(solution)/shard_map/ppermute | solution.py:632
  101.5 5.9 %update.1 = (f32[32,512]{1,0:T(8,128)}, f32[32,512]{1,0:T(8,128)}) custom-call(f32[64,128]{1,0:T(8,128)S(1)} %add_add_fusion.own_sums, f32[64,128]{1,0:T(8,128)S(1)} %collective-permute-done.26.other_sums, f32[64,512]{1,0:T(8,128)S(1)} %get-tuple-element.143.r, f32[64,512]{1,0:T(8,128)S(1)} %get-tuple-element.144.d, f32[64,512]{1,0:T(8,128)S(1)} %get-tuple-element.145.q, ...), custom_call_target="tpu_custom_call" | custom-call | flops 5000000000 | tf_op jit(solution)/shard_map/update/pallas_call | solution.py:634
  (81 shorter events, 22.7 us)
Async XLA Ops:
  3.5 9.0 %collective-permute-start.2 = (f32[4,136,128]{2,1,0:T(8,128)}, f32[4,136,128]{2,1,0:T(8,128)S(1)}, u32[]{:S(2)}, u32[]{:S(2)}) collective-permute-start(f32[4,136,128]{2,1,0:T(8,128)} %get-tuple-element.78), channel_id=1, source_target_pairs={{0,8},{2,10},{4,12},{6,14},{8,0},{10,2},{12,4},{14,6},{1,9},{3,11}... | collective-permute-start | bytes 835592 | tf_op jit(solution)/shard_map/ppermute | solution.py:440
  4.0 8.5 %collective-permute-start.8 = (f32[4,136,128]{2,1,0:T(8,128)}, f32[4,136,128]{2,1,0:T(8,128)S(1)}, u32[]{:S(2)}, u32[]{:S(2)}) collective-permute-start(f32[4,136,128]{2,1,0:T(8,128)} %get-tuple-element.78), channel_id=1, source_target_pairs={{0,4},{2,6},{4,0},{6,2},{8,12},{10,14},{12,8},{14,10},{1,5},{3,7},... | collective-permute-start | bytes 835592 | tf_op jit(solution)/shard_map/ppermute | solution.py:440
  4.5 10.7 %collective-permute-start.1 = (f32[4,136,128]{2,1,0:T(8,128)}, f32[4,136,128]{2,1,0:T(8,128)S(1)}, u32[]{:S(2)}, u32[]{:S(2)}) collective-permute-start(f32[4,136,128]{2,1,0:T(8,128)} %get-tuple-element.78), channel_id=1, source_target_pairs={{0,2},{2,0},{4,6},{6,4},{8,10},{10,8},{12,14},{14,12},{1,3},{3,1},... | collective-permute-start | bytes 835592 | tf_op jit(solution)/shard_map/ppermute | solution.py:440
  5.3 9.9 %all-to-all-start = ((f32[8,4,512]{2,1,0:T(4,128)}), f32[8,4,512]{2,1,0:T(4,128)S(1)}, u32[]{:S(2)}, u32[]{:S(2)}) async-start(f32[8,4,512]{2,1,0:T(4,128)} %reshape.7), calls=%async_computation | async-start | bytes 131072 | tf_op jit(solution)/shard_map/all_to_all | solution.py:509
  12.5 7.4 %collective-permute-start.9 = (f32[4,128,128]{2,1,0:T(8,128)S(1)}, f32[4,128,128]{2,1,0:T(8,128)S(1)}, u32[]{:S(2)}, u32[]{:S(2)}) collective-permute-start(f32[4,128,128]{2,1,0:T(8,128)S(1)} %pad_maximum_fusion.2), channel_id=1, source_target_pairs={{0,2},{2,0},{4,6},{6,4},{8,10},{10,8},{12,14},{14,12},{1,3},{3,1},... | collective-permute-start | bytes 786440 | tf_op jit(solution)/shard_map/ppermute | solution.py:440
  15.3 9.2 %collective-permute-start.3 = (f32[4,136,128]{2,1,0:T(8,128)S(1)}, f32[4,136,128]{2,1,0:T(8,128)S(1)}, u32[]{:S(2)}, u32[]{:S(2)}) collective-permute-start(f32[4,136,128]{2,1,0:T(8,128)S(1)} %pad_maximum_fusion.1), channel_id=1, source_target_pairs={{0,4},{2,6},{4,0},{6,2},{8,12},{10,14},{12,8},{14,10},{1,5},{3,7},... | collective-permute-start | bytes 835592 | tf_op jit(solution)/shard_map/ppermute | solution.py:440
  16.7 10.5 %collective-permute-start.12 = (f32[4,144,128]{2,1,0:T(8,128)S(1)}, f32[4,144,128]{2,1,0:T(8,128)S(1)}, u32[]{:S(2)}, u32[]{:S(2)}) collective-permute-start(f32[4,144,128]{2,1,0:T(8,128)S(1)} %pad_maximum_fusion), channel_id=1, source_target_pairs={{0,8},{2,10},{4,12},{6,14},{8,0},{10,2},{12,4},{14,6},{1,9},{3,11}... | collective-permute-start | bytes 884744 | tf_op jit(solution)/shard_map/ppermute | solution.py:440
  18.2 7.0 %collective-permute-start.15 = (f32[4,136,128]{2,1,0:T(8,128)S(1)}, f32[4,136,128]{2,1,0:T(8,128)S(1)}, u32[]{:S(2)}, u32[]{:S(2)}) collective-permute-start(f32[4,136,128]{2,1,0:T(8,128)S(1)} %collective-permute-done.8.refs_3_), channel_id=1, source_target_pairs={{0,1},{1,0},{2,3},{3,2},{4,5},{5,4},{6,7},{7,6},{8,9},{9,8},{10,11... | collective-permute-start | bytes 835592 | tf_op jit(solution)/shard_map/ppermute | solution.py:440
  18.2 8.4 %collective-permute-start.14 = (f32[4,136,128]{2,1,0:T(8,128)S(1)}, f32[4,136,128]{2,1,0:T(8,128)S(1)}, u32[]{:S(2)}, u32[]{:S(2)}) collective-permute-start(f32[4,136,128]{2,1,0:T(8,128)S(1)} %collective-permute-done.1.refs_1_), channel_id=1, source_target_pairs={{0,1},{1,0},{2,3},{3,2},{4,5},{5,4},{6,7},{7,6},{8,9},{9,8},{10,11... | collective-permute-start | bytes 835592 | tf_op jit(solution)/shard_map/ppermute | solution.py:440
  19.9 7.3 %collective-permute-start.16 = (f32[4,136,128]{2,1,0:T(8,128)S(1)}, f32[4,136,128]{2,1,0:T(8,128)S(1)}, u32[]{:S(2)}, u32[]{:S(2)}) collective-permute-start(f32[4,136,128]{2,1,0:T(8,128)S(1)} %collective-permute-done.2.refs_5_), channel_id=1, source_target_pairs={{0,1},{1,0},{2,3},{3,2},{4,5},{5,4},{6,7},{7,6},{8,9},{9,8},{10,11... | collective-permute-start | bytes 835592 | tf_op jit(solution)/shard_map/ppermute | solution.py:440
  24.5 9.9 %collective-permute-start.10 = (f32[4,128,128]{2,1,0:T(8,128)S(1)}, f32[4,128,128]{2,1,0:T(8,128)S(1)}, u32[]{:S(2)}, u32[]{:S(2)}) collective-permute-start(f32[4,128,128]{2,1,0:T(8,128)S(1)} %collective-permute-done.9.refs_1_), channel_id=1, source_target_pairs={{0,1},{1,0},{2,3},{3,2},{4,5},{5,4},{6,7},{7,6},{8,9},{9,8},{10,11... | collective-permute-start | bytes 786440 | tf_op jit(solution)/shard_map/ppermute | solution.py:440
  25.1 8.9 %collective-permute-start.6 = (f32[4,72,128]{2,1,0:T(8,128)S(1)}, f32[4,72,128]{2,1,0:T(8,128)S(1)}, u32[]{:S(2)}, u32[]{:S(2)}) collective-permute-start(f32[4,72,128]{2,1,0:T(8,128)S(1)} %slice.29), channel_id=1, source_target_pairs={{0,8},{2,10},{4,12},{6,14},{8,0},{10,2},{12,4},{14,6},{1,9},{3,11}... | collective-permute-start | bytes 442376 | tf_op jit(solution)/shard_map/ppermute | solution.py:440
  26.6 7.3 %collective-permute-start.4 = (f32[4,64,128]{2,1,0:T(8,128)S(1)}, f32[4,64,128]{2,1,0:T(8,128)S(1)}, u32[]{:S(2)}, u32[]{:S(2)}) collective-permute-start(f32[4,64,128]{2,1,0:T(8,128)S(1)} %slice.28), channel_id=1, source_target_pairs={{0,2},{2,0},{4,6},{6,4},{8,10},{10,8},{12,14},{14,12},{1,3},{3,1},... | collective-permute-start | bytes 393224 | tf_op jit(solution)/shard_map/ppermute | solution.py:440
  27.2 7.4 %collective-permute-start.11 = (f32[4,136,128]{2,1,0:T(8,128)S(1)}, f32[4,136,128]{2,1,0:T(8,128)S(1)}, u32[]{:S(2)}, u32[]{:S(2)}) collective-permute-start(f32[4,136,128]{2,1,0:T(8,128)S(1)} %collective-permute-done.3.refs_3_), channel_id=1, source_target_pairs={{0,1},{1,0},{2,3},{3,2},{4,5},{5,4},{6,7},{7,6},{8,9},{9,8},{10,11... | collective-permute-start | bytes 835592 | tf_op jit(solution)/shard_map/ppermute | solution.py:440
  27.2 7.3 %collective-permute-start.13 = (f32[4,144,128]{2,1,0:T(8,128)S(1)}, f32[4,144,128]{2,1,0:T(8,128)S(1)}, u32[]{:S(2)}, u32[]{:S(2)}) collective-permute-start(f32[4,144,128]{2,1,0:T(8,128)S(1)} %collective-permute-done.12.refs_5_), channel_id=1, source_target_pairs={{0,1},{1,0},{2,3},{3,2},{4,5},{5,4},{6,7},{7,6},{8,9},{9,8},{10,11... | collective-permute-start | bytes 884744 | tf_op jit(solution)/shard_map/ppermute | solution.py:440
  33.9 45.8 %collective-permute-start = (f32[32,512]{1,0:T(8,128)S(1)}, f32[32,512]{1,0:T(8,128)S(1)}, u32[]{:S(2)}, u32[]{:S(2)}) collective-permute-start(f32[32,512]{1,0:T(8,128)S(1)} %copy-done), channel_id=1, source_target_pairs={{0,1},{1,0},{2,3},{3,2},{4,5},{5,4},{6,7},{7,6},{8,9},{9,8},{10,11... | collective-permute-start | bytes 196616 | tf_op jit(solution)/shard_map/ppermute | solution.py:440
  34.0 6.7 %collective-permute-start.5 = (f32[4,64,128]{2,1,0:T(8,128)S(1)}, f32[4,64,128]{2,1,0:T(8,128)S(1)}, u32[]{:S(2)}, u32[]{:S(2)}) collective-permute-start(f32[4,64,128]{2,1,0:T(8,128)S(1)} %collective-permute-done.4.refs_1_), channel_id=1, source_target_pairs={{0,1},{1,0},{2,3},{3,2},{4,5},{5,4},{6,7},{7,6},{8,9},{9,8},{10,11... | collective-permute-start | bytes 393224 | tf_op jit(solution)/shard_map/ppermute | solution.py:440
  34.5 6.3 %collective-permute-start.7 = (f32[4,72,128]{2,1,0:T(8,128)S(1)}, f32[4,72,128]{2,1,0:T(8,128)S(1)}, u32[]{:S(2)}, u32[]{:S(2)}) collective-permute-start(f32[4,72,128]{2,1,0:T(8,128)S(1)} %collective-permute-done.6.refs_3_), channel_id=1, source_target_pairs={{0,1},{1,0},{2,3},{3,2},{4,5},{5,4},{6,7},{7,6},{8,9},{9,8},{10,11... | collective-permute-start | bytes 442376 | tf_op jit(solution)/shard_map/ppermute | solution.py:440
  51.7 4.9 %collective-permute-start.17 = (f32[3,4,512]{2,1,0:T(4,128)S(1)}, f32[3,4,512]{2,1,0:T(4,128)S(1)}, u32[]{:S(2)}, u32[]{:S(2)}) collective-permute-start(f32[3,4,512]{2,1,0:T(4,128)S(1)} %get-tuple-element.122), channel_id=1, source_target_pairs={{0,16},{16,0},{1,17},{17,1},{2,18},{18,2},{3,19},{19,3},{4,20},{20... | collective-permute-start | bytes 73736 | tf_op jit(solution)/shard_map/ppermute | solution.py:460
  60.8 6.9 %collective-permute-start.18 = (f32[4,512]{1,0:T(4,128)S(1)}, f32[4,512]{1,0:T(4,128)S(1)}, u32[]{:S(2)}, u32[]{:S(2)}) collective-permute-start(f32[4,512]{1,0:T(4,128)S(1)} %get-tuple-element.130.refs_1_), channel_id=1, source_target_pairs={{0,16},{16,0},{1,17},{17,1},{2,18},{18,2},{3,19},{19,3},{4,20},{20... | collective-permute-start | bytes 24584 | tf_op jit(solution)/shard_map/ppermute | solution.py:460
  68.4 9.5 %all-to-all-start.1 = ((f32[8,2,3,4,512]{4,3,2,1,0:T(4,128)}), f32[8,2,3,4,512]{4,3,2,1,0:T(4,128)S(1)}, u32[]{:S(2)}, u32[]{:S(2)}) async-start(f32[8,2,3,4,512]{4,3,2,1,0:T(4,128)} %halo.1), calls=%async_computation.1 | async-start | bytes 786432 | tf_op jit(solution)/shard_map/all_to_all | solution.py:619
  88.9 4.8 %collective-permute-start.23 = (f32[64,128]{1,0:T(8,128)S(1)}, f32[64,128]{1,0:T(8,128)S(1)}, u32[]{:S(2)}, u32[]{:S(2)}) collective-permute-start(f32[64,128]{1,0:T(8,128)S(1)} %add_add_fusion.1), channel_id=1, source_target_pairs={{0,8},{2,10},{4,12},{6,14},{8,0},{10,2},{12,4},{14,6},{16,24},{18,... | collective-permute-start | bytes 98312 | tf_op jit(solution)/shard_map/ppermute | solution.py:440
  92.5 8.6 %collective-permute-start.27 = (f32[64,512]{1,0:T(8,128)S(1)}, f32[64,512]{1,0:T(8,128)S(1)}, u32[]{:S(2)}, u32[]{:S(2)}) collective-permute-start(f32[64,512]{1,0:T(8,128)S(1)} %get-tuple-element.146.e), channel_id=1, source_target_pairs={{16,14},{17,15}} | collective-permute-start | bytes 393224 | tf_op jit(solution)/shard_map/ppermute | solution.py:632
  95.1 6.3 %collective-permute-start.26 = (f32[64,128]{1,0:T(8,128)S(1)}, f32[64,128]{1,0:T(8,128)S(1)}, u32[]{:S(2)}, u32[]{:S(2)}) collective-permute-start(f32[64,128]{1,0:T(8,128)S(1)} %add_add_fusion.own_sums), channel_id=1, source_target_pairs={{0,1},{1,0},{2,3},{3,2},{4,5},{5,4},{6,7},{7,6},{8,9},{9,8},{10,11... | collective-permute-start | bytes 98312 | tf_op jit(solution)/shard_map/ppermute | solution.py:440
  (14 other events, 45.2 us)

commit v6 on v5

--- a/solution.py
+++ b/solution.py
@@ -349,7 +349,7 @@
 
 def products_kernel(n, *refs):
     r_pieces, pieces, bands = refs[:n], refs[n : 2 * n], refs[2 * n : 2 * n + 4]
-    r, d, q, e, w, sums, wide = refs[2 * n + 4 :]
+    r, d, q, e, w, under, sums, wide = refs[2 * n + 4 :]
     rhs, cells, total = lax.axis_index("rhs"), pieces[0].shape[4], r.shape[0]
     for t in range(n):
         place_rows(r, t, rhs, r_pieces[t][...])
@@ -365,15 +365,11 @@
     own = slice(cells, 2 * cells)
     d[...], e[...] = wide[:total, own], wide[total:, own]
     q[...], w[...] = image[:total], image[total:]
+    under[...] = wide[total:, :cells]
     odd = rhs % 2 == 1
     left = jnp.where(odd, e[...], d[...])
     rights = jnp.where(odd, q[...], r[...]), jnp.where(odd, w[...] + below_e, q[...])
     sums[...] = jnp.concatenate([inner(left, right) for right in rights], axis=1)
-
-
-def complete_kernel(value, arrived, *refs):
-    cells = value.shape[1]
-    refs[4][...] = value[...] + along(arrived[...], refs[:4], 2 * cells, 3 * cells)
 
 
 def small(a, b):
@@ -417,7 +413,8 @@
     return 0.5 * (a + a.T)
 
 
-def last_kernel(own_sums, other_sums, r, d, q, e, w, solution, residual, all_weights):
+def last_kernel(own_sums, other_sums, r, d, q, e, w, arrived, *refs):
+    bands, (solution, residual, all_weights) = refs[:4], refs[4:]
     count, total = solution.shape[0], r.shape[0]
     rhs = lax.axis_index("rhs")
     odd = rhs % 2 == 1
@@ -433,7 +430,9 @@
     weights = all_weights[pl.ds(pl.multiple_of(rhs * count, count), count), :]
     own = r[pl.ds(pl.multiple_of(rhs * count, count), count), :]
     solution[...] = small(weights, jnp.concatenate([d[...], e[...]], axis=0))
-    residual[...] = own - small(weights, jnp.concatenate([q[...], w[...]], axis=0))
+    cells, last = own.shape[1], lax.axis_index("pos") == SPAN - 1
+    above = along(arrived[...] * jnp.where(last, 1.0, 0.0), bands, 2 * cells, 3 * cells)
+    residual[...] = own - small(weights, jnp.concatenate([q[...], w[...] + above], axis=0))
 
 
 def swapped(value, axis, bit):
@@ -479,7 +478,7 @@
     each = count // SPAN
     total = count * parts
     S = jax.ShapeDtypeStruct
-    down_rows = [(SPAN * (i + 1), SPAN * (i + 1) - 1) for i in range(blocks - 1)]
+    edges = [(SPAN * i - 1, SPAN * i + 1) for i in range(1, blocks)]
 
     def others(value):
         return [value] + [swapped(value, "rhs", t) for t in range(1, parts)]
@@ -619,27 +618,26 @@
     rows = lax.all_to_all(rows, "pos", 0, 0, tiled=True)
 
     full, sums_shape = S((total, cells), F32), S((total, 2 * total), F32)
-    r_full, d, q, e, w_part, sums = call(
+    r_full, d, q, e, w, under, sums = call(
         functools.partial(products_kernel, parts),
         "products",
-        [full] * 5 + [sums_shape],
+        [full] * 6 + [sums_shape],
         [VMEM] * (2 * parts + 4),
-        [VMEM] * 6,
+        [VMEM] * 7,
         [pltpu.VMEM((2 * total, 3 * cells), F32)],
         cost=2,
     )(*r_pieces, *others(rows), *bands)
     sums = summed(sums)
-    e_above = lax.ppermute(e, ("blk", "pos"), down_rows)
-    w = call(complete_kernel, "complete", full, [VMEM] * 6)(w_part, e_above, *bands)
+    e_above = lax.ppermute(under, ("blk", "pos"), edges + [(b, a) for a, b in edges])
     return call(
         last_kernel,
         "update",
         [S((count, cells), F32)] * 2,
-        [VMEM] * 7,
+        [VMEM] * 12,
         [VMEM] * 2,
         [pltpu.VMEM((total, 2 * total), F32)],
-        cost=5,
-    )(sums, swapped(sums, "rhs", 1), r_full, d, q, e, w)
+        cost=4,
+    )(sums, swapped(sums, "rhs", 1), r_full, d, q, e, w, e_above, *bands)
 
 
 def solution(mesh):

time: 108 us -> 107 us (level)
  waiting for transfers between devices: 15.8 us -> 13.8 us
  starting transfers between devices: 34.9 us -> 36.1 us
    ppermute x1, waiting for transfers between devices: 5.94 us -> 3.85 us  [shards(): lax.ppermute(under, ('blk', 'pos'), edges + [(b, a) for a, b in edges])]
    ppermute x1, starting transfers between devices: 1.28 us -> 2.42 us  [shards(): lax.ppermute(under, ('blk', 'pos'), edges + [(b, a) for a, b in edges])]
    pallas_call x3 -> x2, Pallas kernels: 7.6 us -> 7.65 us  [the longest x1 6.22 us: shards(): call(last_kernel, 'update', [S((count, cells), F32)] * 2, [VMEM] * 12, [V...]
where the time goes in v6:
time: 107 us; the launch traced here: 106 us
  Pallas kernels  52.4 us (49%)
  starting transfers between devices  36.1 us (34%)
  waiting for transfers between devices  13.8 us (13%)
  local copies, waits for them, and re-layouts  3.17 us (3%)
    pallas_call x8, Pallas kernels, with_mats(): call(body, name, [*out_shapes, *mat_shapes], [*specs, *[VMEM] * 6], [VMEM...  33.8 us
    ppermute x25, starting transfers between devices, swapped(): lax.ppermute(value, axis, [(i, i ^ bit) for i in range(lax.axis_size(axis...  16.1 us
    all_to_all x1, starting transfers between devices, shards(): lax.all_to_all(right_side.reshape(SPAN, each, cells), 'pos', 0, 0, tiled=...  7.13 us
    ppermute x25, waiting for transfers between devices, swapped(): lax.ppermute(value, axis, [(i, i ^ bit) for i in range(lax.axis_size(axis...  6.88 us
    pallas_call x1, Pallas kernels, shards(): call(last_kernel, 'update', [S((count, cells), F32)] * 2, [VMEM] * 12, [V...  6.22 us
    ppermute x2, starting transfers between devices, exchanged(): got.append(lax.ppermute(value, 'blk', pairs + [(b, a) for a, b in pairs]))  5.32 us
    all_to_all x1, starting transfers between devices, shards(): rows = lax.all_to_all(rows, 'pos', 0, 0, tiled=True)  5.1 us
    pallas_call x1, Pallas kernels, shards(): call(own_factor_kernel, 'factors_own', mat_shapes, [SMEM, VMEM], [VMEM] *...  3.98 us
  transfers between devices with their start and end apart: 30, of which 9 were waited for; matrix products, arithmetic and copies ran while one was open for 1% of the time, Pallas kernels for 39%

profile of v6, /device:TPU:14, one launch (start us, length us, event | category | flops | bytes accessed | tf_op | source)
XLA Modules:
  0.0 106.5 jit_solution(17817920776710970144)
XLA Ops:
  0.6 2.8 %pack_tiles.1 = (f32[8,136,128]{2,1,0:T(8,128)S(1)}, f32[4,136,128]{2,1,0:T(8,128)}, s32[1,3]{1,0:T(1,128)}) custom-call(s32[8,7]{1,0:T(8,128)} %columns.3, f32[8,7,64,64]{3,2,1,0:T(8,128)} %tiles.3, f32[8,64,64]{2,1,0:T(8,128)} %pivots_far.1), custom_call_target="tpu_custom_call" | custom-call | flops 2000000000 | tf_op jit(solution)/shard_map/pack_tiles/pallas_call | solution.py:487
  5.3 7.1 %all-to-all-start = ((f32[8,4,512]{2,1,0:T(4,128)}), f32[8,4,512]{2,1,0:T(4,128)S(1)}, u32[]{:S(2)}, u32[]{:S(2)}) async-start(f32[8,4,512]{2,1,0:T(4,128)} %reshape.7), calls=%async_computation | async-start | bytes 131072 | tf_op jit(solution)/shard_map/all_to_all | solution.py:508
  13.1 2.1 %all-to-all-done.refs_0_ = f32[8,4,512]{2,1,0:T(4,128)S(1)} async-done(((f32[8,4,512]{2,1,0:T(4,128)}), f32[8,4,512]{2,1,0:T(4,128)S(1)}, u32[]{:S(2)}, u32[]{:S(2)}) %all-to-all-start) | async-done | bytes 65568 | tf_op jit(solution)/shard_map/all_to_all | solution.py:508
  20.5 4.0 %factors_own.1 = (bf16[8,2,512,512]{3,2,1,0:T(8,128)(2,1)S(1)}, bf16[8,2,512,512]{3,2,1,0:T(8,128)(2,1)S(1)}, bf16[8,512,512]{2,1,0:T(8,128)(2,1)S(1)}, bf16[8,5...) custom-call(s32[1,3]{1,0:T(1,128)S(1)} %copy-done.1, ...), custom_call_target="tpu_custom_call" | custom-call | flops 4000000000 | tf_op jit(solution)/shard_map/factors_own/pallas_call | solution.py:532
  27.7 6.1 %factors_near.1 = (bf16[8,2,512,512]{3,2,1,0:T(8,128)(2,1)S(1)}, bf16[8,2,512,512]{3,2,1,0:T(8,128)(2,1)S(1)}, bf16[8,512,512]{2,1,0:T(8,128)(2,1)S(1)}, bf16[8,...) custom-call(s32[1,3]{1,0:T(1,128)S(1)} %copy-done.1, ...), custom_call_target="tpu_custom_call", output_to_operand_aliasing={{0}: (7, {}), {1}: (8, {}), {2}: (9, {}), {3}: (10, {}), {4... | custom-call | flops 6000000000 | tf_op jit(solution)/shard_map/factors_near/pallas_call | solution.py:549
  34.6 6.1 %factors_mid.1 = (bf16[8,2,512,512]{3,2,1,0:T(8,128)(2,1)S(1)}, bf16[8,2,512,512]{3,2,1,0:T(8,128)(2,1)S(1)}, bf16[8,512,512]{2,1,0:T(8,128)(2,1)S(1)}, bf16[8,5...) custom-call(s32[1,3]{1,0:T(1,128)S(1)} %copy-done.1, ...), custom_call_target="tpu_custom_call", output_to_operand_aliasing={{0}: (7, {}), {1}: (8, {}), {2}: (9, {}), {3}: (10, {}), {4... | custom-call | flops 6000000000 | tf_op jit(solution)/shard_map/factors_mid/pallas_call | solution.py:549
  40.7 2.7 %factors_far.1 = (bf16[8,2,512,512]{3,2,1,0:T(8,128)(2,1)S(1)}, bf16[8,2,512,512]{3,2,1,0:T(8,128)(2,1)S(1)}, bf16[8,512,512]{2,1,0:T(8,128)(2,1)S(1)}, bf16[8,5...) custom-call(s32[1,3]{1,0:T(1,128)S(1)} %copy-done.1, ...), custom_call_target="tpu_custom_call", output_to_operand_aliasing={{0}: (5, {}), {1}: (6, {}), {2}: (7, {}), {3}: (8, {}), {4}... | custom-call | flops 3000000000 | tf_op jit(solution)/shard_map/factors_far/pallas_call | solution.py:549
  43.5 4.1 %forward_r.1 = (f32[8,4,512]{2,1,0:T(4,128)S(1)}, f32[2,4,512]{2,1,0:T(4,128)S(1)}, bf16[8,2,512,512]{3,2,1,0:T(8,128)(2,1)S(1)}, bf16[8,2,512,512]{3,2,1,0:T(8,...) custom-call(f32[8,4,512]{2,1,0:T(4,128)S(1)} %all-to-all-done.refs_0, ...), custom_call_target="tpu_custom_call", output_to_operand_aliasing={{2}: (1, {}), {3}: (2, {}), {4}: (3, {}), {5}: (4, {}), {6}... | custom-call | flops 4000000000 | tf_op jit(solution)/shard_map/forward_r/pallas_call | solution.py:549
  47.6 4.1 %backward_r.1 = (f32[8,4,512]{2,1,0:T(4,128)S(1)}, f32[8,4,512]{2,1,0:T(4,128)S(1)}, f32[3,4,512]{2,1,0:T(4,128)S(1)}, bf16[8,2,512,512]{3,2,1,0:T(8,128)(2,1)S(...) custom-call(f32[8,4,512]{2,1,0:T(4,128)S(1)} %get-tuple-element.105., ...), custom_call_target="tpu_custom_call", output_to_operand_aliasing={{3}: (2, {}), {4}: (3, {}), {5}: (4, {}), {6}: (5, {}), {7}... | custom-call | flops 4000000000 | tf_op jit(solution)/shard_map/backward_r/pallas_call | solution.py:549
  51.7 2.6 %collective-permute-start.17 = (f32[3,4,512]{2,1,0:T(4,128)S(1)}, f32[3,4,512]{2,1,0:T(4,128)S(1)}, u32[]{:S(2)}, u32[]{:S(2)}) collective-permute-start(f32[3,4,512]{2,1,0:T(4,128)S(1)} %get-tuple-element.123), channel_id=1, source_target_pairs={{0,16},{16,0},{1,17},{17,1},{2,18},{18,2},{3,19},{19,3},{4,20},{20... | collective-permute-start | bytes 73736 | tf_op jit(solution)/shard_map/ppermute | solution.py:459
  54.4 2.3 %residue_of_z.1 = (f32[8,4,512]{2,1,0:T(4,128)S(1)}, f32[8,4,512]{2,1,0:T(4,128)S(1)}, bf16[8,2,512,512]{3,2,1,0:T(8,128)(2,1)S(1)}, bf16[8,2,512,512]{3,2,1,0:T...) custom-call(f32[8,4,512]{2,1,0:T(4,128)S(1)} %all-to-all-done.refs_0, ...), custom_call_target="tpu_custom_call", output_to_operand_aliasing={{2}: (4, {}), {3}: (5, {}), {4}: (6, {}), {5}: (7, {}), {6}... | custom-call | flops 2000000000 | tf_op jit(solution)/shard_map/residue_of_z/pallas_call | solution.py:549
  56.7 4.1 %forward_v.1 = (f32[8,4,512]{2,1,0:T(4,128)S(1)}, f32[4,512]{1,0:T(4,128)S(1)}, bf16[8,2,512,512]{3,2,1,0:T(8,128)(2,1)S(1)}, bf16[8,2,512,512]{3,2,1,0:T(8,128)...) custom-call(f32[8,4,512]{2,1,0:T(4,128)S(1)} %get-tuple-element.121., ...), custom_call_target="tpu_custom_call", output_to_operand_aliasing={{2}: (4, {}), {3}: (5, {}), {4}: (6, {}), {5}: (7, {}), {6}... | custom-call | flops 4000000000 | tf_op jit(solution)/shard_map/forward_v/pallas_call | solution.py:549
  60.8 2.7 %collective-permute-start.18 = (f32[4,512]{1,0:T(4,128)S(1)}, f32[4,512]{1,0:T(4,128)S(1)}, u32[]{:S(2)}, u32[]{:S(2)}) collective-permute-start(f32[4,512]{1,0:T(4,128)S(1)} %get-tuple-element.131.refs_1_), channel_id=1, source_target_pairs={{0,16},{16,0},{1,17},{17,1},{2,18},{18,2},{3,19},{19,3},{4,20},{20... | collective-permute-start | bytes 24584 | tf_op jit(solution)/shard_map/ppermute | solution.py:459
  63.5 4.1 %backward_v.1 = (f32[8,2,3,4,512]{4,3,2,1,0:T(4,128)S(1)}, bf16[8,2,512,512]{3,2,1,0:T(8,128)(2,1)S(1)}, bf16[8,2,512,512]{3,2,1,0:T(8,128)(2,1)S(1)}, bf16[8,51...) custom-call(f32[8,4,512]{2,1,0:T(4,128)S(1)} %get-tuple-element.130., ...), custom_call_target="tpu_custom_call", output_to_operand_aliasing={{1}: (5, {}), {2}: (6, {}), {3}: (7, {}), {4}: (8, {}), {5}... | custom-call | flops 4000000000 | tf_op jit(solution)/shard_map/backward_v/pallas_call | solution.py:549
  68.4 5.1 %all-to-all-start.1 = ((f32[8,2,3,4,512]{4,3,2,1,0:T(4,128)}), f32[8,2,3,4,512]{4,3,2,1,0:T(4,128)S(1)}, u32[]{:S(2)}, u32[]{:S(2)}) async-start(f32[8,2,3,4,512]{4,3,2,1,0:T(4,128)} %halo.1), calls=%async_computation.1 | async-start | bytes 786432 | tf_op jit(solution)/shard_map/all_to_all | solution.py:618
  73.5 1.7 %row_band.2 = (bf16[1536,256]{1,0:T(8,128)(2,1)S(1)}, bf16[1536,256]{1,0:T(8,128)(2,1)S(1)}) custom-call(s32[8,7]{1,0:T(8,128)S(1)} %copy-done.3, f32[8,7,64,64]{3,2,1,0:T(8,128)S(1)} %copy-done.2), custom_call_target="tpu_custom_call" | custom-call | flops 20000000000 | tf_op jit(solution)/shard_map/row_band/pallas_call | solution.py:521
  78.0 1.7 %row_band.3 = (bf16[1536,256]{1,0:T(8,128)(2,1)S(1)}, bf16[1536,256]{1,0:T(8,128)(2,1)S(1)}) custom-call(s32[8,7]{1,0:T(8,128)S(1)} %copy-done.3, f32[8,7,64,64]{3,2,1,0:T(8,128)S(1)} %copy-done.2), custom_call_target="tpu_custom_call" | custom-call | flops 20000000000 | tf_op jit(solution)/shard_map/row_band/pallas_call | solution.py:521
  81.1 1.5 %collective-permute-start.20 = (f32[64,128]{1,0:T(8,128)S(1)}, f32[64,128]{1,0:T(8,128)S(1)}, u32[]{:S(2)}, u32[]{:S(2)}) collective-permute-start(f32[64,128]{1,0:T(8,128)S(1)} %get-tuple-element.143), channel_id=1, source_target_pairs={{0,2},{2,0},{4,6},{6,4},{8,10},{10,8},{12,14},{14,12},{16,18},{18,... | collective-permute-start | bytes 98312 | tf_op jit(solution)/shard_map/ppermute | solution.py:439
  82.7 1.5 %collective-permute-start.21 = (f32[64,128]{1,0:T(8,128)S(1)}, f32[64,128]{1,0:T(8,128)S(1)}, u32[]{:S(2)}, u32[]{:S(2)}) collective-permute-start(f32[64,128]{1,0:T(8,128)S(1)} %get-tuple-element.143), channel_id=1, source_target_pairs={{0,4},{2,6},{4,0},{6,2},{8,12},{10,14},{12,8},{14,10},{16,20},{18,... | collective-permute-start | bytes 98312 | tf_op jit(solution)/shard_map/ppermute | solution.py:439
  86.6 2.4 %collective-permute-done.22 = f32[64,128]{1,0:T(8,128)S(1)} collective-permute-done((f32[64,128]{1,0:T(8,128)S(1)}, f32[64,128]{1,0:T(8,128)S(1)}, u32[]{:S(2)}, u32[]{:S(2)}) %collective-permute-start.22) | collective-permute-done | bytes 32800 | tf_op jit(solution)/shard_map/ppermute | solution.py:439
  91.0 1.5 %collective-permute-start.25 = (f32[64,128]{1,0:T(8,128)S(1)}, f32[64,128]{1,0:T(8,128)S(1)}, u32[]{:S(2)}, u32[]{:S(2)}) collective-permute-start(f32[64,128]{1,0:T(8,128)S(1)} %add_add_fusion.1), channel_id=1, source_target_pairs={{0,24},{2,26},{4,28},{6,30},{8,16},{10,18},{12,20},{14,22},{16,8},... | collective-permute-start | bytes 98312 | tf_op jit(solution)/shard_map/ppermute | solution.py:439
  92.5 2.4 %collective-permute-start.27 = (f32[64,512]{1,0:T(8,128)S(1)}, f32[64,512]{1,0:T(8,128)S(1)}, u32[]{:S(2)}, u32[]{:S(2)}) collective-permute-start(f32[64,512]{1,0:T(8,128)S(1)} %get-tuple-element.149), channel_id=1, source_target_pairs={{14,18},{18,14},{15,19},{19,15}} | collective-permute-start | bytes 393224 | tf_op jit(solution)/shard_map/ppermute | solution.py:631
  96.4 3.8 %collective-permute-done.27.arrived = f32[64,512]{1,0:T(8,128)S(1)} collective-permute-done((f32[64,512]{1,0:T(8,128)S(1)}, f32[64,512]{1,0:T(8,128)S(1)}, u32[]{:S(2)}, u32[]{:S(2)}) %collective-permute-start.27) | collective-permute-done | bytes 131104 | tf_op jit(solution)/shard_map/ppermute | solution.py:631
  100.2 6.2 %update.1 = (f32[32,512]{1,0:T(8,128)}, f32[32,512]{1,0:T(8,128)}) custom-call(f32[64,128]{1,0:T(8,128)S(1)} %add_add_fusion.own_sums, f32[64,128]{1,0:T(8,128)S(1)} %collective-permute-done.26.other_sums, f32[64,512]{1,0:T(8,128)S(1)} %get-tuple-element.144.r, f32[64,512]{1,0:T(8,128)S(1)} %get-tuple-element.145.d, f32[64,512]{1,0:T(8,128)S(1)} %get-tuple-element.146.q, ...), custom_call_target="tpu_custom_call" | custom-call | flops 4000000000 | tf_op jit(solution)/shard_map/update/pallas_call | solution.py:632
  (80 shorter events, 22.6 us)
Async XLA Ops:
  3.5 9.0 %collective-permute-start.2 = (f32[4,136,128]{2,1,0:T(8,128)}, f32[4,136,128]{2,1,0:T(8,128)S(1)}, u32[]{:S(2)}, u32[]{:S(2)}) collective-permute-start(f32[4,136,128]{2,1,0:T(8,128)} %get-tuple-element.79), channel_id=1, source_target_pairs={{0,8},{2,10},{4,12},{6,14},{8,0},{10,2},{12,4},{14,6},{1,9},{3,11}... | collective-permute-start | bytes 835592 | tf_op jit(solution)/shard_map/ppermute | solution.py:439
  4.0 8.5 %collective-permute-start.8 = (f32[4,136,128]{2,1,0:T(8,128)}, f32[4,136,128]{2,1,0:T(8,128)S(1)}, u32[]{:S(2)}, u32[]{:S(2)}) collective-permute-start(f32[4,136,128]{2,1,0:T(8,128)} %get-tuple-element.79), channel_id=1, source_target_pairs={{0,4},{2,6},{4,0},{6,2},{8,12},{10,14},{12,8},{14,10},{1,5},{3,7},... | collective-permute-start | bytes 835592 | tf_op jit(solution)/shard_map/ppermute | solution.py:439
  4.5 10.7 %collective-permute-start.1 = (f32[4,136,128]{2,1,0:T(8,128)}, f32[4,136,128]{2,1,0:T(8,128)S(1)}, u32[]{:S(2)}, u32[]{:S(2)}) collective-permute-start(f32[4,136,128]{2,1,0:T(8,128)} %get-tuple-element.79), channel_id=1, source_target_pairs={{0,2},{2,0},{4,6},{6,4},{8,10},{10,8},{12,14},{14,12},{1,3},{3,1},... | collective-permute-start | bytes 835592 | tf_op jit(solution)/shard_map/ppermute | solution.py:439
  5.3 9.9 %all-to-all-start = ((f32[8,4,512]{2,1,0:T(4,128)}), f32[8,4,512]{2,1,0:T(4,128)S(1)}, u32[]{:S(2)}, u32[]{:S(2)}) async-start(f32[8,4,512]{2,1,0:T(4,128)} %reshape.7), calls=%async_computation | async-start | bytes 131072 | tf_op jit(solution)/shard_map/all_to_all | solution.py:508
  12.5 7.4 %collective-permute-start.9 = (f32[4,128,128]{2,1,0:T(8,128)S(1)}, f32[4,128,128]{2,1,0:T(8,128)S(1)}, u32[]{:S(2)}, u32[]{:S(2)}) collective-permute-start(f32[4,128,128]{2,1,0:T(8,128)S(1)} %pad_maximum_fusion.2), channel_id=1, source_target_pairs={{0,2},{2,0},{4,6},{6,4},{8,10},{10,8},{12,14},{14,12},{1,3},{3,1},... | collective-permute-start | bytes 786440 | tf_op jit(solution)/shard_map/ppermute | solution.py:439
  15.3 9.2 %collective-permute-start.3 = (f32[4,136,128]{2,1,0:T(8,128)S(1)}, f32[4,136,128]{2,1,0:T(8,128)S(1)}, u32[]{:S(2)}, u32[]{:S(2)}) collective-permute-start(f32[4,136,128]{2,1,0:T(8,128)S(1)} %pad_maximum_fusion.1), channel_id=1, source_target_pairs={{0,4},{2,6},{4,0},{6,2},{8,12},{10,14},{12,8},{14,10},{1,5},{3,7},... | collective-permute-start | bytes 835592 | tf_op jit(solution)/shard_map/ppermute | solution.py:439
  16.7 10.5 %collective-permute-start.12 = (f32[4,144,128]{2,1,0:T(8,128)S(1)}, f32[4,144,128]{2,1,0:T(8,128)S(1)}, u32[]{:S(2)}, u32[]{:S(2)}) collective-permute-start(f32[4,144,128]{2,1,0:T(8,128)S(1)} %pad_maximum_fusion), channel_id=1, source_target_pairs={{0,8},{2,10},{4,12},{6,14},{8,0},{10,2},{12,4},{14,6},{1,9},{3,11}... | collective-permute-start | bytes 884744 | tf_op jit(solution)/shard_map/ppermute | solution.py:439
  18.2 7.0 %collective-permute-start.15 = (f32[4,136,128]{2,1,0:T(8,128)S(1)}, f32[4,136,128]{2,1,0:T(8,128)S(1)}, u32[]{:S(2)}, u32[]{:S(2)}) collective-permute-start(f32[4,136,128]{2,1,0:T(8,128)S(1)} %collective-permute-done.8.refs_3_), channel_id=1, source_target_pairs={{0,1},{1,0},{2,3},{3,2},{4,5},{5,4},{6,7},{7,6},{8,9},{9,8},{10,11... | collective-permute-start | bytes 835592 | tf_op jit(solution)/shard_map/ppermute | solution.py:439
  18.2 8.4 %collective-permute-start.14 = (f32[4,136,128]{2,1,0:T(8,128)S(1)}, f32[4,136,128]{2,1,0:T(8,128)S(1)}, u32[]{:S(2)}, u32[]{:S(2)}) collective-permute-start(f32[4,136,128]{2,1,0:T(8,128)S(1)} %collective-permute-done.1.refs_1_), channel_id=1, source_target_pairs={{0,1},{1,0},{2,3},{3,2},{4,5},{5,4},{6,7},{7,6},{8,9},{9,8},{10,11... | collective-permute-start | bytes 835592 | tf_op jit(solution)/shard_map/ppermute | solution.py:439
  19.9 7.3 %collective-permute-start.16 = (f32[4,136,128]{2,1,0:T(8,128)S(1)}, f32[4,136,128]{2,1,0:T(8,128)S(1)}, u32[]{:S(2)}, u32[]{:S(2)}) collective-permute-start(f32[4,136,128]{2,1,0:T(8,128)S(1)} %collective-permute-done.2.refs_5_), channel_id=1, source_target_pairs={{0,1},{1,0},{2,3},{3,2},{4,5},{5,4},{6,7},{7,6},{8,9},{9,8},{10,11... | collective-permute-start | bytes 835592 | tf_op jit(solution)/shard_map/ppermute | solution.py:439
  24.5 9.9 %collective-permute-start.10 = (f32[4,128,128]{2,1,0:T(8,128)S(1)}, f32[4,128,128]{2,1,0:T(8,128)S(1)}, u32[]{:S(2)}, u32[]{:S(2)}) collective-permute-start(f32[4,128,128]{2,1,0:T(8,128)S(1)} %collective-permute-done.9.refs_1_), channel_id=1, source_target_pairs={{0,1},{1,0},{2,3},{3,2},{4,5},{5,4},{6,7},{7,6},{8,9},{9,8},{10,11... | collective-permute-start | bytes 786440 | tf_op jit(solution)/shard_map/ppermute | solution.py:439
  25.1 8.9 %collective-permute-start.6 = (f32[4,72,128]{2,1,0:T(8,128)S(1)}, f32[4,72,128]{2,1,0:T(8,128)S(1)}, u32[]{:S(2)}, u32[]{:S(2)}) collective-permute-start(f32[4,72,128]{2,1,0:T(8,128)S(1)} %slice.29), channel_id=1, source_target_pairs={{0,8},{2,10},{4,12},{6,14},{8,0},{10,2},{12,4},{14,6},{1,9},{3,11}... | collective-permute-start | bytes 442376 | tf_op jit(solution)/shard_map/ppermute | solution.py:439
  26.6 7.3 %collective-permute-start.4 = (f32[4,64,128]{2,1,0:T(8,128)S(1)}, f32[4,64,128]{2,1,0:T(8,128)S(1)}, u32[]{:S(2)}, u32[]{:S(2)}) collective-permute-start(f32[4,64,128]{2,1,0:T(8,128)S(1)} %slice.28), channel_id=1, source_target_pairs={{0,2},{2,0},{4,6},{6,4},{8,10},{10,8},{12,14},{14,12},{1,3},{3,1},... | collective-permute-start | bytes 393224 | tf_op jit(solution)/shard_map/ppermute | solution.py:439
  27.2 7.4 %collective-permute-start.11 = (f32[4,136,128]{2,1,0:T(8,128)S(1)}, f32[4,136,128]{2,1,0:T(8,128)S(1)}, u32[]{:S(2)}, u32[]{:S(2)}) collective-permute-start(f32[4,136,128]{2,1,0:T(8,128)S(1)} %collective-permute-done.3.refs_3_), channel_id=1, source_target_pairs={{0,1},{1,0},{2,3},{3,2},{4,5},{5,4},{6,7},{7,6},{8,9},{9,8},{10,11... | collective-permute-start | bytes 835592 | tf_op jit(solution)/shard_map/ppermute | solution.py:439
  27.2 7.3 %collective-permute-start.13 = (f32[4,144,128]{2,1,0:T(8,128)S(1)}, f32[4,144,128]{2,1,0:T(8,128)S(1)}, u32[]{:S(2)}, u32[]{:S(2)}) collective-permute-start(f32[4,144,128]{2,1,0:T(8,128)S(1)} %collective-permute-done.12.refs_5_), channel_id=1, source_target_pairs={{0,1},{1,0},{2,3},{3,2},{4,5},{5,4},{6,7},{7,6},{8,9},{9,8},{10,11... | collective-permute-start | bytes 884744 | tf_op jit(solution)/shard_map/ppermute | solution.py:439
  33.9 45.8 %collective-permute-start = (f32[32,512]{1,0:T(8,128)S(1)}, f32[32,512]{1,0:T(8,128)S(1)}, u32[]{:S(2)}, u32[]{:S(2)}) collective-permute-start(f32[32,512]{1,0:T(8,128)S(1)} %copy-done), channel_id=1, source_target_pairs={{0,1},{1,0},{2,3},{3,2},{4,5},{5,4},{6,7},{7,6},{8,9},{9,8},{10,11... | collective-permute-start | bytes 196616 | tf_op jit(solution)/shard_map/ppermute | solution.py:439
  34.0 6.7 %collective-permute-start.5 = (f32[4,64,128]{2,1,0:T(8,128)S(1)}, f32[4,64,128]{2,1,0:T(8,128)S(1)}, u32[]{:S(2)}, u32[]{:S(2)}) collective-permute-start(f32[4,64,128]{2,1,0:T(8,128)S(1)} %collective-permute-done.4.refs_1_), channel_id=1, source_target_pairs={{0,1},{1,0},{2,3},{3,2},{4,5},{5,4},{6,7},{7,6},{8,9},{9,8},{10,11... | collective-permute-start | bytes 393224 | tf_op jit(solution)/shard_map/ppermute | solution.py:439
  34.5 6.3 %collective-permute-start.7 = (f32[4,72,128]{2,1,0:T(8,128)S(1)}, f32[4,72,128]{2,1,0:T(8,128)S(1)}, u32[]{:S(2)}, u32[]{:S(2)}) collective-permute-start(f32[4,72,128]{2,1,0:T(8,128)S(1)} %collective-permute-done.6.refs_3_), channel_id=1, source_target_pairs={{0,1},{1,0},{2,3},{3,2},{4,5},{5,4},{6,7},{7,6},{8,9},{9,8},{10,11... | collective-permute-start | bytes 442376 | tf_op jit(solution)/shard_map/ppermute | solution.py:439
  51.7 4.9 %collective-permute-start.17 = (f32[3,4,512]{2,1,0:T(4,128)S(1)}, f32[3,4,512]{2,1,0:T(4,128)S(1)}, u32[]{:S(2)}, u32[]{:S(2)}) collective-permute-start(f32[3,4,512]{2,1,0:T(4,128)S(1)} %get-tuple-element.123), channel_id=1, source_target_pairs={{0,16},{16,0},{1,17},{17,1},{2,18},{18,2},{3,19},{19,3},{4,20},{20... | collective-permute-start | bytes 73736 | tf_op jit(solution)/shard_map/ppermute | solution.py:459
  60.8 6.9 %collective-permute-start.18 = (f32[4,512]{1,0:T(4,128)S(1)}, f32[4,512]{1,0:T(4,128)S(1)}, u32[]{:S(2)}, u32[]{:S(2)}) collective-permute-start(f32[4,512]{1,0:T(4,128)S(1)} %get-tuple-element.131.refs_1_), channel_id=1, source_target_pairs={{0,16},{16,0},{1,17},{17,1},{2,18},{18,2},{3,19},{19,3},{4,20},{20... | collective-permute-start | bytes 24584 | tf_op jit(solution)/shard_map/ppermute | solution.py:459
  68.4 9.5 %all-to-all-start.1 = ((f32[8,2,3,4,512]{4,3,2,1,0:T(4,128)}), f32[8,2,3,4,512]{4,3,2,1,0:T(4,128)S(1)}, u32[]{:S(2)}, u32[]{:S(2)}) async-start(f32[8,2,3,4,512]{4,3,2,1,0:T(4,128)} %halo.1), calls=%async_computation.1 | async-start | bytes 786432 | tf_op jit(solution)/shard_map/all_to_all | solution.py:618
  88.9 6.0 %collective-permute-start.23 = (f32[64,128]{1,0:T(8,128)S(1)}, f32[64,128]{1,0:T(8,128)S(1)}, u32[]{:S(2)}, u32[]{:S(2)}) collective-permute-start(f32[64,128]{1,0:T(8,128)S(1)} %add_add_fusion.1), channel_id=1, source_target_pairs={{0,8},{2,10},{4,12},{6,14},{8,0},{10,2},{12,4},{14,6},{16,24},{18,... | collective-permute-start | bytes 98312 | tf_op jit(solution)/shard_map/ppermute | solution.py:439
  89.9 5.0 %collective-permute-start.24 = (f32[64,128]{1,0:T(8,128)S(1)}, f32[64,128]{1,0:T(8,128)S(1)}, u32[]{:S(2)}, u32[]{:S(2)}) collective-permute-start(f32[64,128]{1,0:T(8,128)S(1)} %add_add_fusion.1), channel_id=1, source_target_pairs={{0,16},{2,18},{4,20},{6,22},{8,24},{10,26},{12,28},{14,30},{16,0},... | collective-permute-start | bytes 98312 | tf_op jit(solution)/shard_map/ppermute | solution.py:439
  92.5 7.7 %collective-permute-start.27 = (f32[64,512]{1,0:T(8,128)S(1)}, f32[64,512]{1,0:T(8,128)S(1)}, u32[]{:S(2)}, u32[]{:S(2)}) collective-permute-start(f32[64,512]{1,0:T(8,128)S(1)} %get-tuple-element.149), channel_id=1, source_target_pairs={{14,18},{18,14},{15,19},{19,15}} | collective-permute-start | bytes 393224 | tf_op jit(solution)/shard_map/ppermute | solution.py:631
  (14 other events, 41.6 us)

commit v7 on v6

--- a/solution.py
+++ b/solution.py
@@ -489,7 +489,7 @@
         "pack_tiles",
         [
             pltpu.VMEM((shard_rows, tall, 2 * order), F32),
-            S((rows_part, tall, 2 * order), F32),
+            pltpu.VMEM((rows_part, tall, 2 * order), F32),
             S((1, 3), jnp.int32),
         ],
         [pl.BlockSpec(memory_space=pl.ANY)] * 3,

time: 107 us -> 106 us (level)
  transfers between devices with their start and end apart: 30 -> 30, of which waited for: 9 -> 8; matrix products, arithmetic and copies ran while one was open for 1% -> 1% of each run, Pallas kernels for 39% -> 40%
where the time goes in v7:
time: 106 us
  Pallas kernels  52.1 us (49%)
  starting transfers between devices  36 us (34%)
  waiting for transfers between devices  13.6 us (13%)
  local copies, waits for them, and re-layouts  3.17 us (3%)
    pallas_call x8, Pallas kernels, with_mats(): call(body, name, [*out_shapes, *mat_shapes], [*specs, *[VMEM] * 6], [VMEM...  33.8 us
    ppermute x25, starting transfers between devices, swapped(): lax.ppermute(value, axis, [(i, i ^ bit) for i in range(lax.axis_size(axis...  16 us
    all_to_all x1, starting transfers between devices, shards(): lax.all_to_all(right_side.reshape(SPAN, each, cells), 'pos', 0, 0, tiled=...  7.13 us
    ppermute x25, waiting for transfers between devices, swapped(): lax.ppermute(value, axis, [(i, i ^ bit) for i in range(lax.axis_size(axis...  6.71 us
    pallas_call x1, Pallas kernels, shards(): call(last_kernel, 'update', [S((count, cells), F32)] * 2, [VMEM] * 12, [V...  6.22 us
    all_to_all x1, starting transfers between devices, shards(): rows = lax.all_to_all(rows, 'pos', 0, 0, tiled=True)  5.1 us
    ppermute x2, starting transfers between devices, exchanged(): got.append(lax.ppermute(value, 'blk', pairs + [(b, a) for a, b in pairs]))  5.08 us
    pallas_call x1, Pallas kernels, shards(): call(own_factor_kernel, 'factors_own', mat_shapes, [SMEM, VMEM], [VMEM] *...  3.98 us
  transfers between devices with their start and end apart: 30, of which 8 were waited for; matrix products, arithmetic and copies ran while one was open for 1% of the time, Pallas kernels for 40%

profile of v7, /device:TPU:14, one launch (start us, length us, event | category | flops | bytes accessed | tf_op | source)
XLA Modules:
  0.0 105.9 jit_solution(6952097815483126784)
XLA Ops:
  0.6 2.5 %pack_tiles.1 = (f32[8,136,128]{2,1,0:T(8,128)S(1)}, f32[4,136,128]{2,1,0:T(8,128)S(1)}, s32[1,3]{1,0:T(1,128)}) custom-call(s32[8,7]{1,0:T(8,128)} %columns.3, f32[8,7,64,64]{3,2,1,0:T(8,128)} %tiles.3, f32[8,64,64]{2,1,0:T(8,128)} %pivots_far.1), custom_call_target="tpu_custom_call" | custom-call | flops 2000000000 | tf_op jit(solution)/shard_map/pack_tiles/pallas_call | solution.py:487
  5.0 7.1 %all-to-all-start = ((f32[8,4,512]{2,1,0:T(4,128)}), f32[8,4,512]{2,1,0:T(4,128)S(1)}, u32[]{:S(2)}, u32[]{:S(2)}) async-start(f32[8,4,512]{2,1,0:T(4,128)} %reshape.7), calls=%async_computation | async-start | bytes 131072 | tf_op jit(solution)/shard_map/all_to_all | solution.py:508
  12.8 2.1 %all-to-all-done.refs_0_ = f32[8,4,512]{2,1,0:T(4,128)S(1)} async-done(((f32[8,4,512]{2,1,0:T(4,128)}), f32[8,4,512]{2,1,0:T(4,128)S(1)}, u32[]{:S(2)}, u32[]{:S(2)}) %all-to-all-start) | async-done | bytes 65568 | tf_op jit(solution)/shard_map/all_to_all | solution.py:508
  20.2 4.0 %factors_own.1 = (bf16[8,2,512,512]{3,2,1,0:T(8,128)(2,1)S(1)}, bf16[8,2,512,512]{3,2,1,0:T(8,128)(2,1)S(1)}, bf16[8,512,512]{2,1,0:T(8,128)(2,1)S(1)}, bf16[8,5...) custom-call(s32[1,3]{1,0:T(1,128)S(1)} %copy-done.1, ...), custom_call_target="tpu_custom_call" | custom-call | flops 4000000000 | tf_op jit(solution)/shard_map/factors_own/pallas_call | solution.py:532
  27.3 6.1 %factors_near.1 = (bf16[8,2,512,512]{3,2,1,0:T(8,128)(2,1)S(1)}, bf16[8,2,512,512]{3,2,1,0:T(8,128)(2,1)S(1)}, bf16[8,512,512]{2,1,0:T(8,128)(2,1)S(1)}, bf16[8,...) custom-call(s32[1,3]{1,0:T(1,128)S(1)} %copy-done.1, ...), custom_call_target="tpu_custom_call", output_to_operand_aliasing={{0}: (7, {}), {1}: (8, {}), {2}: (9, {}), {3}: (10, {}), {4... | custom-call | flops 6000000000 | tf_op jit(solution)/shard_map/factors_near/pallas_call | solution.py:549
  34.1 6.1 %factors_mid.1 = (bf16[8,2,512,512]{3,2,1,0:T(8,128)(2,1)S(1)}, bf16[8,2,512,512]{3,2,1,0:T(8,128)(2,1)S(1)}, bf16[8,512,512]{2,1,0:T(8,128)(2,1)S(1)}, bf16[8,5...) custom-call(s32[1,3]{1,0:T(1,128)S(1)} %copy-done.1, ...), custom_call_target="tpu_custom_call", output_to_operand_aliasing={{0}: (7, {}), {1}: (8, {}), {2}: (9, {}), {3}: (10, {}), {4... | custom-call | flops 6000000000 | tf_op jit(solution)/shard_map/factors_mid/pallas_call | solution.py:549
  40.3 2.7 %factors_far.1 = (bf16[8,2,512,512]{3,2,1,0:T(8,128)(2,1)S(1)}, bf16[8,2,512,512]{3,2,1,0:T(8,128)(2,1)S(1)}, bf16[8,512,512]{2,1,0:T(8,128)(2,1)S(1)}, bf16[8,5...) custom-call(s32[1,3]{1,0:T(1,128)S(1)} %copy-done.1, ...), custom_call_target="tpu_custom_call", output_to_operand_aliasing={{0}: (5, {}), {1}: (6, {}), {2}: (7, {}), {3}: (8, {}), {4}... | custom-call | flops 3000000000 | tf_op jit(solution)/shard_map/factors_far/pallas_call | solution.py:549
  43.0 4.1 %forward_r.1 = (f32[8,4,512]{2,1,0:T(4,128)S(1)}, f32[2,4,512]{2,1,0:T(4,128)S(1)}, bf16[8,2,512,512]{3,2,1,0:T(8,128)(2,1)S(1)}, bf16[8,2,512,512]{3,2,1,0:T(8,...) custom-call(f32[8,4,512]{2,1,0:T(4,128)S(1)} %all-to-all-done.refs_0, ...), custom_call_target="tpu_custom_call", output_to_operand_aliasing={{2}: (1, {}), {3}: (2, {}), {4}: (3, {}), {5}: (4, {}), {6}... | custom-call | flops 4000000000 | tf_op jit(solution)/shard_map/forward_r/pallas_call | solution.py:549
  47.1 4.1 %backward_r.1 = (f32[8,4,512]{2,1,0:T(4,128)S(1)}, f32[8,4,512]{2,1,0:T(4,128)S(1)}, f32[3,4,512]{2,1,0:T(4,128)S(1)}, bf16[8,2,512,512]{3,2,1,0:T(8,128)(2,1)S(...) custom-call(f32[8,4,512]{2,1,0:T(4,128)S(1)} %get-tuple-element.105., ...), custom_call_target="tpu_custom_call", output_to_operand_aliasing={{3}: (2, {}), {4}: (3, {}), {5}: (4, {}), {6}: (5, {}), {7}... | custom-call | flops 4000000000 | tf_op jit(solution)/shard_map/backward_r/pallas_call | solution.py:549
  51.3 2.6 %collective-permute-start.17 = (f32[3,4,512]{2,1,0:T(4,128)S(1)}, f32[3,4,512]{2,1,0:T(4,128)S(1)}, u32[]{:S(2)}, u32[]{:S(2)}) collective-permute-start(f32[3,4,512]{2,1,0:T(4,128)S(1)} %get-tuple-element.123), channel_id=1, source_target_pairs={{0,16},{16,0},{1,17},{17,1},{2,18},{18,2},{3,19},{19,3},{4,20},{20... | collective-permute-start | bytes 73736 | tf_op jit(solution)/shard_map/ppermute | solution.py:459
  53.9 2.3 %residue_of_z.1 = (f32[8,4,512]{2,1,0:T(4,128)S(1)}, f32[8,4,512]{2,1,0:T(4,128)S(1)}, bf16[8,2,512,512]{3,2,1,0:T(8,128)(2,1)S(1)}, bf16[8,2,512,512]{3,2,1,0:T...) custom-call(f32[8,4,512]{2,1,0:T(4,128)S(1)} %all-to-all-done.refs_0, ...), custom_call_target="tpu_custom_call", output_to_operand_aliasing={{2}: (4, {}), {3}: (5, {}), {4}: (6, {}), {5}: (7, {}), {6}... | custom-call | flops 2000000000 | tf_op jit(solution)/shard_map/residue_of_z/pallas_call | solution.py:549
  56.3 4.1 %forward_v.1 = (f32[8,4,512]{2,1,0:T(4,128)S(1)}, f32[4,512]{1,0:T(4,128)S(1)}, bf16[8,2,512,512]{3,2,1,0:T(8,128)(2,1)S(1)}, bf16[8,2,512,512]{3,2,1,0:T(8,128)...) custom-call(f32[8,4,512]{2,1,0:T(4,128)S(1)} %get-tuple-element.121., ...), custom_call_target="tpu_custom_call", output_to_operand_aliasing={{2}: (4, {}), {3}: (5, {}), {4}: (6, {}), {5}: (7, {}), {6}... | custom-call | flops 4000000000 | tf_op jit(solution)/shard_map/forward_v/pallas_call | solution.py:549
  60.3 2.5 %collective-permute-start.18 = (f32[4,512]{1,0:T(4,128)S(1)}, f32[4,512]{1,0:T(4,128)S(1)}, u32[]{:S(2)}, u32[]{:S(2)}) collective-permute-start(f32[4,512]{1,0:T(4,128)S(1)} %get-tuple-element.131.refs_1_), channel_id=1, source_target_pairs={{0,16},{16,0},{1,17},{17,1},{2,18},{18,2},{3,19},{19,3},{4,20},{20... | collective-permute-start | bytes 24584 | tf_op jit(solution)/shard_map/ppermute | solution.py:459
  62.8 4.1 %backward_v.1 = (f32[8,2,3,4,512]{4,3,2,1,0:T(4,128)S(1)}, bf16[8,2,512,512]{3,2,1,0:T(8,128)(2,1)S(1)}, bf16[8,2,512,512]{3,2,1,0:T(8,128)(2,1)S(1)}, bf16[8,51...) custom-call(f32[8,4,512]{2,1,0:T(4,128)S(1)} %get-tuple-element.130., ...), custom_call_target="tpu_custom_call", output_to_operand_aliasing={{1}: (5, {}), {2}: (6, {}), {3}: (7, {}), {4}: (8, {}), {5}... | custom-call | flops 4000000000 | tf_op jit(solution)/shard_map/backward_v/pallas_call | solution.py:549
  67.7 5.1 %all-to-all-start.1 = ((f32[8,2,3,4,512]{4,3,2,1,0:T(4,128)}), f32[8,2,3,4,512]{4,3,2,1,0:T(4,128)S(1)}, u32[]{:S(2)}, u32[]{:S(2)}) async-start(f32[8,2,3,4,512]{4,3,2,1,0:T(4,128)} %halo.1), calls=%async_computation.1 | async-start | bytes 786432 | tf_op jit(solution)/shard_map/all_to_all | solution.py:618
  72.9 1.7 %row_band.2 = (bf16[1536,256]{1,0:T(8,128)(2,1)S(1)}, bf16[1536,256]{1,0:T(8,128)(2,1)S(1)}) custom-call(s32[8,7]{1,0:T(8,128)S(1)} %copy-done.3, f32[8,7,64,64]{3,2,1,0:T(8,128)S(1)} %copy-done.2), custom_call_target="tpu_custom_call" | custom-call | flops 20000000000 | tf_op jit(solution)/shard_map/row_band/pallas_call | solution.py:521
  77.4 1.7 %row_band.3 = (bf16[1536,256]{1,0:T(8,128)(2,1)S(1)}, bf16[1536,256]{1,0:T(8,128)(2,1)S(1)}) custom-call(s32[8,7]{1,0:T(8,128)S(1)} %copy-done.3, f32[8,7,64,64]{3,2,1,0:T(8,128)S(1)} %copy-done.2), custom_call_target="tpu_custom_call" | custom-call | flops 20000000000 | tf_op jit(solution)/shard_map/row_band/pallas_call | solution.py:521
  80.6 1.5 %collective-permute-start.20 = (f32[64,128]{1,0:T(8,128)S(1)}, f32[64,128]{1,0:T(8,128)S(1)}, u32[]{:S(2)}, u32[]{:S(2)}) collective-permute-start(f32[64,128]{1,0:T(8,128)S(1)} %get-tuple-element.143), channel_id=1, source_target_pairs={{0,2},{2,0},{4,6},{6,4},{8,10},{10,8},{12,14},{14,12},{16,18},{18,... | collective-permute-start | bytes 98312 | tf_op jit(solution)/shard_map/ppermute | solution.py:439
  82.1 1.5 %collective-permute-start.21 = (f32[64,128]{1,0:T(8,128)S(1)}, f32[64,128]{1,0:T(8,128)S(1)}, u32[]{:S(2)}, u32[]{:S(2)}) collective-permute-start(f32[64,128]{1,0:T(8,128)S(1)} %get-tuple-element.143), channel_id=1, source_target_pairs={{0,4},{2,6},{4,0},{6,2},{8,12},{10,14},{12,8},{14,10},{16,20},{18,... | collective-permute-start | bytes 98312 | tf_op jit(solution)/shard_map/ppermute | solution.py:439
  84.6 1.4 %collective-permute-done.21 = f32[64,128]{1,0:T(8,128)S(1)} collective-permute-done((f32[64,128]{1,0:T(8,128)S(1)}, f32[64,128]{1,0:T(8,128)S(1)}, u32[]{:S(2)}, u32[]{:S(2)}) %collective-permute-start.21) | collective-permute-done | bytes 32800 | tf_op jit(solution)/shard_map/ppermute | solution.py:439
  86.0 2.4 %collective-permute-done.22 = f32[64,128]{1,0:T(8,128)S(1)} collective-permute-done((f32[64,128]{1,0:T(8,128)S(1)}, f32[64,128]{1,0:T(8,128)S(1)}, u32[]{:S(2)}, u32[]{:S(2)}) %collective-permute-start.22) | collective-permute-done | bytes 32800 | tf_op jit(solution)/shard_map/ppermute | solution.py:439
  91.9 2.7 %collective-permute-start.27 = (f32[64,512]{1,0:T(8,128)S(1)}, f32[64,512]{1,0:T(8,128)S(1)}, u32[]{:S(2)}, u32[]{:S(2)}) collective-permute-start(f32[64,512]{1,0:T(8,128)S(1)} %get-tuple-element.149), channel_id=1, source_target_pairs={{14,18},{18,14},{15,19},{19,15}} | collective-permute-start | bytes 393224 | tf_op jit(solution)/shard_map/ppermute | solution.py:631
  96.0 3.7 %collective-permute-done.27.arrived = f32[64,512]{1,0:T(8,128)S(1)} collective-permute-done((f32[64,512]{1,0:T(8,128)S(1)}, f32[64,512]{1,0:T(8,128)S(1)}, u32[]{:S(2)}, u32[]{:S(2)}) %collective-permute-start.27) | collective-permute-done | bytes 131104 | tf_op jit(solution)/shard_map/ppermute | solution.py:631
  99.7 6.2 %update.1 = (f32[32,512]{1,0:T(8,128)}, f32[32,512]{1,0:T(8,128)}) custom-call(f32[64,128]{1,0:T(8,128)S(1)} %add_add_fusion.own_sums, f32[64,128]{1,0:T(8,128)S(1)} %collective-permute-done.26.other_sums, f32[64,512]{1,0:T(8,128)S(1)} %get-tuple-element.144.r, f32[64,512]{1,0:T(8,128)S(1)} %get-tuple-element.145.d, f32[64,512]{1,0:T(8,128)S(1)} %get-tuple-element.146.q, ...), custom_call_target="tpu_custom_call" | custom-call | flops 4000000000 | tf_op jit(solution)/shard_map/update/pallas_call | solution.py:632
  (80 shorter events, 22.4 us)
Async XLA Ops:
  3.2 9.0 %collective-permute-start.2 = (f32[4,136,128]{2,1,0:T(8,128)S(1)}, f32[4,136,128]{2,1,0:T(8,128)S(1)}, u32[]{:S(2)}, u32[]{:S(2)}) collective-permute-start(f32[4,136,128]{2,1,0:T(8,128)S(1)} %get-tuple-element.79), channel_id=1, source_target_pairs={{0,8},{2,10},{4,12},{6,14},{8,0},{10,2},{12,4},{14,6},{1,9},{3,11}... | collective-permute-start | bytes 835592 | tf_op jit(solution)/shard_map/ppermute | solution.py:439
  3.7 8.5 %collective-permute-start.8 = (f32[4,136,128]{2,1,0:T(8,128)S(1)}, f32[4,136,128]{2,1,0:T(8,128)S(1)}, u32[]{:S(2)}, u32[]{:S(2)}) collective-permute-start(f32[4,136,128]{2,1,0:T(8,128)S(1)} %get-tuple-element.79), channel_id=1, source_target_pairs={{0,4},{2,6},{4,0},{6,2},{8,12},{10,14},{12,8},{14,10},{1,5},{3,7},... | collective-permute-start | bytes 835592 | tf_op jit(solution)/shard_map/ppermute | solution.py:439
  4.2 10.7 %collective-permute-start.1 = (f32[4,136,128]{2,1,0:T(8,128)S(1)}, f32[4,136,128]{2,1,0:T(8,128)S(1)}, u32[]{:S(2)}, u32[]{:S(2)}) collective-permute-start(f32[4,136,128]{2,1,0:T(8,128)S(1)} %get-tuple-element.79), channel_id=1, source_target_pairs={{0,2},{2,0},{4,6},{6,4},{8,10},{10,8},{12,14},{14,12},{1,3},{3,1},... | collective-permute-start | bytes 835592 | tf_op jit(solution)/shard_map/ppermute | solution.py:439
  5.0 9.9 %all-to-all-start = ((f32[8,4,512]{2,1,0:T(4,128)}), f32[8,4,512]{2,1,0:T(4,128)S(1)}, u32[]{:S(2)}, u32[]{:S(2)}) async-start(f32[8,4,512]{2,1,0:T(4,128)} %reshape.7), calls=%async_computation | async-start | bytes 131072 | tf_op jit(solution)/shard_map/all_to_all | solution.py:508
  12.2 7.3 %collective-permute-start.9 = (f32[4,128,128]{2,1,0:T(8,128)S(1)}, f32[4,128,128]{2,1,0:T(8,128)S(1)}, u32[]{:S(2)}, u32[]{:S(2)}) collective-permute-start(f32[4,128,128]{2,1,0:T(8,128)S(1)} %pad_maximum_fusion.2), channel_id=1, source_target_pairs={{0,2},{2,0},{4,6},{6,4},{8,10},{10,8},{12,14},{14,12},{1,3},{3,1},... | collective-permute-start | bytes 786440 | tf_op jit(solution)/shard_map/ppermute | solution.py:439
  15.0 9.2 %collective-permute-start.3 = (f32[4,136,128]{2,1,0:T(8,128)S(1)}, f32[4,136,128]{2,1,0:T(8,128)S(1)}, u32[]{:S(2)}, u32[]{:S(2)}) collective-permute-start(f32[4,136,128]{2,1,0:T(8,128)S(1)} %pad_maximum_fusion.1), channel_id=1, source_target_pairs={{0,4},{2,6},{4,0},{6,2},{8,12},{10,14},{12,8},{14,10},{1,5},{3,7},... | collective-permute-start | bytes 835592 | tf_op jit(solution)/shard_map/ppermute | solution.py:439
  16.4 10.4 %collective-permute-start.12 = (f32[4,144,128]{2,1,0:T(8,128)S(1)}, f32[4,144,128]{2,1,0:T(8,128)S(1)}, u32[]{:S(2)}, u32[]{:S(2)}) collective-permute-start(f32[4,144,128]{2,1,0:T(8,128)S(1)} %pad_maximum_fusion), channel_id=1, source_target_pairs={{0,8},{2,10},{4,12},{6,14},{8,0},{10,2},{12,4},{14,6},{1,9},{3,11}... | collective-permute-start | bytes 884744 | tf_op jit(solution)/shard_map/ppermute | solution.py:439
  17.9 7.0 %collective-permute-start.15 = (f32[4,136,128]{2,1,0:T(8,128)S(1)}, f32[4,136,128]{2,1,0:T(8,128)S(1)}, u32[]{:S(2)}, u32[]{:S(2)}) collective-permute-start(f32[4,136,128]{2,1,0:T(8,128)S(1)} %collective-permute-done.8.refs_3_), channel_id=1, source_target_pairs={{0,1},{1,0},{2,3},{3,2},{4,5},{5,4},{6,7},{7,6},{8,9},{9,8},{10,11... | collective-permute-start | bytes 835592 | tf_op jit(solution)/shard_map/ppermute | solution.py:439
  17.9 8.2 %collective-permute-start.14 = (f32[4,136,128]{2,1,0:T(8,128)S(1)}, f32[4,136,128]{2,1,0:T(8,128)S(1)}, u32[]{:S(2)}, u32[]{:S(2)}) collective-permute-start(f32[4,136,128]{2,1,0:T(8,128)S(1)} %collective-permute-done.1.refs_1_), channel_id=1, source_target_pairs={{0,1},{1,0},{2,3},{3,2},{4,5},{5,4},{6,7},{7,6},{8,9},{9,8},{10,11... | collective-permute-start | bytes 835592 | tf_op jit(solution)/shard_map/ppermute | solution.py:439
  19.6 7.2 %collective-permute-start.16 = (f32[4,136,128]{2,1,0:T(8,128)S(1)}, f32[4,136,128]{2,1,0:T(8,128)S(1)}, u32[]{:S(2)}, u32[]{:S(2)}) collective-permute-start(f32[4,136,128]{2,1,0:T(8,128)S(1)} %collective-permute-done.2.refs_5_), channel_id=1, source_target_pairs={{0,1},{1,0},{2,3},{3,2},{4,5},{5,4},{6,7},{7,6},{8,9},{9,8},{10,11... | collective-permute-start | bytes 835592 | tf_op jit(solution)/shard_map/ppermute | solution.py:439
  24.2 9.8 %collective-permute-start.10 = (f32[4,128,128]{2,1,0:T(8,128)S(1)}, f32[4,128,128]{2,1,0:T(8,128)S(1)}, u32[]{:S(2)}, u32[]{:S(2)}) collective-permute-start(f32[4,128,128]{2,1,0:T(8,128)S(1)} %collective-permute-done.9.refs_1_), channel_id=1, source_target_pairs={{0,1},{1,0},{2,3},{3,2},{4,5},{5,4},{6,7},{7,6},{8,9},{9,8},{10,11... | collective-permute-start | bytes 786440 | tf_op jit(solution)/shard_map/ppermute | solution.py:439
  24.8 8.7 %collective-permute-start.6 = (f32[4,72,128]{2,1,0:T(8,128)S(1)}, f32[4,72,128]{2,1,0:T(8,128)S(1)}, u32[]{:S(2)}, u32[]{:S(2)}) collective-permute-start(f32[4,72,128]{2,1,0:T(8,128)S(1)} %slice.29), channel_id=1, source_target_pairs={{0,8},{2,10},{4,12},{6,14},{8,0},{10,2},{12,4},{14,6},{1,9},{3,11}... | collective-permute-start | bytes 442376 | tf_op jit(solution)/shard_map/ppermute | solution.py:439
  26.0 7.4 %collective-permute-start.4 = (f32[4,64,128]{2,1,0:T(8,128)S(1)}, f32[4,64,128]{2,1,0:T(8,128)S(1)}, u32[]{:S(2)}, u32[]{:S(2)}) collective-permute-start(f32[4,64,128]{2,1,0:T(8,128)S(1)} %slice.28), channel_id=1, source_target_pairs={{0,2},{2,0},{4,6},{6,4},{8,10},{10,8},{12,14},{14,12},{1,3},{3,1},... | collective-permute-start | bytes 393224 | tf_op jit(solution)/shard_map/ppermute | solution.py:439
  26.8 7.3 %collective-permute-start.11 = (f32[4,136,128]{2,1,0:T(8,128)S(1)}, f32[4,136,128]{2,1,0:T(8,128)S(1)}, u32[]{:S(2)}, u32[]{:S(2)}) collective-permute-start(f32[4,136,128]{2,1,0:T(8,128)S(1)} %collective-permute-done.3.refs_3_), channel_id=1, source_target_pairs={{0,1},{1,0},{2,3},{3,2},{4,5},{5,4},{6,7},{7,6},{8,9},{9,8},{10,11... | collective-permute-start | bytes 835592 | tf_op jit(solution)/shard_map/ppermute | solution.py:439
  26.8 7.3 %collective-permute-start.13 = (f32[4,144,128]{2,1,0:T(8,128)S(1)}, f32[4,144,128]{2,1,0:T(8,128)S(1)}, u32[]{:S(2)}, u32[]{:S(2)}) collective-permute-start(f32[4,144,128]{2,1,0:T(8,128)S(1)} %collective-permute-done.12.refs_5_), channel_id=1, source_target_pairs={{0,1},{1,0},{2,3},{3,2},{4,5},{5,4},{6,7},{7,6},{8,9},{9,8},{10,11... | collective-permute-start | bytes 884744 | tf_op jit(solution)/shard_map/ppermute | solution.py:439
  33.4 45.7 %collective-permute-start = (f32[32,512]{1,0:T(8,128)S(1)}, f32[32,512]{1,0:T(8,128)S(1)}, u32[]{:S(2)}, u32[]{:S(2)}) collective-permute-start(f32[32,512]{1,0:T(8,128)S(1)} %copy-done), channel_id=1, source_target_pairs={{0,1},{1,0},{2,3},{3,2},{4,5},{5,4},{6,7},{7,6},{8,9},{9,8},{10,11... | collective-permute-start | bytes 196616 | tf_op jit(solution)/shard_map/ppermute | solution.py:439
  33.6 6.7 %collective-permute-start.5 = (f32[4,64,128]{2,1,0:T(8,128)S(1)}, f32[4,64,128]{2,1,0:T(8,128)S(1)}, u32[]{:S(2)}, u32[]{:S(2)}) collective-permute-start(f32[4,64,128]{2,1,0:T(8,128)S(1)} %collective-permute-done.4.refs_1_), channel_id=1, source_target_pairs={{0,1},{1,0},{2,3},{3,2},{4,5},{5,4},{6,7},{7,6},{8,9},{9,8},{10,11... | collective-permute-start | bytes 393224 | tf_op jit(solution)/shard_map/ppermute | solution.py:439
  34.0 6.3 %collective-permute-start.7 = (f32[4,72,128]{2,1,0:T(8,128)S(1)}, f32[4,72,128]{2,1,0:T(8,128)S(1)}, u32[]{:S(2)}, u32[]{:S(2)}) collective-permute-start(f32[4,72,128]{2,1,0:T(8,128)S(1)} %collective-permute-done.6.refs_3_), channel_id=1, source_target_pairs={{0,1},{1,0},{2,3},{3,2},{4,5},{5,4},{6,7},{7,6},{8,9},{9,8},{10,11... | collective-permute-start | bytes 442376 | tf_op jit(solution)/shard_map/ppermute | solution.py:439
  51.3 4.9 %collective-permute-start.17 = (f32[3,4,512]{2,1,0:T(4,128)S(1)}, f32[3,4,512]{2,1,0:T(4,128)S(1)}, u32[]{:S(2)}, u32[]{:S(2)}) collective-permute-start(f32[3,4,512]{2,1,0:T(4,128)S(1)} %get-tuple-element.123), channel_id=1, source_target_pairs={{0,16},{16,0},{1,17},{17,1},{2,18},{18,2},{3,19},{19,3},{4,20},{20... | collective-permute-start | bytes 73736 | tf_op jit(solution)/shard_map/ppermute | solution.py:459
  60.3 6.6 %collective-permute-start.18 = (f32[4,512]{1,0:T(4,128)S(1)}, f32[4,512]{1,0:T(4,128)S(1)}, u32[]{:S(2)}, u32[]{:S(2)}) collective-permute-start(f32[4,512]{1,0:T(4,128)S(1)} %get-tuple-element.131.refs_1_), channel_id=1, source_target_pairs={{0,16},{16,0},{1,17},{17,1},{2,18},{18,2},{3,19},{19,3},{4,20},{20... | collective-permute-start | bytes 24584 | tf_op jit(solution)/shard_map/ppermute | solution.py:459
  67.7 9.6 %all-to-all-start.1 = ((f32[8,2,3,4,512]{4,3,2,1,0:T(4,128)}), f32[8,2,3,4,512]{4,3,2,1,0:T(4,128)S(1)}, u32[]{:S(2)}, u32[]{:S(2)}) async-start(f32[8,2,3,4,512]{4,3,2,1,0:T(4,128)} %halo.1), calls=%async_computation.1 | async-start | bytes 786432 | tf_op jit(solution)/shard_map/all_to_all | solution.py:618
  88.4 6.2 %collective-permute-start.23 = (f32[64,128]{1,0:T(8,128)S(1)}, f32[64,128]{1,0:T(8,128)S(1)}, u32[]{:S(2)}, u32[]{:S(2)}) collective-permute-start(f32[64,128]{1,0:T(8,128)S(1)} %add_add_fusion.1), channel_id=1, source_target_pairs={{0,8},{2,10},{4,12},{6,14},{8,0},{10,2},{12,4},{14,6},{16,24},{18,... | collective-permute-start | bytes 98312 | tf_op jit(solution)/shard_map/ppermute | solution.py:439
  89.4 5.2 %collective-permute-start.24 = (f32[64,128]{1,0:T(8,128)S(1)}, f32[64,128]{1,0:T(8,128)S(1)}, u32[]{:S(2)}, u32[]{:S(2)}) collective-permute-start(f32[64,128]{1,0:T(8,128)S(1)} %add_add_fusion.1), channel_id=1, source_target_pairs={{0,16},{2,18},{4,20},{6,22},{8,24},{10,26},{12,28},{14,30},{16,0},... | collective-permute-start | bytes 98312 | tf_op jit(solution)/shard_map/ppermute | solution.py:439
  91.9 7.7 %collective-permute-start.27 = (f32[64,512]{1,0:T(8,128)S(1)}, f32[64,512]{1,0:T(8,128)S(1)}, u32[]{:S(2)}, u32[]{:S(2)}) collective-permute-start(f32[64,512]{1,0:T(8,128)S(1)} %get-tuple-element.149), channel_id=1, source_target_pairs={{14,18},{18,14},{15,19},{19,15}} | collective-permute-start | bytes 393224 | tf_op jit(solution)/shard_map/ppermute | solution.py:631
  (14 other events, 41.1 us)
